TPU v7x, 32 devices: a whole 2x2x4 slice. The times are simulated.
32 devices in a mesh: inp: 4 (over z), out: 2 (over y), tok: 4 (over x, core).
Axes of the slice: x: 2, y: 2, z: 4, core: 2. Of those that a mesh axis runs over, the one named last changes fastest.
Arguments:
- saved_input: float32 [512, 4096], P('tok', 'inp'), may hold values from -6 to 6
- saved_gate: float32 [512, 28672], P('inp', ('out', 'tok')), may hold values from -6 to 6
- saved_up: float32 [512, 28672], P('inp', ('out', 'tok')), may hold values from -6 to 6
- out_grad: bfloat16 [512, 4096], P('tok', 'inp'), may hold values from -1.5 to 1.5
- w_gate: bfloat16 [4096, 28672], P('inp', ('out', 'tok')), may hold values from -0.09375 to 0.09375
- w_up: bfloat16 [4096, 28672], P('inp', ('out', 'tok')), may hold values from -0.09375 to 0.09375
- w_down: bfloat16 [28672, 4096], P(('out', 'tok'), 'inp'), may hold values from -0.03125 to 0.03125
Outputs:
- input_grad: bfloat16 [512, 4096], P(('out', 'tok'), 'inp')
- gate_wgrad: bfloat16 [4096, 28672], P('inp', ('out', 'tok'))
- up_wgrad: bfloat16 [4096, 28672], P('inp', ('out', 'tok'))
- down_wgrad: bfloat16 [28672, 4096], P(('out', 'tok'), 'inp')
All inputs are finite; a program needn't handle non-finite values.
Results may differ from a plain program's by a relative error of at most 0.0057.
Values may be sent and summed in bfloat16 or wider, within the bound.
No kernel may reach another device: no remote copies, remote signals or barrier semaphores. Data moves between devices by JAX's collectives and lax.ppermute only.
A program may use at most 128 MiB of HBM per device.

v0:
```python
import jax
import jax.numpy as jnp
from jax import lax
from jax.sharding import PartitionSpec as P


def local_terms(hidden_grad, gate_vals, up_vals):
    sig = jax.nn.sigmoid(gate_vals)
    hidden = (gate_vals * sig * up_vals).astype(jnp.bfloat16)
    gate_grad = (hidden_grad * up_vals * sig * (1.0 + gate_vals * (1.0 - sig))).astype(jnp.bfloat16)
    up_grad = (hidden_grad * gate_vals * sig).astype(jnp.bfloat16)
    return (gate_grad, up_grad, hidden)


def local(saved_input, saved_gate, saved_up, out_grad, w_gate, w_up, w_down):
    last_dims = (((1,), (1,)), ((), ()))
    lead_dims = (((0,), (0,)), ((), ()))
    input_b = saved_input.astype(jnp.bfloat16)
    all_inputs, all_grads = (
        lax.all_gather(input_b, "tok", axis=0, tiled=True),
        lax.all_gather(out_grad, "tok", axis=0, tiled=True),
    )
    share = lax.psum_scatter(
        lax.dot_general(all_grads, w_down, last_dims, preferred_element_type=jnp.float32),
        "inp",
        scatter_dimension=0,
        tiled=True,
    )
    gate_part, up_part, hidden_part = local_terms(share, saved_gate, saved_up)
    gate_grad, up_grad, hidden = (
        lax.all_gather(gate_part, "inp", axis=0, tiled=True),
        lax.all_gather(up_part, "inp", axis=0, tiled=True),
        lax.all_gather(hidden_part, "inp", axis=0, tiled=True),
    )
    gate_wgrad = lax.dot_general(
        all_inputs, gate_grad, lead_dims, preferred_element_type=jnp.float32
    ).astype(jnp.bfloat16)
    up_wgrad = lax.dot_general(
        all_inputs, up_grad, lead_dims, preferred_element_type=jnp.float32
    ).astype(jnp.bfloat16)
    down_wgrad = lax.dot_general(
        hidden, all_grads, lead_dims, preferred_element_type=jnp.float32
    ).astype(jnp.bfloat16)
    result = lax.dot_general(gate_grad, w_gate, last_dims, preferred_element_type=jnp.float32)
    summed = lax.psum_scatter(
        result + lax.dot_general(up_grad, w_up, last_dims, preferred_element_type=jnp.float32),
        ("out", "tok"),
        scatter_dimension=0,
        tiled=True,
    )
    return (summed.astype(jnp.bfloat16), gate_wgrad, up_wgrad, down_wgrad)


def solution(mesh):
    placed = (
        P("tok", "inp"),
        P("inp", ("out", "tok")),
        P("inp", ("out", "tok")),
        P("tok", "inp"),
        P("inp", ("out", "tok")),
        P("inp", ("out", "tok")),
        P(("out", "tok"), "inp"),
    )
    return jax.shard_map(
        local,
        mesh=mesh,
        in_specs=placed,
        out_specs=(
            P(("out", "tok"), "inp"),
            P("inp", ("out", "tok")),
            P("inp", ("out", "tok")),
            P(("out", "tok"), "inp"),
        ),
        check_vma=False,
    )
```

profile of v0, /device:TPU:0, one launch (start us, length us, event | category | flops | bytes accessed | tf_op | source)
XLA Modules:
  0.0 460.2 jit_solution(7159718349823339550)
XLA Ops:
  7.2 0.7 all-gather.6.cloned.1.call-update
  7.9 21.1 %all-gather.6.cloned.1.call-done = bf16[512,1024]{1,0:T(8,128)(2,1)} async-done(((bf16[128,1024]{1,0:T(8,128)(2,1)}), bf16[512,1024]{1,0:T(8,128)(2,1)}) %all-gather.6.cloned.1.call-update) | async-done | bytes 1048592 | tf_op jit(solution)/shard_map/all_gather | solution.py:21
  29.0 10.5 %fusion.2 = f32[512,3584]{1,0:T(8,128)} fusion(bf16[512,1024]{1,0:T(8,128)(2,1)} %all-gather.6.cloned.1.call-done, bf16[3584,1024]{1,0:T(8,128)(2,1)} %param.13), kind=kOutput, calls=%fused_computation.10 | convolution fusion | flops 3758096384 | bytes 15728640 | tf_op jit(solution)/shard_map/dot_general | solution.py:24
  39.5 0.0 all-gather.8.cloned.1.call-start
  39.6 127.9 %reduce-scatter.3.cloned.1.call-done = f32[128,3584]{1,0:T(8,128)} async-done(((f32[512,3584]{1,0:T(8,128)}), f32[128,3584]{1,0:T(8,128)}) %reduce-scatter.3.cloned.1.call-update) | async-done | bytes 1835024 | tf_op jit(solution)/shard_map/reduce_scatter | solution.py:23
  167.4 4.7 %multiply_convert_fusion = (bf16[128,3584]{1,0:T(8,128)(2,1)}, bf16[128,3584]{1,0:T(8,128)(2,1)}, bf16[128,3584]{1,0:T(8,128)(2,1)}) fusion(f32[128,3584]{1,0:T(8,128)S(1)} %copy-done, f32[128,3584]{1,0:T(8,128)} %param.8, f32[128,3584]{1,0:T(8,128)} %reduce-scatter.3.cloned.1.call-done), kind=kLoop, calls=%fused_computation.5 | loop fusion | flops 7340032 | bytes 8257536 | tf_op jit(solution)/shard_map/convert_element_type | solution.py:9
  172.1 0.0 all-gather.10.cloned.1.call-start
  172.2 0.5 all-gather.10.cloned.1.call-update
  172.8 0.7 convert_element_type.33
  173.6 0.5 all-gather.14.cloned.1.call-update
  174.1 0.2 reduce-scatter.5.cloned.1.call-start
  174.3 70.6 %all-gather.8.cloned.1.call-done = bf16[512,3584]{1,0:T(8,128)(2,1)} async-done(((bf16[128,3584]{1,0:T(8,128)(2,1)}), bf16[512,3584]{1,0:T(8,128)(2,1)}) %all-gather.8.cloned.1.call-update) | async-done | bytes 3670032 | tf_op jit(solution)/shard_map/all_gather | solution.py:31
  244.9 7.4 %fusion.3 = f32[512,1024]{1,0:T(8,128)S(1)} fusion(bf16[512,3584]{1,0:T(8,128)(2,1)} %all-gather.8.cloned.1.call-done, bf16[1024,3584]{1,0:T(8,128)(2,1)} %param.11), kind=kOutput, calls=%fused_computation.11 | convolution fusion | flops 3758096384 | bytes 13107200 | tf_op jit(solution)/shard_map/dot_general | solution.py:44
  252.3 65.4 %all-gather.10.cloned.1.call-done = bf16[512,3584]{1,0:T(8,128)(2,1)} async-done(((bf16[128,3584]{1,0:T(8,128)(2,1)}), bf16[512,3584]{1,0:T(8,128)(2,1)}) %all-gather.10.cloned.1.call-update) | async-done | bytes 3670032 | tf_op jit(solution)/shard_map/all_gather | solution.py:32
  317.6 9.6 %convolution_add_fusion = f32[512,1024]{1,0:T(8,128)} fusion(f32[512,1024]{1,0:T(8,128)S(1)} %fusion.3, bf16[512,3584]{1,0:T(8,128)(2,1)} %all-gather.10.cloned.1.call-done, bf16[1024,3584]{1,0:T(8,128)(2,1)} %param.12), kind=kOutput, calls=%fused_computation.9 | convolution fusion | flops 3758620672 | bytes 15204352 | tf_op jit(solution)/shard_map/dot_general | solution.py:46
  327.3 7.7 %all-gather.12.cloned.1.call-done = bf16[512,1024]{1,0:T(8,128)(2,1)} async-done(((bf16[128,1024]{1,0:T(8,128)(2,1)}), bf16[512,1024]{1,0:T(8,128)(2,1)}) %all-gather.12.cloned.1.call-update) | async-done | bytes 1048592 | tf_op jit(solution)/shard_map/all_gather | solution.py:20
  335.0 9.4 %fusion = bf16[1024,3584]{0,1:T(8,128)(2,1)} fusion(bf16[512,3584]{1,0:T(8,128)(2,1)} %all-gather.8.cloned.1.call-done, bf16[512,1024]{1,0:T(8,128)(2,1)} %all-gather.12.cloned.1.call-done), kind=kOutput, calls=%fused_computation.3 | convolution fusion | flops 3761766400 | bytes 12058624 | tf_op jit(solution)/shard_map/dot_general | solution.py:35
  344.4 10.1 %copy.11 = bf16[1024,3584]{1,0:T(8,128)(2,1)} copy(bf16[1024,3584]{0,1:T(8,128)(2,1)} %fusion) | data formatting | bytes 14680064
  354.5 8.1 %fusion.1 = bf16[1024,3584]{0,1:T(8,128)(2,1)} fusion(bf16[512,3584]{1,0:T(8,128)(2,1)} %all-gather.10.cloned.1.call-done, bf16[512,1024]{1,0:T(8,128)(2,1)S(1)} %copy-done.3), kind=kOutput, calls=%fused_computation.4 | convolution fusion | flops 3761766400 | bytes 12058624 | tf_op jit(solution)/shard_map/dot_general | solution.py:38
  362.6 10.0 %copy.12 = bf16[1024,3584]{1,0:T(8,128)(2,1)} copy(bf16[1024,3584]{0,1:T(8,128)(2,1)} %fusion.1) | data formatting | bytes 14680064
  372.6 36.0 %all-gather.14.cloned.1.call-done = bf16[512,3584]{1,0:T(8,128)(2,1)} async-done(((bf16[128,3584]{1,0:T(8,128)(2,1)}), bf16[512,3584]{1,0:T(8,128)(2,1)}) %all-gather.14.cloned.1.call-update) | async-done | bytes 3670032 | tf_op jit(solution)/shard_map/all_gather | solution.py:33
  408.6 8.1 %convolution_convert_fusion = bf16[3584,1024]{1,0:T(8,128)(2,1)} fusion(bf16[512,3584]{1,0:T(8,128)(2,1)} %all-gather.14.cloned.1.call-done, bf16[512,1024]{1,0:T(8,128)(2,1)S(1)} %copy-done.2), kind=kOutput, calls=%fused_computation | convolution fusion | flops 3761766400 | bytes 12058624 | tf_op jit(solution)/shard_map/dot_general | solution.py:41
  416.7 35.0 %reduce-scatter.5.cloned.1.call-done = f32[64,1024]{1,0:T(8,128)} async-done(((f32[512,1024]{1,0:T(8,128)}), f32[64,1024]{1,0:T(8,128)}) %reduce-scatter.5.cloned.1.call-update) | async-done | bytes 262160 | tf_op jit(solution)/shard_map/reduce_scatter | solution.py:45
  451.7 1.6 convert_element_type.32
  (16 shorter events, 0.2 us)
Async XLA Ops:
  7.2 21.8 %all-gather.6.cloned.1.call-start = ((), (), s32[]{:S(2)}) async-start(), calls=%async_computation.2 | async-start | bytes 1310720 | tf_op jit(solution)/shard_map/all_gather | solution.py:21
  7.9 159.5 %reduce-scatter.3.cloned.1.call-start = ((), (), s32[]{:S(2)}) async-start(), calls=%async_computation.3 | async-start | bytes 9175040 | tf_op jit(solution)/shard_map/reduce_scatter | solution.py:23
  39.5 127.9 %copy-start = (f32[128,3584]{1,0:T(8,128)S(1)}, f32[128,3584]{1,0:T(8,128)}, u32[]{:S(2)}) copy-start(f32[128,3584]{1,0:T(8,128)} %param.9) | copy-start | bytes 5505028
  39.5 133.2 %copy-start.1 = (f32[128,1024]{1,0:T(8,128)S(1)}, f32[128,1024]{1,0:T(8,128)}, u32[]{:S(2)}) copy-start(f32[128,1024]{1,0:T(8,128)} %param.7) | copy-start | bytes 1572868
  39.5 205.4 %all-gather.8.cloned.1.call-start = ((), (), s32[]{:S(2)}) async-start(), calls=%async_computation.4 | async-start | bytes 4587520 | tf_op jit(solution)/shard_map/all_gather | solution.py:31
  172.1 145.5 %all-gather.10.cloned.1.call-start = ((), (), s32[]{:S(2)}) async-start(), calls=%async_computation.5 | async-start | bytes 4587520 | tf_op jit(solution)/shard_map/all_gather | solution.py:32
  172.7 162.3 %all-gather.12.cloned.1.call-start = ((), (), s32[]{:S(2)}) async-start(), calls=%async_computation.7 | async-start | bytes 1310720 | tf_op jit(solution)/shard_map/all_gather | solution.py:20
  173.5 235.1 %all-gather.14.cloned.1.call-start = ((), (), s32[]{:S(2)}) async-start(), calls=%async_computation.8 | async-start | bytes 4587520 | tf_op jit(solution)/shard_map/all_gather | solution.py:33
  174.1 277.6 %reduce-scatter.5.cloned.1.call-start = ((), (), s32[]{:S(2)}) async-start(), calls=%async_computation.6 | async-start | bytes 2359296 | tf_op jit(solution)/shard_map/reduce_scatter | solution.py:45
  344.4 10.1 %copy-start.3 = (bf16[512,1024]{1,0:T(8,128)(2,1)S(1)}, bf16[512,1024]{1,0:T(8,128)(2,1)}, u32[]{:S(2)}) copy-start(bf16[512,1024]{1,0:T(8,128)(2,1)} %all-gather.12.cloned.1.call-done) | copy-start | bytes 3145732
  362.6 46.0 %copy-start.2 = (bf16[512,1024]{1,0:T(8,128)(2,1)S(1)}, bf16[512,1024]{1,0:T(8,128)(2,1)}, u32[]{:S(2)}) copy-start(bf16[512,1024]{1,0:T(8,128)(2,1)} %all-gather.6.cloned.1.call-done) | copy-start | bytes 3145732
Sparse Core Ops, SparseCore 0:
  9.6 19.4 all-gather.5
  39.6 127.7 reduce-scatter.2
  172.2 72.6 all-gather.7
  246.9 70.7 all-gather.9
  319.6 15.3 all-gather.11
  336.4 72.1 all-gather.13
  411.9 39.7 reduce-scatter.4
where the time goes:
time: 461 us; the launch traced here: 460 us
  waiting for transfers between devices  365 us (79%)
  matrix products  53 us (11%)
  local copies, waits for them, and re-layouts  20.1 us (4%)
  between operations  14.2 us (3%)
  other arithmetic  7.03 us (2%)
    reduce_scatter x1, waiting for transfers between devices, local(): lax.psum_scatter(lax.dot_general(all_grads, w_down, last_dims, preferred_...  128 us
    all_gather x1, waiting for transfers between devices, local(): lax.all_gather(gate_part, 'inp', axis=0, tiled=True)  70.6 us
    all_gather x1, waiting for transfers between devices, local(): lax.all_gather(up_part, 'inp', axis=0, tiled=True)  65.4 us
    all_gather x1, waiting for transfers between devices, local(): lax.all_gather(hidden_part, 'inp', axis=0, tiled=True)  36 us
    reduce_scatter x1, waiting for transfers between devices, local(): lax.psum_scatter(result + lax.dot_general(up_grad, w_up, last_dims, prefe...  35 us
    all_gather x1, waiting for transfers between devices, local(): lax.all_gather(out_grad, 'tok', axis=0, tiled=True)  21.1 us
    unnamed x10, local copies, waits for them, and re-layouts  20.1 us
    dot_general x1, matrix products, local(): lax.dot_general(all_grads, w_down, last_dims, preferred_element_type=jnp....  10.5 us
  transfers between devices with their start and end apart: 7, of which 7 were waited for; matrix products, arithmetic and copies ran while one was open for 14% of the time, Pallas kernels for 0%

commit v1 on v0

v1 whole, which is shorter than its diff:
```python
import functools

import jax
import jax.numpy as jnp
from jax import lax
from jax.experimental import pallas as pl
from jax.experimental.pallas import tpu as pltpu
from jax.sharding import PartitionSpec as P

BF, F32 = jnp.bfloat16, jnp.float32
LAST = (((1,), (1,)), ((), ()))
LEAD = (((0,), (0,)), ((), ()))
STRAIGHT = (((1,), (0,)), ((), ()))
ANY = pl.BlockSpec(memory_space=pl.ANY)
VMEM_LIMIT = 64 * 1024 * 1024

ENDS_IN = [(0, 1), (3, 2)]
MIDDLE = [(1, 2), (2, 1)]
PAIRS = [(0, 1), (1, 0), (2, 3), (3, 2)]
OUTWARD = [(1, 0), (2, 3)]
X_SWAP = [(0, 2), (2, 0), (1, 3), (3, 1)]
CORE_SWAP = [(0, 1), (1, 0), (2, 3), (3, 2)]
Y_SWAP = [(0, 1), (1, 0)]
XY_SWAP = [(4 * o + t, 4 * (1 - o) + (t ^ 2)) for o in range(2) for t in range(4)]


def send(x, perm):
    return lax.ppermute(x, "inp", perm)


def place(k, z):
    return jnp.where(k // 2 == z // 2, k ^ z, jnp.where(z < 2, k, 3 - k))


def dot(a, b, dims):
    return lax.dot_general(a, b, dims, preferred_element_type=F32)


class Chain:
    def __init__(self, token):
        self.token = token

    def call(self, body, grid, ins, in_specs, outs, out_specs, aliases=(), scalars=None, scratch=()):
        lead = 0 if scalars is None else 1

        def kernel(*refs):
            body(*refs[:lead], *refs[lead + 1 : lead + 1 + len(ins)], *refs[lead + 2 + len(ins) :])

        pairs = {lead: 0, **{lead + 1 + i: 1 + o for i, o in aliases}}
        given = pl.pallas_call(
            kernel,
            grid_spec=pltpu.PrefetchScalarGridSpec(
                num_scalar_prefetch=lead,
                grid=grid,
                in_specs=[ANY, *in_specs],
                out_specs=[ANY, *out_specs],
                scratch_shapes=list(scratch),
            ),
            out_shape=[jax.ShapeDtypeStruct(self.token.shape, self.token.dtype), *outs],
            input_output_aliases=pairs,
            compiler_params=pltpu.CompilerParams(vmem_limit_bytes=VMEM_LIMIT),
        )(*(() if scalars is None else (scalars,)), self.token, *ins)
        self.token = given[0]
        return given[1:]

    def relay(self, *arrays):
        return self.call(
            lambda *refs: None,
            (1,),
            arrays,
            [ANY] * len(arrays),
            [jax.ShapeDtypeStruct(a.shape, a.dtype) for a in arrays],
            [ANY] * len(arrays),
            aliases=[(i, i) for i in range(len(arrays))],
        )


TILE = 256
CUTS = (7, 7)


def swiglu_grads(part_ref, second_ref, third_ref, g_ref, u_ref, out_ref):
    share = part_ref[...] + third_ref[...].astype(F32) + second_ref[...].astype(F32)
    g, u = g_ref[...], u_ref[...]
    sig = jax.nn.sigmoid(g)
    out_ref[0] = (share * u * sig * (1.0 + g * (1.0 - sig))).astype(BF)
    out_ref[1] = (share * g * sig).astype(BF)


def add_part(got_ref, part_ref, out_ref):
    out_ref[...] = (got_ref[...].astype(F32) + part_ref[...]).astype(BF)


def add_parts(second_ref, part_ref, first_ref, next_ref, third_ref, pass_ref):
    add_part(second_ref, part_ref, third_ref)
    add_part(first_ref, next_ref, pass_ref)


def partial_sums(grads_ref, w_ref, part_ref, rest_ref):
    part = dot(grads_ref[...], w_ref[...], LAST)
    part_ref[...] = part
    rest_ref[...] = part[part.shape[0] // 2 :].astype(BF)


def arrange(turn, where_ref, *refs):
    out_ref, rows = refs[4], refs[0].shape[0]
    for r, block in enumerate(refs[:4]):
        at = pl.multiple_of(place(r ^ where_ref[2], where_ref[0]) * rows, rows)
        if turn:
            out_ref[:, pl.ds(at, rows)] = block[...].T
        else:
            out_ref[pl.ds(at, rows), :] = block[...]


def first_partial_sums(where_ref, *refs):
    blocks, w_ref, part_ref, rest_ref, grads_ref = refs[:4], *refs[4:]

    @pl.when(pl.program_id(0) == 0)
    def _():
        arrange(False, where_ref, *blocks, grads_ref)

    partial_sums(grads_ref, w_ref, part_ref, rest_ref)


def hidden_values(g_ref, u_ref, out_ref):
    g = g_ref[...]
    out_ref[...] = (g * jax.nn.sigmoid(g) * u_ref[...]).astype(BF)


def joined(own, pair, near, near_end, far, far_end):
    return jnp.concatenate([own, pair, near + near_end, far + far_end], axis=0)


def input_sums(piece_refs, held, wg_ref, wu_ref):
    @pl.when(pl.program_id(0) == 0)
    def _():
        for which in range(2):
            held[which] = joined(*[r[which] for r in piece_refs])

    return dot(held[0], wg_ref[...], LAST) + dot(held[1], wu_ref[...], LAST)


def input_sums_first(*refs):
    refs[8][...] = input_sums(refs[:6], refs[9], *refs[6:8])


def input_sums_last(where_ref, *refs):
    mine_ref, other_ref, held, total = refs[9:]
    total[...] = refs[8][...] + input_sums(refs[:6], held, *refs[6:8])
    half = total.shape[0] // 8
    z, core = where_ref[0], where_ref[2] % 2
    for k in range(4):
        start = place(k, z) * 2
        rows = slice(k * half, (k + 1) * half)
        mine_ref[rows, :] = total[pl.ds(pl.multiple_of((start + core) * half, half), half), :]
        other_ref[rows, :] = total[pl.ds(pl.multiple_of((start + 1 - core) * half, half), half), :].astype(BF)


def weight_grads(inputs_ref, *refs):
    gate_ref, up_ref = refs[-2:]
    gate_ref[...] = dot(inputs_ref[...], joined(*[r[0] for r in refs[:6]]), STRAIGHT).astype(BF)
    up_ref[...] = dot(inputs_ref[...], joined(*[r[1] for r in refs[:6]]), STRAIGHT).astype(BF)


def down_grads(grads_ref, *refs):
    own, pair, pair_end, *rest = [r[...] for r in refs[:7]]
    refs[-1][...] = dot(joined(own, pair + pair_end, *rest), grads_ref[...], LEAD).astype(BF)


def split_again(where_ref, mine_ref, got_ref, keep_ref, y_ref, x_ref, xy_ref):
    rows = keep_ref.shape[0]
    o, half = where_ref[1], where_ref[2] // 2

    def summed(to_o, to_half):
        at = pl.ds(pl.multiple_of((2 * to_o + to_half) * rows, rows), rows)
        return mine_ref[at, :] + got_ref[at, :].astype(F32)

    keep_ref[...] = summed(o, half)
    y_ref[...] = summed(1 - o, half).astype(BF)
    x_ref[...] = summed(o, 1 - half).astype(BF)
    xy_ref[...] = summed(1 - o, 1 - half).astype(BF)


def add_last(keep_ref, y_ref, x_ref, xy_ref, out_ref):
    total = keep_ref[...] + y_ref[...].astype(F32) + x_ref[...].astype(F32) + xy_ref[...].astype(F32)
    out_ref[...] = total.astype(BF)


def shape(dims, dtype):
    return jax.ShapeDtypeStruct(dims, dtype)


def line_of_four(saved_input, saved_gate, saved_up, out_grad, w_gate, w_up, w_down):
    rows, ff = saved_gate.shape
    depth = w_gate.shape[0]
    tokens = 4 * rows
    z, o, t = lax.axis_index("inp"), lax.axis_index("out"), lax.axis_index("tok")
    where = jnp.stack([z, o, t]).astype(jnp.int32)
    chain = Chain(jnp.zeros((8, 128), F32))
    step = ff // 14
    widths = [c * step for c in CUTS]
    cuts = [(sum(widths[:c]), w) for c, w in enumerate(widths)]

    def cols(height, tile, start, row=0):
        return pl.BlockSpec((height, tile), lambda j, *_: (row, start // tile + j))

    def whole(*dims):
        return pl.BlockSpec(dims, lambda *_: (0,) * len(dims))

    def gathered(x):
        other = lax.ppermute(x, "tok", X_SWAP)
        return x, lax.ppermute(x, "tok", CORE_SWAP), other, lax.ppermute(other, "tok", CORE_SWAP)

    def hidden_of():
        tile = ff // 7
        return chain.call(
            hidden_values,
            (7,),
            (saved_gate, saved_up),
            [cols(rows, tile, 0)] * 2,
            [shape((rows, ff), BF)],
            [cols(rows, tile, 0)],
        )[0]

    def partial(c):
        start, w = cuts[c]
        tile = TILE
        w_spec = pl.BlockSpec((tile, depth), lambda j, *_: (start // tile + j, 0))
        outs = [shape((tokens, w), F32), shape((tokens // 2, w), BF)]
        specs = [cols(tokens, tile, 0), cols(tokens // 2, tile, 0)]
        if c:
            part, rest = chain.call(
                partial_sums, (w // tile,), (grads, w_down), [whole(tokens, depth), w_spec], outs, specs
            )
            given = grads
        else:
            part, rest, given = chain.call(
                first_partial_sums,
                (w // tile,),
                (*gathered(out_grad), w_down),
                [whole(rows, depth)] * 4 + [w_spec],
                [*outs, shape((tokens, depth), BF)],
                [*specs, whole(tokens, depth)],
                scalars=where,
            )
        return given, part, send(rest, ENDS_IN)

    def pass_on(c):
        w = widths[c]
        tile = TILE
        second = chain.call(
            add_part,
            (w // tile,),
            (firsts[c], parts[c]),
            [cols(2 * rows, tile, 0), cols(2 * rows, tile, 0, 1)],
            [shape((2 * rows, w), BF)],
            [cols(2 * rows, tile, 0)],
        )[0]
        seconds[c] = send(second, MIDDLE)

    def hand_out(c):
        w = widths[c]
        third_in = [cols(rows, w, 0, 1)] * 2
        if c + 1 == len(cuts):
            third = chain.call(
                add_part, (1,), (seconds[c], parts[c]), third_in, [shape((rows, w), BF)], [whole(rows, w)]
            )[0]
        else:
            v = widths[c + 1]
            third, second = chain.call(
                add_parts,
                (1,),
                (seconds[c], parts[c], firsts[c + 1], parts[c + 1]),
                [*third_in, whole(2 * rows, v), cols(2 * rows, v, 0, 1)],
                [shape((rows, w), BF), shape((2 * rows, v), BF)],
                [whole(rows, w), whole(2 * rows, v)],
            )
            seconds[c + 1] = send(second, MIDDLE)
        thirds[c] = send(third, PAIRS)

    def grads_of(c):
        start, w = cuts[c]
        tile = TILE
        own = chain.call(
            swiglu_grads,
            (w // tile,),
            (parts[c], seconds[c], thirds[c], saved_gate, saved_up),
            [cols(rows, tile, 0)] * 3 + [cols(rows, tile, start)] * 2,
            [shape((2, rows, w), BF)],
            [pl.BlockSpec((2, rows, tile), lambda j: (0, 0, j))],
        )[0]
        return spread(own)

    def spread(own):
        return {"own": own, "pair": send(own, PAIRS), "near": send(own, MIDDLE)}

    def spread_far(x, *others):
        x["pair"], x["near"], *others = chain.relay(x["pair"], x["near"], *others)
        x["near_end"] = send(x["near"], OUTWARD)
        x["far"] = send(x["pair"], MIDDLE)
        return others

    def spread_end(x, *others):
        x["far"], *others = chain.relay(x["far"], *others)
        x["far_end"] = send(x["far"], OUTWARD)
        return others

    def pieces(x):
        return [x[k] for k in ("own", "pair", "near", "near_end", "far", "far_end")]

    def input_step(c, before):
        start, w = cuts[c]
        tile = TILE
        first, last = before is None, c + 1 == len(cuts)
        wide = pl.BlockSpec((pl.Element(tile), pl.Element(w)), lambda j, *_: (j * tile, start))
        across = cols(tokens, tile, 0)
        held = [pltpu.VMEM((2, tokens, w), BF)]
        ins = [*pieces(groups[c]), w_gate, w_up]
        specs = [whole(2, rows, w)] * 6 + [wide, wide]
        if first:
            return chain.call(
                input_sums_first, (depth // tile,), ins, specs, [shape((tokens, depth), F32)], [across], scratch=held
            )[0]
        return chain.call(
            input_sums_last,
            (depth // tile,),
            [*ins, before],
            [*specs, across],
            [shape((tokens // 2, depth), F32), shape((tokens // 2, depth), BF)],
            [cols(tokens // 2, tile, 0)] * 2,
            scalars=where,
            scratch=[*held, pltpu.VMEM((tokens, tile), F32)],
        )

    def weights_step(c, before):
        start, w = cuts[c]
        tile = TILE
        return chain.call(
            weight_grads,
            (w // tile,),
            (inputs, *pieces(groups[c]), *before),
            [whole(depth, tokens)] + [pl.BlockSpec((2, rows, tile), lambda j: (0, 0, j))] * 6 + [ANY] * len(before),
            [shape((depth, ff), BF)] * 2,
            [cols(depth, tile, start)] * 2,
            aliases=[(7, 0), (8, 1)] if before else (),
        )

    def down_step():
        tile = TILE
        return chain.call(
            down_grads,
            (ff // tile,),
            [grads, *[h[k] for k in ("own", "pair", "pair_end", "near", "near_end", "far", "far_end")]],
            [whole(tokens, depth)] + [cols(rows, tile, 0)] * 7,
            [shape((ff, depth), BF)],
            [pl.BlockSpec((tile, depth), lambda j, *_: (j, 0))],
        )[0]

    n = len(cuts)
    parts, firsts, seconds, thirds, groups = ([None] * n for _ in range(5))
    h = {"own": hidden_of()}
    h["pair_end"] = send(h["own"], OUTWARD)
    h["near"] = send(h["own"], MIDDLE)
    grads, parts[0], firsts[0] = partial(0)
    _, parts[1], firsts[1] = partial(1)
    h["near"], h["pair_end"], h_again = chain.relay(h["near"], h["pair_end"], h["own"])
    h["near_end"] = send(h["near"], OUTWARD)
    pass_on(0)
    hand_out(0)
    (h["near_end"],) = chain.relay(h["near_end"])
    groups[0] = grads_of(0)
    hand_out(1)
    h_again, = spread_far(groups[0], h_again)
    h["pair"] = send(h_again, ENDS_IN)
    groups[1] = grads_of(1)
    (inputs_b,) = spread_end(groups[0], saved_input.astype(BF))
    inputs = chain.call(
        functools.partial(arrange, True),
        (1,),
        gathered(inputs_b),
        [whole(rows, depth)] * 4,
        [shape((depth, tokens), BF)],
        [whole(depth, tokens)],
        scalars=where,
    )[0]
    (h["pair"],) = chain.relay(h["pair"])
    h["far"] = send(h["pair"], MIDDLE)
    (groups[0]["near_end"],) = spread_far(groups[1], groups[0]["near_end"])
    h["far"], groups[0]["far_end"] = spread_end(groups[1], h["far"], groups[0]["far_end"])
    h["far_end"] = send(h["far"], OUTWARD)
    total = input_step(0, None)
    weights = weights_step(0, ())
    mine, other = input_step(1, total)
    got = lax.ppermute(other, "tok", CORE_SWAP)
    keep, *others = chain.call(
        split_again,
        (1,),
        (mine, got),
        [whole(tokens // 2, depth)] * 2,
        [shape((rows // 2, depth), F32), *[shape((rows // 2, depth), BF)] * 3],
        [whole(rows // 2, depth)] * 4,
        scalars=where,
    )
    got = (
        lax.ppermute(others[2], ("out", "tok"), XY_SWAP),
        lax.ppermute(others[0], "out", Y_SWAP),
        lax.ppermute(others[1], "tok", X_SWAP),
    )
    weights = weights_step(1, weights)
    result = chain.call(
        add_last,
        (1,),
        (keep, got[1], got[2], got[0]),
        [whole(rows // 2, depth)] * 4,
        [shape((rows // 2, depth), BF)],
        [whole(rows // 2, depth)],
    )[0]
    down = down_step()
    return result, weights[0], weights[1], down


def any_line(saved_input, saved_gate, saved_up, out_grad, w_gate, w_up, w_down):
    inputs = lax.all_gather(saved_input.astype(BF), "tok", axis=0, tiled=True)
    grads = lax.all_gather(out_grad, "tok", axis=0, tiled=True)
    part = dot(grads, w_down, LAST)
    share = lax.psum_scatter(part, "inp", scatter_dimension=0, tiled=True)
    sig = jax.nn.sigmoid(saved_gate)
    gate = share * saved_up * sig * (1.0 + saved_gate * (1.0 - sig))
    up = share * saved_gate * sig
    hidden = saved_gate * sig * saved_up
    gate, up, hidden = (
        lax.all_gather(v.astype(BF), "inp", axis=0, tiled=True) for v in (gate, up, hidden)
    )
    total = dot(gate, w_gate, LAST) + dot(up, w_up, LAST)
    total = lax.psum_scatter(total, ("out", "tok"), scatter_dimension=0, tiled=True)
    return (
        total.astype(BF),
        dot(inputs, gate, LEAD).astype(BF),
        dot(inputs, up, LEAD).astype(BF),
        dot(hidden, grads, LEAD).astype(BF),
    )


def solution(mesh):
    sizes = dict(mesh.shape)
    placed = (
        P("tok", "inp"),
        P("inp", ("out", "tok")),
        P("inp", ("out", "tok")),
        P("tok", "inp"),
        P("inp", ("out", "tok")),
        P("inp", ("out", "tok")),
        P(("out", "tok"), "inp"),
    )

    def local(*args):
        rows, ff = args[1].shape
        fits = (sizes["inp"], sizes["out"], sizes["tok"]) == (4, 2, 4)
        if fits and rows % 32 == 0 and ff % 3584 == 0:
            return line_of_four(*args)
        return any_line(*args)

    return jax.shard_map(
        local,
        mesh=mesh,
        in_specs=placed,
        out_specs=(
            P(("out", "tok"), "inp"),
            P("inp", ("out", "tok")),
            P("inp", ("out", "tok")),
            P(("out", "tok"), "inp"),
        ),
        check_vma=False,
    )
```

time: 461 us -> 303 us (0.66)
  waiting for transfers between devices: 365 us -> 119 us
  Pallas kernels: 0 us -> 106 us
  starting transfers between devices: 0.46 us -> 68.4 us
  matrix products: 53 us -> 0 us
  local copies, waits for them, and re-layouts: 20.1 us -> 3.5 us
  between operations: 14.2 us -> 0.76 us
  other arithmetic: 7.03 us -> 2.38 us
    all_gather x5 -> x0, waiting for transfers between devices: 201 us -> none  [the longest x1 70.6 us: local(): lax.all_gather(gate_part, 'inp', axis=0, tiled=True)]
    reduce_scatter x2 -> x0, waiting for transfers between devices: 163 us -> none  [the longest x1 128 us: local(): lax.psum_scatter(lax.dot_general(all_grads, w_down, last_dims, preferred_...]
    ppermute x0 -> x32, waiting for transfers between devices: none -> 119 us  [the longest x22 102 us: send(): return lax.ppermute(x, 'inp', perm)]
    pallas_call x0 -> x23, Pallas kernels: none -> 106 us  [call(): pl.pallas_call(kernel, grid_spec=pltpu.PrefetchScalarGridSpec(num_scalar_...]
    ppermute x0 -> x32, starting transfers between devices: none -> 68.4 us  [the longest x22 60.4 us: send(): return lax.ppermute(x, 'inp', perm)]
    dot_general x6 -> x0, matrix products: 53 us -> none  [the longest x1 10.5 us: local(): lax.dot_general(all_grads, w_down, last_dims, preferred_element_type=jnp....]
    unnamed x10 -> x7, local copies, waits for them, and re-layouts: 20.1 us -> 2.91 us
    convert_element_type x3 -> x1, other arithmetic: 7.03 us -> 1.78 us  [line_of_four(): inputs_b, = spread_end(groups[0], saved_input.astype(BF))]
  transfers between devices with their start and end apart: 7 -> 32, of which waited for: 7 -> 14; matrix products, arithmetic and copies ran while one was open for 14% -> 2% of each run, Pallas kernels for 0% -> 31%
where the time goes in v1:
time: 303 us; the launch traced here: 301 us
  waiting for transfers between devices  119 us (39%)
  Pallas kernels  106 us (35%)
  starting transfers between devices  68.4 us (23%)
  local copies, waits for them, and re-layouts  3.5 us (1%)
    pallas_call x23, Pallas kernels, call(): pl.pallas_call(kernel, grid_spec=pltpu.PrefetchScalarGridSpec(num_scalar_...  106 us
    ppermute x22, waiting for transfers between devices, send(): return lax.ppermute(x, 'inp', perm)  102 us
    ppermute x22, starting transfers between devices, send(): return lax.ppermute(x, 'inp', perm)  60.4 us
    ppermute x2, waiting for transfers between devices, gathered(): other = lax.ppermute(x, 'tok', X_SWAP)  11.8 us
  transfers between devices with their start and end apart: 32, of which 14 were waited for; matrix products, arithmetic and copies ran while one was open for 2% of the time, Pallas kernels for 31%

profile of v1, /device:TPU:0, one launch (start us, length us, event | category | flops | bytes accessed | tf_op | source)
XLA Modules:
  0.0 300.7 jit_solution(11752810489824092979)
XLA Ops:
  3.6 6.6 %collective-permute-done.1.refs_4_ = bf16[128,1024]{1,0:T(8,128)(2,1)} collective-permute-done((bf16[128,1024]{1,0:T(8,128)(2,1)}, bf16[128,1024]{1,0:T(8,128)(2,1)}, u32[]{:S(2)}, u32[]{:S(2)}) %collective-permute-start.1) | collective-permute-done | bytes 262176 | tf_op jit(solution)/shard_map/ppermute | solution.py:211
  10.9 5.4 %shard_map.102 = (f32[8,128]{1,0:T(8,128)}, bf16[128,3584]{1,0:T(8,128)(2,1)}) custom-call(f32[8,128]{1,0:T(8,128)} %broadcast_in_dim.3.refs_0_, f32[128,3584]{1,0:T(8,128)} %refs_4_.3, f32[128,3584]{1,0:T(8,128)} %refs_5_.3), custom_call_target="tpu_custom_call", output_to_operand_aliasing={{0}: (0, {})} | custom-call | tf_op jit(solution)/shard_map/pallas_call | solution.py:50
  19.7 8.8 %shard_map.103 = (f32[8,128]{1,0:T(8,128)}, f32[512,1792]{1,0:T(8,128)}, bf16[256,1792]{1,0:T(8,128)(2,1)}, bf16[512,1024]{1,0:T(8,128)(2,1)}) custom-call(s32[3]{0:T(128)} %pad_add_fusion.refs_0_, f32[8,128]{1,0:T(8,128)} %get-tuple-element.68.refs_1_, bf16[128,1024]{1,0:T(8,128)(2,1)} %refs_2_.4, ...), custom_call_target="tpu_custom_call", output_to_operand_aliasing={{0}: (1, {})} | custom-call | tf_op jit(solution)/shard_map/pallas_call | solution.py:50
  28.5 7.5 %collective-permute-start.5 = (bf16[256,1792]{1,0:T(8,128)(2,1)}, bf16[256,1792]{1,0:T(8,128)(2,1)}, u32[]{:S(2)}, u32[]{:S(2)}) collective-permute-start(bf16[256,1792]{1,0:T(8,128)(2,1)} %get-tuple-element.74), channel_id=1, source_target_pairs={{0,8},{24,16},{1,9},{25,17},{2,10},{26,18},{3,11},{27,19},{4,12},{... | collective-permute-start | bytes 2752520 | tf_op jit(solution)/shard_map/ppermute | solution.py:28
  38.2 8.1 %shard_map.104 = (f32[8,128]{1,0:T(8,128)}, f32[512,1792]{1,0:T(8,128)}, bf16[256,1792]{1,0:T(8,128)(2,1)}) custom-call(f32[8,128]{1,0:T(8,128)} %get-tuple-element.69.refs_0_, bf16[512,1024]{1,0:T(8,128)(2,1)} %get-tuple-element.70.refs_1_, bf16[3584,1024]{1,0:T(8,128)(2,1)} %refs_2_.5), custom_call_target="tpu_custom_call", output_to_operand_aliasing={{0}: (0, {})} | custom-call | tf_op jit(solution)/shard_map/pallas_call | solution.py:50
  48.5 7.5 %collective-permute-done.5.refs_1_ = bf16[256,1792]{1,0:T(8,128)(2,1)} collective-permute-done((bf16[256,1792]{1,0:T(8,128)(2,1)}, bf16[256,1792]{1,0:T(8,128)(2,1)}, u32[]{:S(2)}, u32[]{:S(2)}) %collective-permute-start.5) | collective-permute-done | bytes 917536 | tf_op jit(solution)/shard_map/ppermute | solution.py:28
  64.2 10.9 %collective-permute-done.7.refs_3_ = bf16[256,1792]{1,0:T(8,128)(2,1)} collective-permute-done((bf16[256,1792]{1,0:T(8,128)(2,1)}, bf16[256,1792]{1,0:T(8,128)(2,1)}, u32[]{:S(2)}, u32[]{:S(2)}) %collective-permute-start.7) | collective-permute-done | bytes 917536 | tf_op jit(solution)/shard_map/ppermute | solution.py:28
  78.4 12.0 %collective-permute-start.9 = (bf16[128,1792]{1,0:T(8,128)(2,1)}, bf16[128,1792]{1,0:T(8,128)(2,1)}, u32[]{:S(2)}, u32[]{:S(2)}) collective-permute-start(bf16[128,1792]{1,0:T(8,128)(2,1)} %get-tuple-element.83), channel_id=1, source_target_pairs={{0,8},{8,0},{16,24},{24,16},{1,9},{9,1},{17,25},{25,17},{2,10},{10... | collective-permute-start | bytes 1376264 | tf_op jit(solution)/shard_map/ppermute | solution.py:28
  92.0 7.3 %collective-permute-done.9.refs_3_ = bf16[128,1792]{1,0:T(8,128)(2,1)} collective-permute-done((bf16[128,1792]{1,0:T(8,128)(2,1)}, bf16[128,1792]{1,0:T(8,128)(2,1)}, u32[]{:S(2)}, u32[]{:S(2)}) %collective-permute-start.9) | collective-permute-done | bytes 458784 | tf_op jit(solution)/shard_map/ppermute | solution.py:28
  99.3 5.6 %shard_map.109 = (f32[8,128]{1,0:T(8,128)}, bf16[2,128,1792]{2,1,0:T(8,128)(2,1)}) custom-call(f32[8,128]{1,0:T(8,128)} %get-tuple-element.82.refs_0_, f32[512,1792]{1,0:T(8,128)} %get-tuple-element.75.refs_2_.refs_1_, bf16[256,1792]{1,0:T(8,128)(2,1)} %collective-permute-done.6.refs_1_.refs_2_, ...), custom_call_target="tpu_custom_call", output_to_operand_aliasing={{0}: (0, {})} | custom-call | tf_op jit(solution)/shard_map/pallas_call | solution.py:50
  110.3 14.3 %collective-permute-done.11.refs_1_ = bf16[2,128,1792]{2,1,0:T(8,128)(2,1)} collective-permute-done((bf16[2,128,1792]{2,1,0:T(8,128)(2,1)}, bf16[2,128,1792]{2,1,0:T(8,128)(2,1)}, u32[]{:S(2)}, u32[]{:S(2)}) %collective-permute-start.11) | collective-permute-done | bytes 917536 | tf_op jit(solution)/shard_map/ppermute | solution.py:28
  126.3 9.7 %collective-permute-start.13 = (bf16[128,1792]{1,0:T(8,128)(2,1)}, bf16[128,1792]{1,0:T(8,128)(2,1)}, u32[]{:S(2)}, u32[]{:S(2)}) collective-permute-start(bf16[128,1792]{1,0:T(8,128)(2,1)} %get-tuple-element.90), channel_id=1, source_target_pairs={{0,8},{8,0},{16,24},{24,16},{1,9},{9,1},{17,25},{25,17},{2,10},{10... | collective-permute-start | bytes 1376264 | tf_op jit(solution)/shard_map/ppermute | solution.py:28
  138.9 8.4 %collective-permute-done.13.refs_3_ = bf16[128,1792]{1,0:T(8,128)(2,1)} collective-permute-done((bf16[128,1792]{1,0:T(8,128)(2,1)}, bf16[128,1792]{1,0:T(8,128)(2,1)}, u32[]{:S(2)}, u32[]{:S(2)}) %collective-permute-start.13) | collective-permute-done | bytes 458784 | tf_op jit(solution)/shard_map/ppermute | solution.py:28
  147.3 5.5 %shard_map.112 = (f32[8,128]{1,0:T(8,128)}, bf16[2,128,1792]{2,1,0:T(8,128)(2,1)}) custom-call(f32[8,128]{1,0:T(8,128)} %get-tuple-element.89.refs_0_, f32[512,1792]{1,0:T(8,128)} %get-tuple-element.79.refs_4_.refs_2_.refs_1_, bf16[256,1792]{1,0:T(8,128)(2,1)} %collective-permute-done.10.refs_1_.refs_2_, ...), custom_call_target="tpu_custom_call", output_to_operand_aliasing={{0}: (0, {})} | custom-call | tf_op jit(solution)/shard_map/pallas_call | solution.py:50
  161.3 5.2 %collective-permute-done.16.refs_4_ = bf16[128,1024]{1,0:T(8,128)(2,1)S(1)} collective-permute-done((bf16[128,1024]{1,0:T(8,128)(2,1)}, bf16[128,1024]{1,0:T(8,128)(2,1)S(1)}, u32[]{:S(2)}, u32[]{:S(2)}) %collective-permute-start.16) | collective-permute-done | bytes 262176 | tf_op jit(solution)/shard_map/ppermute | solution.py:211
  175.0 7.2 %collective-permute-done.19.refs_1_ = bf16[2,128,1792]{2,1,0:T(8,128)(2,1)} collective-permute-done((bf16[2,128,1792]{2,1,0:T(8,128)(2,1)}, bf16[2,128,1792]{2,1,0:T(8,128)(2,1)}, u32[]{:S(2)}, u32[]{:S(2)}) %collective-permute-start.19) | collective-permute-done | bytes 917536 | tf_op jit(solution)/shard_map/ppermute | solution.py:28
  182.2 14.3 %collective-permute-done.21.refs_3_ = bf16[2,128,1792]{2,1,0:T(8,128)(2,1)} collective-permute-done((bf16[2,128,1792]{2,1,0:T(8,128)(2,1)}, bf16[2,128,1792]{2,1,0:T(8,128)(2,1)}, u32[]{:S(2)}, u32[]{:S(2)}) %collective-permute-start.21) | collective-permute-done | bytes 917536 | tf_op jit(solution)/shard_map/ppermute | solution.py:28
  201.0 15.2 %collective-permute-done.24.refs_3_ = bf16[2,128,1792]{2,1,0:T(8,128)(2,1)} collective-permute-done((bf16[2,128,1792]{2,1,0:T(8,128)(2,1)}, bf16[2,128,1792]{2,1,0:T(8,128)(2,1)}, u32[]{:S(2)}, u32[]{:S(2)}) %collective-permute-start.24) | collective-permute-done | bytes 917536 | tf_op jit(solution)/shard_map/ppermute | solution.py:28
  218.8 9.5 %shard_map.118 = (f32[8,128]{1,0:T(8,128)}, f32[512,1024]{1,0:T(8,128)}) custom-call(f32[8,128]{1,0:T(8,128)} %get-tuple-element.104.refs_0_, bf16[2,128,1792]{2,1,0:T(8,128)(2,1)} %get-tuple-element.87.refs_1_.refs_2_, bf16[2,128,1792]{2,1,0:T(8,128)(2,1)} %get-tuple-element.92.refs_2_.refs_3_, ...), custom_call_target="tpu_custom_call", output_to_operand_aliasing={{0}: (0, {})} | custom-call | tf_op jit(solution)/shard_map/pallas_call | solution.py:50
  228.3 10.3 %shard_map.119 = (f32[8,128]{1,0:T(8,128)}, bf16[1024,3584]{1,0:T(8,128)(2,1)}, bf16[1024,3584]{1,0:T(8,128)(2,1)}) custom-call(f32[8,128]{1,0:T(8,128)} %get-tuple-element.107.refs_0_, bf16[1024,512]{1,0:T(8,128)(2,1)} %get-tuple-element.108.refs_1_, bf16[2,128,1792]{2,1,0:T(8,128)(2,1)} %get-tuple-element.87.refs_1_.refs_2_, ...), custom_call_target="tpu_custom_call", output_to_operand_aliasing={{0}: (0, {})} | custom-call | tf_op jit(solution)/shard_map/pallas_call | solution.py:50
  238.6 16.9 %collective-permute-done.26.refs_7_ = bf16[2,128,1792]{2,1,0:T(8,128)(2,1)} collective-permute-done((bf16[2,128,1792]{2,1,0:T(8,128)(2,1)}, bf16[2,128,1792]{2,1,0:T(8,128)(2,1)}, u32[]{:S(2)}, u32[]{:S(2)}) %collective-permute-start.26) | collective-permute-done | bytes 917536 | tf_op jit(solution)/shard_map/ppermute | solution.py:28
  255.5 10.8 %shard_map.120 = (f32[8,128]{1,0:T(8,128)}, f32[256,1024]{1,0:T(8,128)}, bf16[256,1024]{1,0:T(8,128)(2,1)}) custom-call(s32[3]{0:T(128)} %pad_add_fusion.refs_0_, f32[8,128]{1,0:T(8,128)} %get-tuple-element.109.refs_1_, bf16[2,128,1792]{2,1,0:T(8,128)(2,1)} %get-tuple-element.98.refs_2_, ...), custom_call_target="tpu_custom_call", output_to_operand_aliasing={{0}: (1, {})} | custom-call | tf_op jit(solution)/shard_map/pallas_call | solution.py:50
  275.0 10.3 %shard_map.122 = (f32[8,128]{1,0:T(8,128)}, bf16[1024,3584]{1,0:T(8,128)(2,1)}, bf16[1024,3584]{1,0:T(8,128)(2,1)}) custom-call(f32[8,128]{1,0:T(8,128)} %get-tuple-element.116.refs_0_, bf16[1024,512]{1,0:T(8,128)(2,1)} %get-tuple-element.108.refs_1_, ...), custom_call_target="tpu_custom_call", output_to_operand_aliasing={{0}: (0, {}), {1}: (8, {}), {2}: (9, {})} | custom-call | tf_op jit(solution)/shard_map/pallas_call | solution.py:50
  287.2 13.5 %shard_map.124 = (f32[8,128]{1,0:T(8,128)}, bf16[3584,1024]{1,0:T(8,128)(2,1)}) custom-call(f32[8,128]{1,0:T(8,128)} %get-tuple-element.127.refs_0_, bf16[512,1024]{1,0:T(8,128)(2,1)} %get-tuple-element.70.refs_1_, bf16[128,3584]{1,0:T(8,128)(2,1)} %get-tuple-element.72.refs_2_, ...), custom_call_target="tpu_custom_call", output_to_operand_aliasing={{0}: (0, {})} | custom-call | tf_op jit(solution)/shard_map/pallas_call | solution.py:50
  (73 shorter events, 69.1 us)
Async XLA Ops:
  3.6 16.1 %collective-permute-start = (bf16[128,1024]{1,0:T(8,128)(2,1)}, bf16[128,1024]{1,0:T(8,128)(2,1)}, u32[]{:S(2)}, u32[]{:S(2)}) collective-permute-start(bf16[128,1024]{1,0:T(8,128)(2,1)} %refs_2_.4), channel_id=1, source_target_pairs={{0,1},{1,0},{2,3},{3,2},{4,5},{5,4},{6,7},{7,6},{8,9},{9,8},{10,11... | collective-permute-start | bytes 786440 | tf_op jit(solution)/shard_map/ppermute | solution.py:212
  16.2 32.3 %collective-permute-start.3 = (bf16[128,3584]{1,0:T(8,128)(2,1)}, bf16[128,3584]{1,0:T(8,128)(2,1)}, u32[]{:S(2)}, u32[]{:S(2)}) collective-permute-start(bf16[128,3584]{1,0:T(8,128)(2,1)} %get-tuple-element.72.refs_2_), channel_id=1, source_target_pairs={{8,16},{16,8},{9,17},{17,9},{10,18},{18,10},{11,19},{19,11},{12,20... | collective-permute-start | bytes 2752520 | tf_op jit(solution)/shard_map/ppermute | solution.py:28
  17.8 30.7 %collective-permute-start.4 = (bf16[128,3584]{1,0:T(8,128)(2,1)}, bf16[128,3584]{1,0:T(8,128)(2,1)}, u32[]{:S(2)}, u32[]{:S(2)}) collective-permute-start(bf16[128,3584]{1,0:T(8,128)(2,1)} %get-tuple-element.72.refs_2_), channel_id=1, source_target_pairs={{8,0},{16,24},{9,1},{17,25},{10,2},{18,26},{11,3},{19,27},{12,4},{... | collective-permute-start | bytes 2752520 | tf_op jit(solution)/shard_map/ppermute | solution.py:28
  28.5 27.6 %collective-permute-start.5 = (bf16[256,1792]{1,0:T(8,128)(2,1)}, bf16[256,1792]{1,0:T(8,128)(2,1)}, u32[]{:S(2)}, u32[]{:S(2)}) collective-permute-start(bf16[256,1792]{1,0:T(8,128)(2,1)} %get-tuple-element.74), channel_id=1, source_target_pairs={{0,8},{24,16},{1,9},{25,17},{2,10},{26,18},{3,11},{27,19},{4,12},{... | collective-permute-start | bytes 2752520 | tf_op jit(solution)/shard_map/ppermute | solution.py:28
  46.3 28.7 %collective-permute-start.7 = (bf16[256,1792]{1,0:T(8,128)(2,1)}, bf16[256,1792]{1,0:T(8,128)(2,1)}, u32[]{:S(2)}, u32[]{:S(2)}) collective-permute-start(bf16[256,1792]{1,0:T(8,128)(2,1)} %get-tuple-element.78), channel_id=1, source_target_pairs={{0,8},{24,16},{1,9},{25,17},{2,10},{26,18},{3,11},{27,19},{4,12},{... | collective-permute-start | bytes 2752520 | tf_op jit(solution)/shard_map/ppermute | solution.py:28
  61.2 13.8 %collective-permute-start.6 = (bf16[256,1792]{1,0:T(8,128)(2,1)}, bf16[256,1792]{1,0:T(8,128)(2,1)}, u32[]{:S(2)}, u32[]{:S(2)}) collective-permute-start(bf16[256,1792]{1,0:T(8,128)(2,1)} %get-tuple-element.77), channel_id=1, source_target_pairs={{8,16},{16,8},{9,17},{17,9},{10,18},{18,10},{11,19},{19,11},{12,20... | collective-permute-start | bytes 2752520 | tf_op jit(solution)/shard_map/ppermute | solution.py:28
  62.9 29.1 %collective-permute-start.8 = (bf16[128,3584]{1,0:T(8,128)(2,1)}, bf16[128,3584]{1,0:T(8,128)(2,1)}, u32[]{:S(2)}, u32[]{:S(2)}) collective-permute-start(bf16[128,3584]{1,0:T(8,128)(2,1)} %get-tuple-element.81.refs_5_), channel_id=1, source_target_pairs={{8,0},{16,24},{9,1},{17,25},{10,2},{18,26},{11,3},{19,27},{12,4},{... | collective-permute-start | bytes 2752520 | tf_op jit(solution)/shard_map/ppermute | solution.py:28
  78.4 20.9 %collective-permute-start.9 = (bf16[128,1792]{1,0:T(8,128)(2,1)}, bf16[128,1792]{1,0:T(8,128)(2,1)}, u32[]{:S(2)}, u32[]{:S(2)}) collective-permute-start(bf16[128,1792]{1,0:T(8,128)(2,1)} %get-tuple-element.83), channel_id=1, source_target_pairs={{0,8},{8,0},{16,24},{24,16},{1,9},{9,1},{17,25},{25,17},{2,10},{10... | collective-permute-start | bytes 1376264 | tf_op jit(solution)/shard_map/ppermute | solution.py:28
  90.4 17.8 %collective-permute-start.10 = (bf16[256,1792]{1,0:T(8,128)(2,1)}, bf16[256,1792]{1,0:T(8,128)(2,1)}, u32[]{:S(2)}, u32[]{:S(2)}) collective-permute-start(bf16[256,1792]{1,0:T(8,128)(2,1)} %get-tuple-element.85), channel_id=1, source_target_pairs={{8,16},{16,8},{9,17},{17,9},{10,18},{18,10},{11,19},{19,11},{12,20... | collective-permute-start | bytes 2752520 | tf_op jit(solution)/shard_map/ppermute | solution.py:28
  104.8 19.9 %collective-permute-start.11 = (bf16[2,128,1792]{2,1,0:T(8,128)(2,1)}, bf16[2,128,1792]{2,1,0:T(8,128)(2,1)}, u32[]{:S(2)}, u32[]{:S(2)}) collective-permute-start(bf16[2,128,1792]{2,1,0:T(8,128)(2,1)} %get-tuple-element.87.refs_1_.refs_2_), channel_id=1, source_target_pairs={{0,8},{8,0},{16,24},{24,16},{1,9},{9,1},{17,25},{25,17},{2,10},{10... | collective-permute-start | bytes 2752520 | tf_op jit(solution)/shard_map/ppermute | solution.py:28
  106.6 18.1 %collective-permute-start.12 = (bf16[2,128,1792]{2,1,0:T(8,128)(2,1)}, bf16[2,128,1792]{2,1,0:T(8,128)(2,1)}, u32[]{:S(2)}, u32[]{:S(2)}) collective-permute-start(bf16[2,128,1792]{2,1,0:T(8,128)(2,1)} %get-tuple-element.87.refs_1_.refs_2_), channel_id=1, source_target_pairs={{8,16},{16,8},{9,17},{17,9},{10,18},{18,10},{11,19},{19,11},{12,20... | collective-permute-start | bytes 2752520 | tf_op jit(solution)/shard_map/ppermute | solution.py:28
  124.7 35.3 %collective-permute-start.14 = (bf16[2,128,1792]{2,1,0:T(8,128)(2,1)}, bf16[2,128,1792]{2,1,0:T(8,128)(2,1)}, u32[]{:S(2)}, u32[]{:S(2)}) collective-permute-start(bf16[2,128,1792]{2,1,0:T(8,128)(2,1)} %get-tuple-element.92.refs_2_.refs_3_), channel_id=1, source_target_pairs={{8,16},{16,8},{9,17},{17,9},{10,18},{18,10},{11,19},{19,11},{12,20... | collective-permute-start | bytes 2752520 | tf_op jit(solution)/shard_map/ppermute | solution.py:28
  126.3 21.0 %collective-permute-start.13 = (bf16[128,1792]{1,0:T(8,128)(2,1)}, bf16[128,1792]{1,0:T(8,128)(2,1)}, u32[]{:S(2)}, u32[]{:S(2)}) collective-permute-start(bf16[128,1792]{1,0:T(8,128)(2,1)} %get-tuple-element.90), channel_id=1, source_target_pairs={{0,8},{8,0},{16,24},{24,16},{1,9},{9,1},{17,25},{25,17},{2,10},{10... | collective-permute-start | bytes 1376264 | tf_op jit(solution)/shard_map/ppermute | solution.py:28
  136.0 39.0 %collective-permute-start.18 = (bf16[128,3584]{1,0:T(8,128)(2,1)}, bf16[128,3584]{1,0:T(8,128)(2,1)}, u32[]{:S(2)}, u32[]{:S(2)}) collective-permute-start(bf16[128,3584]{1,0:T(8,128)(2,1)} %get-tuple-element.96), channel_id=1, source_target_pairs={{0,8},{24,16},{1,9},{25,17},{2,10},{26,18},{3,11},{27,19},{4,12},{... | collective-permute-start | bytes 2752520 | tf_op jit(solution)/shard_map/ppermute | solution.py:28
  152.8 29.4 %collective-permute-start.19 = (bf16[2,128,1792]{2,1,0:T(8,128)(2,1)}, bf16[2,128,1792]{2,1,0:T(8,128)(2,1)}, u32[]{:S(2)}, u32[]{:S(2)}) collective-permute-start(bf16[2,128,1792]{2,1,0:T(8,128)(2,1)} %get-tuple-element.98.refs_2_), channel_id=1, source_target_pairs={{0,8},{8,0},{16,24},{24,16},{1,9},{9,1},{17,25},{25,17},{2,10},{10... | collective-permute-start | bytes 2752520 | tf_op jit(solution)/shard_map/ppermute | solution.py:28
  155.3 26.9 %collective-permute-start.20 = (bf16[2,128,1792]{2,1,0:T(8,128)(2,1)}, bf16[2,128,1792]{2,1,0:T(8,128)(2,1)}, u32[]{:S(2)}, u32[]{:S(2)}) collective-permute-start(bf16[2,128,1792]{2,1,0:T(8,128)(2,1)} %get-tuple-element.98.refs_2_), channel_id=1, source_target_pairs={{8,16},{16,8},{9,17},{17,9},{10,18},{18,10},{11,19},{19,11},{12,20... | collective-permute-start | bytes 2752520 | tf_op jit(solution)/shard_map/ppermute | solution.py:28
  156.9 39.7 %collective-permute-start.21 = (bf16[2,128,1792]{2,1,0:T(8,128)(2,1)}, bf16[2,128,1792]{2,1,0:T(8,128)(2,1)}, u32[]{:S(2)}, u32[]{:S(2)}) collective-permute-start(bf16[2,128,1792]{2,1,0:T(8,128)(2,1)} %get-tuple-element.99.refs_3_.refs_4_), channel_id=1, source_target_pairs={{8,0},{16,24},{9,1},{17,25},{10,2},{18,26},{11,3},{19,27},{12,4},{... | collective-permute-start | bytes 2752520 | tf_op jit(solution)/shard_map/ppermute | solution.py:28
  170.5 45.7 %collective-permute-start.24 = (bf16[2,128,1792]{2,1,0:T(8,128)(2,1)}, bf16[2,128,1792]{2,1,0:T(8,128)(2,1)}, u32[]{:S(2)}, u32[]{:S(2)}) collective-permute-start(bf16[2,128,1792]{2,1,0:T(8,128)(2,1)} %get-tuple-element.103.refs_5_.refs_6_), channel_id=1, source_target_pairs={{8,0},{16,24},{9,1},{17,25},{10,2},{18,26},{11,3},{19,27},{12,4},{... | collective-permute-start | bytes 2752520 | tf_op jit(solution)/shard_map/ppermute | solution.py:28
  196.5 19.7 %collective-permute-start.22 = (bf16[2,128,1792]{2,1,0:T(8,128)(2,1)}, bf16[2,128,1792]{2,1,0:T(8,128)(2,1)}, u32[]{:S(2)}, u32[]{:S(2)}) collective-permute-start(bf16[2,128,1792]{2,1,0:T(8,128)(2,1)} %get-tuple-element.101.refs_3_), channel_id=1, source_target_pairs={{8,16},{16,8},{9,17},{17,9},{10,18},{18,10},{11,19},{19,11},{12,20... | collective-permute-start | bytes 2752520 | tf_op jit(solution)/shard_map/ppermute | solution.py:28
  198.1 18.1 %collective-permute-start.23 = (bf16[128,3584]{1,0:T(8,128)(2,1)}, bf16[128,3584]{1,0:T(8,128)(2,1)}, u32[]{:S(2)}, u32[]{:S(2)}) collective-permute-start(bf16[128,3584]{1,0:T(8,128)(2,1)} %get-tuple-element.102.refs_3_), channel_id=1, source_target_pairs={{8,16},{16,8},{9,17},{17,9},{10,18},{18,10},{11,19},{19,11},{12,20... | collective-permute-start | bytes 2752520 | tf_op jit(solution)/shard_map/ppermute | solution.py:28
  199.7 38.9 %collective-permute-start.25 = (bf16[2,128,1792]{2,1,0:T(8,128)(2,1)}, bf16[2,128,1792]{2,1,0:T(8,128)(2,1)}, u32[]{:S(2)}, u32[]{:S(2)}) collective-permute-start(bf16[2,128,1792]{2,1,0:T(8,128)(2,1)} %get-tuple-element.110.refs_4_), channel_id=1, source_target_pairs={{8,0},{16,24},{9,1},{17,25},{10,2},{18,26},{11,3},{19,27},{12,4},{... | collective-permute-start | bytes 2752520 | tf_op jit(solution)/shard_map/ppermute | solution.py:28
  216.2 39.3 %collective-permute-start.26 = (bf16[2,128,1792]{2,1,0:T(8,128)(2,1)}, bf16[2,128,1792]{2,1,0:T(8,128)(2,1)}, u32[]{:S(2)}, u32[]{:S(2)}) collective-permute-start(bf16[2,128,1792]{2,1,0:T(8,128)(2,1)} %get-tuple-element.111.refs_6_), channel_id=1, source_target_pairs={{8,0},{16,24},{9,1},{17,25},{10,2},{18,26},{11,3},{19,27},{12,4},{... | collective-permute-start | bytes 2752520 | tf_op jit(solution)/shard_map/ppermute | solution.py:28
  217.5 69.7 %collective-permute-start.31 = (bf16[128,3584]{1,0:T(8,128)(2,1)}, bf16[128,3584]{1,0:T(8,128)(2,1)}, u32[]{:S(2)}, u32[]{:S(2)}) collective-permute-start(bf16[128,3584]{1,0:T(8,128)(2,1)} %get-tuple-element.130.refs_7_), channel_id=1, source_target_pairs={{8,0},{16,24},{9,1},{17,25},{10,2},{18,26},{11,3},{19,27},{12,4},{... | collective-permute-start | bytes 2752520 | tf_op jit(solution)/shard_map/ppermute | solution.py:28
  271.5 13.8 %collective-permute-start.28 = (bf16[64,1024]{1,0:T(8,128)(2,1)}, bf16[64,1024]{1,0:T(8,128)(2,1)}, u32[]{:S(2)}, u32[]{:S(2)}) collective-permute-start(bf16[64,1024]{1,0:T(8,128)(2,1)} %get-tuple-element.121), channel_id=1, source_target_pairs={{0,4},{4,0},{1,5},{5,1},{2,6},{6,2},{3,7},{7,3},{8,12},{12,8},{9,1... | collective-permute-start | bytes 393224 | tf_op jit(solution)/shard_map/ppermute | solution.py:406
  (11 other events, 58.3 us)

commit v2 on v1

--- a/solution.py
+++ b/solution.py
@@ -26,6 +26,10 @@
 
 def send(x, perm):
     return lax.ppermute(x, "inp", perm)
+
+
+def tile_of(size, most):
+    return max(t for t in range(128, most + 1, 128) if size % t == 0)
 
 
 def place(k, z):
@@ -75,7 +79,6 @@
         )
 
 
-TILE = 256
 CUTS = (7, 7)
 
 
@@ -163,8 +166,7 @@
 
 
 def down_grads(grads_ref, *refs):
-    own, pair, pair_end, *rest = [r[...] for r in refs[:7]]
-    refs[-1][...] = dot(joined(own, pair + pair_end, *rest), grads_ref[...], LEAD).astype(BF)
+    refs[-1][...] = dot(joined(*[r[...] for r in refs[:6]]), grads_ref[...], LEAD).astype(BF)
 
 
 def split_again(where_ref, mine_ref, got_ref, keep_ref, y_ref, x_ref, xy_ref):
@@ -207,24 +209,27 @@
     def whole(*dims):
         return pl.BlockSpec(dims, lambda *_: (0,) * len(dims))
 
-    def gathered(x):
-        other = lax.ppermute(x, "tok", X_SWAP)
-        return x, lax.ppermute(x, "tok", CORE_SWAP), other, lax.ppermute(other, "tok", CORE_SWAP)
-
-    def hidden_of():
-        tile = ff // 7
-        return chain.call(
+    def tok_swaps(x):
+        return x, lax.ppermute(x, "tok", CORE_SWAP), lax.ppermute(x, "tok", X_SWAP)
+
+    def tok_last(x, sibling, other):
+        (other,) = chain.relay(other)
+        return x, sibling, other, lax.ppermute(other, "tok", CORE_SWAP)
+
+    def hidden_args():
+        tile = tile_of(ff, 2048)
+        return (
             hidden_values,
-            (7,),
+            (ff // tile,),
             (saved_gate, saved_up),
             [cols(rows, tile, 0)] * 2,
             [shape((rows, ff), BF)],
             [cols(rows, tile, 0)],
-        )[0]
+        )
 
     def partial(c):
         start, w = cuts[c]
-        tile = TILE
+        tile = tile_of(w, 1024)
         w_spec = pl.BlockSpec((tile, depth), lambda j, *_: (start // tile + j, 0))
         outs = [shape((tokens, w), F32), shape((tokens // 2, w), BF)]
         specs = [cols(tokens, tile, 0), cols(tokens // 2, tile, 0)]
@@ -237,7 +242,7 @@
             part, rest, given = chain.call(
                 first_partial_sums,
                 (w // tile,),
-                (*gathered(out_grad), w_down),
+                (*out_grads, w_down),
                 [whole(rows, depth)] * 4 + [w_spec],
                 [*outs, shape((tokens, depth), BF)],
                 [*specs, whole(tokens, depth)],
@@ -247,7 +252,7 @@
 
     def pass_on(c):
         w = widths[c]
-        tile = TILE
+        tile = tile_of(w, 1024)
         second = chain.call(
             add_part,
             (w // tile,),
@@ -280,7 +285,7 @@
 
     def grads_of(c):
         start, w = cuts[c]
-        tile = TILE
+        tile = tile_of(w, 1024)
         own = chain.call(
             swiglu_grads,
             (w // tile,),
@@ -294,11 +299,13 @@
     def spread(own):
         return {"own": own, "pair": send(own, PAIRS), "near": send(own, MIDDLE)}
 
-    def spread_far(x, *others):
-        x["pair"], x["near"], *others = chain.relay(x["pair"], x["near"], *others)
+    def spread_near(x):
+        (x["near"],) = chain.relay(x["near"])
         x["near_end"] = send(x["near"], OUTWARD)
+
+    def spread_far(x):
+        (x["pair"],) = chain.relay(x["pair"])
         x["far"] = send(x["pair"], MIDDLE)
-        return others
 
     def spread_end(x, *others):
         x["far"], *others = chain.relay(x["far"], *others)
@@ -310,7 +317,7 @@
 
     def input_step(c, before):
         start, w = cuts[c]
-        tile = TILE
+        tile = tile_of(depth, 512)
         first, last = before is None, c + 1 == len(cuts)
         wide = pl.BlockSpec((pl.Element(tile), pl.Element(w)), lambda j, *_: (j * tile, start))
         across = cols(tokens, tile, 0)
@@ -334,7 +341,7 @@
 
     def weights_step(c, before):
         start, w = cuts[c]
-        tile = TILE
+        tile = tile_of(w, 1024)
         return chain.call(
             weight_grads,
             (w // tile,),
@@ -346,50 +353,55 @@
         )
 
     def down_step():
-        tile = TILE
+        tile = tile_of(ff, 1024)
         return chain.call(
             down_grads,
             (ff // tile,),
-            [grads, *[h[k] for k in ("own", "pair", "pair_end", "near", "near_end", "far", "far_end")]],
-            [whole(tokens, depth)] + [cols(rows, tile, 0)] * 7,
+            [grads, *pieces(h)],
+            [whole(tokens, depth)] + [cols(rows, tile, 0)] * 6,
             [shape((ff, depth), BF)],
             [pl.BlockSpec((tile, depth), lambda j, *_: (j, 0))],
         )[0]
 
     n = len(cuts)
     parts, firsts, seconds, thirds, groups = ([None] * n for _ in range(5))
-    h = {"own": hidden_of()}
-    h["pair_end"] = send(h["own"], OUTWARD)
-    h["near"] = send(h["own"], MIDDLE)
+    out_grads = tok_swaps(out_grad)
+    h = spread(Chain(jnp.zeros((8, 128), F32)).call(*hidden_args())[0])
+    out_grads = tok_last(*out_grads)
     grads, parts[0], firsts[0] = partial(0)
     _, parts[1], firsts[1] = partial(1)
-    h["near"], h["pair_end"], h_again = chain.relay(h["near"], h["pair_end"], h["own"])
-    h["near_end"] = send(h["near"], OUTWARD)
+    spread_near(h)
+    spread_far(h)
     pass_on(0)
+    (h["near_end"],) = spread_end(h, h["near_end"])
     hand_out(0)
-    (h["near_end"],) = chain.relay(h["near_end"])
+    (h["far_end"],) = chain.relay(h["far_end"])
     groups[0] = grads_of(0)
     hand_out(1)
-    h_again, = spread_far(groups[0], h_again)
-    h["pair"] = send(h_again, ENDS_IN)
+    spread_far(groups[0])
+    (thirds[1],) = chain.relay(thirds[1])
+    spread_near(groups[0])
     groups[1] = grads_of(1)
-    (inputs_b,) = spread_end(groups[0], saved_input.astype(BF))
+    spread_end(groups[0])
+    (groups[0]["near_end"],) = chain.relay(groups[0]["near_end"])
+    (inputs_b,) = chain.relay(saved_input.astype(BF))
+    in_raw = tok_last(*tok_swaps(inputs_b))
     inputs = chain.call(
         functools.partial(arrange, True),
         (1,),
-        gathered(inputs_b),
+        in_raw,
         [whole(rows, depth)] * 4,
         [shape((depth, tokens), BF)],
         [whole(depth, tokens)],
         scalars=where,
     )[0]
-    (h["pair"],) = chain.relay(h["pair"])
-    h["far"] = send(h["pair"], MIDDLE)
-    (groups[0]["near_end"],) = spread_far(groups[1], groups[0]["near_end"])
-    h["far"], groups[0]["far_end"] = spread_end(groups[1], h["far"], groups[0]["far_end"])
-    h["far_end"] = send(h["far"], OUTWARD)
+    down = down_step()
+    spread_near(groups[1])
+    spread_far(groups[1])
+    (groups[0]["far_end"],) = chain.relay(groups[0]["far_end"])
     total = input_step(0, None)
     weights = weights_step(0, ())
+    spread_end(groups[1])
     mine, other = input_step(1, total)
     got = lax.ppermute(other, "tok", CORE_SWAP)
     keep, *others = chain.call(
@@ -415,7 +427,6 @@
         [shape((rows // 2, depth), BF)],
         [whole(rows // 2, depth)],
     )[0]
-    down = down_step()
     return result, weights[0], weights[1], down
 
 

time: 303 us -> 253 us (0.83)
  waiting for transfers between devices: 119 us -> 90.8 us
  Pallas kernels: 106 us -> 82.9 us
  starting transfers between devices: 68.4 us -> 74 us
    pallas_call x23 -> x32, Pallas kernels: 106 us -> 82.9 us  [call(): pl.pallas_call(kernel, grid_spec=pltpu.PrefetchScalarGridSpec(num_scalar_...]
    ppermute x22 -> x21, waiting for transfers between devices: 102 us -> 81 us  [send(): return lax.ppermute(x, 'inp', perm)]
    ppermute x6, waiting for transfers between devices: 15 us -> 7.57 us  [the longest x2 6.15 us: tok_swaps(): lax.ppermute(x, 'tok', X_SWAP)]
    ppermute x22 -> x21, starting transfers between devices: 60.4 us -> 66.4 us  [send(): return lax.ppermute(x, 'inp', perm)]
  transfers between devices with their start and end apart: 32 -> 31, of which waited for: 14 -> 15; matrix products, arithmetic and copies ran while one was open for 2% -> 1% of each run, Pallas kernels for 31% -> 27%
where the time goes in v2:
time: 253 us; the launch traced here: 252 us
  waiting for transfers between devices  90.8 us (36%)
  Pallas kernels  82.9 us (33%)
  starting transfers between devices  74 us (29%)
    pallas_call x32, Pallas kernels, call(): pl.pallas_call(kernel, grid_spec=pltpu.PrefetchScalarGridSpec(num_scalar_...  82.9 us
    ppermute x21, waiting for transfers between devices, send(): return lax.ppermute(x, 'inp', perm)  81 us
    ppermute x21, starting transfers between devices, send(): return lax.ppermute(x, 'inp', perm)  66.4 us
    ppermute x2, waiting for transfers between devices, tok_swaps(): lax.ppermute(x, 'tok', X_SWAP)  6.15 us
  transfers between devices with their start and end apart: 31, of which 15 were waited for; matrix products, arithmetic and copies ran while one was open for 1% of the time, Pallas kernels for 27%

profile of v2, /device:TPU:0, one launch (start us, length us, event | category | flops | bytes accessed | tf_op | source)
XLA Modules:
  0.0 252.1 jit_solution(5815409493155079148)
XLA Ops:
  8.8 3.5 %collective-permute-start.4 = (bf16[128,3584]{1,0:T(8,128)(2,1)}, bf16[128,3584]{1,0:T(8,128)(2,1)}, u32[]{:S(2)}, u32[]{:S(2)}) collective-permute-start(bf16[128,3584]{1,0:T(8,128)(2,1)} %get-tuple-element.82.refs_2_), channel_id=1, source_target_pairs={{0,8},{8,0},{16,24},{24,16},{1,9},{9,1},{17,25},{25,17},{2,10},{10... | collective-permute-start | bytes 2752520 | tf_op jit(solution)/shard_map/ppermute | solution.py:28
  14.9 6.5 %shard_map.103 = (f32[8,128]{1,0:T(8,128)}, f32[512,1792]{1,0:T(8,128)}, bf16[256,1792]{1,0:T(8,128)(2,1)}, bf16[512,1024]{1,0:T(8,128)(2,1)}) custom-call(s32[3]{0:T(128)} %pad_add_fusion.refs_0_, f32[8,128]{1,0:T(8,128)} %get-tuple-element.77.refs_1_, bf16[128,1024]{1,0:T(8,128)(2,1)} %refs_2_.3, ...), custom_call_target="tpu_custom_call", output_to_operand_aliasing={{0}: (1, {})} | custom-call | tf_op jit(solution)/shard_map/pallas_call | solution.py:54
  24.4 5.8 %shard_map.104 = (f32[8,128]{1,0:T(8,128)}, f32[512,1792]{1,0:T(8,128)}, bf16[256,1792]{1,0:T(8,128)(2,1)}) custom-call(f32[8,128]{1,0:T(8,128)} %get-tuple-element.79.refs_0_, bf16[512,1024]{1,0:T(8,128)(2,1)} %get-tuple-element.80.refs_1_, bf16[3584,1024]{1,0:T(8,128)(2,1)} %refs_2_.4), custom_call_target="tpu_custom_call", output_to_operand_aliasing={{0}: (0, {})} | custom-call | tf_op jit(solution)/shard_map/pallas_call | solution.py:54
  30.2 3.3 %collective-permute-done.4.refs_1_ = bf16[128,3584]{1,0:T(8,128)(2,1)} collective-permute-done((bf16[128,3584]{1,0:T(8,128)(2,1)}, bf16[128,3584]{1,0:T(8,128)(2,1)}, u32[]{:S(2)}, u32[]{:S(2)}) %collective-permute-start.4) | collective-permute-done | bytes 917536 | tf_op jit(solution)/shard_map/ppermute | solution.py:28
  36.3 7.1 %collective-permute-start.9 = (bf16[256,1792]{1,0:T(8,128)(2,1)}, bf16[256,1792]{1,0:T(8,128)(2,1)}, u32[]{:S(2)}, u32[]{:S(2)}) collective-permute-start(bf16[256,1792]{1,0:T(8,128)(2,1)} %get-tuple-element.92), channel_id=1, source_target_pairs={{0,8},{24,16},{1,9},{25,17},{2,10},{26,18},{3,11},{27,19},{4,12},{... | collective-permute-start | bytes 2752520 | tf_op jit(solution)/shard_map/ppermute | solution.py:28
  43.4 9.7 %collective-permute-done.5.refs_1_ = bf16[256,1792]{1,0:T(8,128)(2,1)} collective-permute-done((bf16[256,1792]{1,0:T(8,128)(2,1)}, bf16[256,1792]{1,0:T(8,128)(2,1)}, u32[]{:S(2)}, u32[]{:S(2)}) %collective-permute-start.5) | collective-permute-done | bytes 917536 | tf_op jit(solution)/shard_map/ppermute | solution.py:28
  58.6 12.4 %collective-permute-done.9.refs_3_ = bf16[256,1792]{1,0:T(8,128)(2,1)} collective-permute-done((bf16[256,1792]{1,0:T(8,128)(2,1)}, bf16[256,1792]{1,0:T(8,128)(2,1)}, u32[]{:S(2)}, u32[]{:S(2)}) %collective-permute-start.9) | collective-permute-done | bytes 917536 | tf_op jit(solution)/shard_map/ppermute | solution.py:28
  71.0 3.4 %shard_map.110 = (f32[8,128]{1,0:T(8,128)}, bf16[128,1792]{1,0:T(8,128)(2,1)}, bf16[256,1792]{1,0:T(8,128)(2,1)}) custom-call(f32[8,128]{1,0:T(8,128)} %get-tuple-element.90.refs_0_, bf16[256,1792]{1,0:T(8,128)(2,1)} %collective-permute-done.8.refs_1_.refs_2_, f32[512,1792]{1,0:T(8,128)} %get-tuple-element.86.refs_2_.refs_1_, ...), custom_call_target="tpu_custom_call", output_to_operand_aliasing={{0}: (0, {})} | custom-call | tf_op jit(solution)/shard_map/pallas_call | solution.py:54
  74.4 8.2 %collective-permute-start.11 = (bf16[128,1792]{1,0:T(8,128)(2,1)}, bf16[128,1792]{1,0:T(8,128)(2,1)}, u32[]{:S(2)}, u32[]{:S(2)}) collective-permute-start(bf16[128,1792]{1,0:T(8,128)(2,1)} %get-tuple-element.97), channel_id=1, source_target_pairs={{0,8},{8,0},{16,24},{24,16},{1,9},{9,1},{17,25},{25,17},{2,10},{10... | collective-permute-start | bytes 1376264 | tf_op jit(solution)/shard_map/ppermute | solution.py:28
  84.1 5.2 %collective-permute-done.11.refs_3_ = bf16[128,1792]{1,0:T(8,128)(2,1)} collective-permute-done((bf16[128,1792]{1,0:T(8,128)(2,1)}, bf16[128,1792]{1,0:T(8,128)(2,1)}, u32[]{:S(2)}, u32[]{:S(2)}) %collective-permute-start.11) | collective-permute-done | bytes 458784 | tf_op jit(solution)/shard_map/ppermute | solution.py:28
  98.2 12.0 %collective-permute-start.14 = (bf16[128,1792]{1,0:T(8,128)(2,1)}, bf16[128,1792]{1,0:T(8,128)(2,1)}, u32[]{:S(2)}, u32[]{:S(2)}) collective-permute-start(bf16[128,1792]{1,0:T(8,128)(2,1)} %get-tuple-element.103), channel_id=1, source_target_pairs={{0,8},{8,0},{16,24},{24,16},{1,9},{9,1},{17,25},{25,17},{2,10},{10... | collective-permute-start | bytes 1376264 | tf_op jit(solution)/shard_map/ppermute | solution.py:28
  110.2 4.5 %collective-permute-done.13.refs_1_ = bf16[2,128,1792]{2,1,0:T(8,128)(2,1)} collective-permute-done((bf16[2,128,1792]{2,1,0:T(8,128)(2,1)}, bf16[2,128,1792]{2,1,0:T(8,128)(2,1)}, u32[]{:S(2)}, u32[]{:S(2)}) %collective-permute-start.13) | collective-permute-done | bytes 917536 | tf_op jit(solution)/shard_map/ppermute | solution.py:28
  116.3 3.3 %collective-permute-done.14.refs_1_ = bf16[128,1792]{1,0:T(8,128)(2,1)} collective-permute-done((bf16[128,1792]{1,0:T(8,128)(2,1)}, bf16[128,1792]{1,0:T(8,128)(2,1)}, u32[]{:S(2)}, u32[]{:S(2)}) %collective-permute-start.14) | collective-permute-done | bytes 458784 | tf_op jit(solution)/shard_map/ppermute | solution.py:28
  125.7 9.8 %collective-permute-start.22 = (bf16[2,128,1792]{2,1,0:T(8,128)(2,1)}, bf16[2,128,1792]{2,1,0:T(8,128)(2,1)}, u32[]{:S(2)}, u32[]{:S(2)}) collective-permute-start(bf16[2,128,1792]{2,1,0:T(8,128)(2,1)} %get-tuple-element.120.refs_2_), channel_id=1, source_target_pairs={{0,8},{8,0},{16,24},{24,16},{1,9},{9,1},{17,25},{25,17},{2,10},{10... | collective-permute-start | bytes 2752520 | tf_op jit(solution)/shard_map/ppermute | solution.py:28
  137.2 11.9 %collective-permute-done.17.refs_1_ = bf16[2,128,1792]{2,1,0:T(8,128)(2,1)} collective-permute-done((bf16[2,128,1792]{2,1,0:T(8,128)(2,1)}, bf16[2,128,1792]{2,1,0:T(8,128)(2,1)}, u32[]{:S(2)}, u32[]{:S(2)}) %collective-permute-start.17) | collective-permute-done | bytes 917536 | tf_op jit(solution)/shard_map/ppermute | solution.py:28
  149.6 6.1 %collective-permute-done.18.refs_1_ = bf16[128,1024]{1,0:T(8,128)(2,1)} collective-permute-done((bf16[128,1024]{1,0:T(8,128)(2,1)}, bf16[128,1024]{1,0:T(8,128)(2,1)}, u32[]{:S(2)}, u32[]{:S(2)}) %collective-permute-start.18) | collective-permute-done | bytes 262176 | tf_op jit(solution)/shard_map/ppermute | solution.py:213
  157.7 3.2 %shard_map.122 = (f32[8,128]{1,0:T(8,128)}, bf16[1024,512]{1,0:T(8,128)(2,1)}) custom-call(s32[3]{0:T(128)} %pad_add_fusion.refs_0_, f32[8,128]{1,0:T(8,128)} %get-tuple-element.114.refs_1_, bf16[128,1024]{1,0:T(8,128)(2,1)} %get-tuple-element.113.refs_2_, bf16[128,1024]{1,0:T(8,128)(2,1)} %collective-permute-done.19.refs_3_, ...), custom_call_target="tpu_custom_call", output_to_operand_aliasing={{0}: (1, {})} | custom-call | tf_op jit(solution)/shard_map/pallas_call | solution.py:54
  160.8 8.8 %shard_map.123 = (f32[8,128]{1,0:T(8,128)}, bf16[3584,1024]{1,0:T(8,128)(2,1)}) custom-call(f32[8,128]{1,0:T(8,128)} %get-tuple-element.116.refs_0_, bf16[512,1024]{1,0:T(8,128)(2,1)} %get-tuple-element.80.refs_1_, bf16[128,3584]{1,0:T(8,128)(2,1)} %get-tuple-element.82.refs_2_, ...), custom_call_target="tpu_custom_call", output_to_operand_aliasing={{0}: (0, {})} | custom-call | tf_op jit(solution)/shard_map/pallas_call | solution.py:54
  172.6 8.5 %collective-permute-done.23.refs_1_ = bf16[2,128,1792]{2,1,0:T(8,128)(2,1)} collective-permute-done((bf16[2,128,1792]{2,1,0:T(8,128)(2,1)}, bf16[2,128,1792]{2,1,0:T(8,128)(2,1)}, u32[]{:S(2)}, u32[]{:S(2)}) %collective-permute-start.23) | collective-permute-done | bytes 917536 | tf_op jit(solution)/shard_map/ppermute | solution.py:28
  181.1 9.2 %shard_map.127 = (f32[8,128]{1,0:T(8,128)}, f32[512,1024]{1,0:T(8,128)}) custom-call(f32[8,128]{1,0:T(8,128)} %get-tuple-element.124.refs_0_, bf16[2,128,1792]{2,1,0:T(8,128)(2,1)} %get-tuple-element.101.refs_1_.refs_2_, bf16[2,128,1792]{2,1,0:T(8,128)(2,1)} %get-tuple-element.108.refs_2_.refs_3_, ...), custom_call_target="tpu_custom_call", output_to_operand_aliasing={{0}: (0, {})} | custom-call | tf_op jit(solution)/shard_map/pallas_call | solution.py:54
  190.3 8.3 %shard_map.128 = (f32[8,128]{1,0:T(8,128)}, bf16[1024,3584]{1,0:T(8,128)(2,1)}, bf16[1024,3584]{1,0:T(8,128)(2,1)}) custom-call(f32[8,128]{1,0:T(8,128)} %get-tuple-element.127.refs_0_, bf16[1024,512]{1,0:T(8,128)(2,1)} %get-tuple-element.128.refs_1_, bf16[2,128,1792]{2,1,0:T(8,128)(2,1)} %get-tuple-element.101.refs_1_.refs_2_, ...), custom_call_target="tpu_custom_call", output_to_operand_aliasing={{0}: (0, {})} | custom-call | tf_op jit(solution)/shard_map/pallas_call | solution.py:54
  200.4 22.0 %collective-permute-done.26.refs_7_ = bf16[2,128,1792]{2,1,0:T(8,128)(2,1)} collective-permute-done((bf16[2,128,1792]{2,1,0:T(8,128)(2,1)}, bf16[2,128,1792]{2,1,0:T(8,128)(2,1)}, u32[]{:S(2)}, u32[]{:S(2)}) %collective-permute-start.26) | collective-permute-done | bytes 917536 | tf_op jit(solution)/shard_map/ppermute | solution.py:28
  222.4 10.8 %shard_map.130 = (f32[8,128]{1,0:T(8,128)}, f32[256,1024]{1,0:T(8,128)}, bf16[256,1024]{1,0:T(8,128)(2,1)}) custom-call(s32[3]{0:T(128)} %pad_add_fusion.refs_0_, f32[8,128]{1,0:T(8,128)} %get-tuple-element.131.refs_1_, bf16[2,128,1792]{2,1,0:T(8,128)(2,1)} %get-tuple-element.120.refs_2_, ...), custom_call_target="tpu_custom_call", output_to_operand_aliasing={{0}: (1, {})} | custom-call | tf_op jit(solution)/shard_map/pallas_call | solution.py:54
  241.9 8.3 %shard_map.132 = (f32[8,128]{1,0:T(8,128)}, bf16[1024,3584]{1,0:T(8,128)(2,1)}, bf16[1024,3584]{1,0:T(8,128)(2,1)}) custom-call(f32[8,128]{1,0:T(8,128)} %get-tuple-element.138.refs_0_, bf16[1024,512]{1,0:T(8,128)(2,1)} %get-tuple-element.128.refs_1_, ...), custom_call_target="tpu_custom_call", output_to_operand_aliasing={{0}: (0, {}), {1}: (8, {}), {2}: (9, {})} | custom-call | tf_op jit(solution)/shard_map/pallas_call | solution.py:54
  (74 shorter events, 59.6 us)
Async XLA Ops:
  0.6 11.7 %collective-permute-start = (bf16[128,1024]{1,0:T(8,128)(2,1)}, bf16[128,1024]{1,0:T(8,128)(2,1)}, u32[]{:S(2)}, u32[]{:S(2)}) collective-permute-start(bf16[128,1024]{1,0:T(8,128)(2,1)} %refs_2_.3), channel_id=1, source_target_pairs={{0,2},{2,0},{1,3},{3,1},{4,6},{6,4},{5,7},{7,5},{8,10},{10,8},{9,1... | collective-permute-start | bytes 786440 | tf_op jit(solution)/shard_map/ppermute | solution.py:213
  7.2 23.0 %collective-permute-start.3 = (bf16[128,3584]{1,0:T(8,128)(2,1)}, bf16[128,3584]{1,0:T(8,128)(2,1)}, u32[]{:S(2)}, u32[]{:S(2)}) collective-permute-start(bf16[128,3584]{1,0:T(8,128)(2,1)} %get-tuple-element.82.refs_2_), channel_id=1, source_target_pairs={{8,16},{16,8},{9,17},{17,9},{10,18},{18,10},{11,19},{19,11},{12,20... | collective-permute-start | bytes 2752520 | tf_op jit(solution)/shard_map/ppermute | solution.py:28
  8.8 24.6 %collective-permute-start.4 = (bf16[128,3584]{1,0:T(8,128)(2,1)}, bf16[128,3584]{1,0:T(8,128)(2,1)}, u32[]{:S(2)}, u32[]{:S(2)}) collective-permute-start(bf16[128,3584]{1,0:T(8,128)(2,1)} %get-tuple-element.82.refs_2_), channel_id=1, source_target_pairs={{0,8},{8,0},{16,24},{24,16},{1,9},{9,1},{17,25},{25,17},{2,10},{10... | collective-permute-start | bytes 2752520 | tf_op jit(solution)/shard_map/ppermute | solution.py:28
  21.4 31.7 %collective-permute-start.5 = (bf16[256,1792]{1,0:T(8,128)(2,1)}, bf16[256,1792]{1,0:T(8,128)(2,1)}, u32[]{:S(2)}, u32[]{:S(2)}) collective-permute-start(bf16[256,1792]{1,0:T(8,128)(2,1)} %get-tuple-element.85), channel_id=1, source_target_pairs={{0,8},{24,16},{1,9},{25,17},{2,10},{26,18},{3,11},{27,19},{4,12},{... | collective-permute-start | bytes 2752520 | tf_op jit(solution)/shard_map/ppermute | solution.py:28
  33.4 23.9 %collective-permute-start.6 = (bf16[128,3584]{1,0:T(8,128)(2,1)}, bf16[128,3584]{1,0:T(8,128)(2,1)}, u32[]{:S(2)}, u32[]{:S(2)}) collective-permute-start(bf16[128,3584]{1,0:T(8,128)(2,1)} %get-tuple-element.88.refs_3_), channel_id=1, source_target_pairs={{8,16},{16,8},{9,17},{17,9},{10,18},{18,10},{11,19},{19,11},{12,20... | collective-permute-start | bytes 2752520 | tf_op jit(solution)/shard_map/ppermute | solution.py:28
  35.0 22.3 %collective-permute-start.7 = (bf16[128,3584]{1,0:T(8,128)(2,1)}, bf16[128,3584]{1,0:T(8,128)(2,1)}, u32[]{:S(2)}, u32[]{:S(2)}) collective-permute-start(bf16[128,3584]{1,0:T(8,128)(2,1)} %get-tuple-element.89.refs_4_), channel_id=1, source_target_pairs={{8,0},{16,24},{9,1},{17,25},{10,2},{18,26},{11,3},{19,27},{12,4},{... | collective-permute-start | bytes 2752520 | tf_op jit(solution)/shard_map/ppermute | solution.py:28
  36.3 34.7 %collective-permute-start.9 = (bf16[256,1792]{1,0:T(8,128)(2,1)}, bf16[256,1792]{1,0:T(8,128)(2,1)}, u32[]{:S(2)}, u32[]{:S(2)}) collective-permute-start(bf16[256,1792]{1,0:T(8,128)(2,1)} %get-tuple-element.92), channel_id=1, source_target_pairs={{0,8},{24,16},{1,9},{25,17},{2,10},{26,18},{3,11},{27,19},{4,12},{... | collective-permute-start | bytes 2752520 | tf_op jit(solution)/shard_map/ppermute | solution.py:28
  55.7 15.3 %collective-permute-start.8 = (bf16[256,1792]{1,0:T(8,128)(2,1)}, bf16[256,1792]{1,0:T(8,128)(2,1)}, u32[]{:S(2)}, u32[]{:S(2)}) collective-permute-start(bf16[256,1792]{1,0:T(8,128)(2,1)} %get-tuple-element.91), channel_id=1, source_target_pairs={{8,16},{16,8},{9,17},{17,9},{10,18},{18,10},{11,19},{19,11},{12,20... | collective-permute-start | bytes 2752520 | tf_op jit(solution)/shard_map/ppermute | solution.py:28
  57.3 26.8 %collective-permute-start.10 = (bf16[128,3584]{1,0:T(8,128)(2,1)}, bf16[128,3584]{1,0:T(8,128)(2,1)}, u32[]{:S(2)}, u32[]{:S(2)}) collective-permute-start(bf16[128,3584]{1,0:T(8,128)(2,1)} %get-tuple-element.95.refs_6_), channel_id=1, source_target_pairs={{8,0},{16,24},{9,1},{17,25},{10,2},{18,26},{11,3},{19,27},{12,4},{... | collective-permute-start | bytes 2752520 | tf_op jit(solution)/shard_map/ppermute | solution.py:28
  74.4 15.0 %collective-permute-start.11 = (bf16[128,1792]{1,0:T(8,128)(2,1)}, bf16[128,1792]{1,0:T(8,128)(2,1)}, u32[]{:S(2)}, u32[]{:S(2)}) collective-permute-start(bf16[128,1792]{1,0:T(8,128)(2,1)} %get-tuple-element.97), channel_id=1, source_target_pairs={{0,8},{8,0},{16,24},{24,16},{1,9},{9,1},{17,25},{25,17},{2,10},{10... | collective-permute-start | bytes 1376264 | tf_op jit(solution)/shard_map/ppermute | solution.py:28
  82.6 13.4 %collective-permute-start.12 = (bf16[256,1792]{1,0:T(8,128)(2,1)}, bf16[256,1792]{1,0:T(8,128)(2,1)}, u32[]{:S(2)}, u32[]{:S(2)}) collective-permute-start(bf16[256,1792]{1,0:T(8,128)(2,1)} %get-tuple-element.99), channel_id=1, source_target_pairs={{8,16},{16,8},{9,17},{17,9},{10,18},{18,10},{11,19},{19,11},{12,20... | collective-permute-start | bytes 2752520 | tf_op jit(solution)/shard_map/ppermute | solution.py:28
  92.4 22.3 %collective-permute-start.13 = (bf16[2,128,1792]{2,1,0:T(8,128)(2,1)}, bf16[2,128,1792]{2,1,0:T(8,128)(2,1)}, u32[]{:S(2)}, u32[]{:S(2)}) collective-permute-start(bf16[2,128,1792]{2,1,0:T(8,128)(2,1)} %get-tuple-element.101.refs_1_.refs_2_), channel_id=1, source_target_pairs={{0,8},{8,0},{16,24},{24,16},{1,9},{9,1},{17,25},{25,17},{2,10},{10... | collective-permute-start | bytes 2752520 | tf_op jit(solution)/shard_map/ppermute | solution.py:28
  94.4 25.2 %collective-permute-start.15 = (bf16[2,128,1792]{2,1,0:T(8,128)(2,1)}, bf16[2,128,1792]{2,1,0:T(8,128)(2,1)}, u32[]{:S(2)}, u32[]{:S(2)}) collective-permute-start(bf16[2,128,1792]{2,1,0:T(8,128)(2,1)} %get-tuple-element.101.refs_1_.refs_2_), channel_id=1, source_target_pairs={{8,16},{16,8},{9,17},{17,9},{10,18},{18,10},{11,19},{19,11},{12,20... | collective-permute-start | bytes 2752520 | tf_op jit(solution)/shard_map/ppermute | solution.py:28
  98.2 21.4 %collective-permute-start.14 = (bf16[128,1792]{1,0:T(8,128)(2,1)}, bf16[128,1792]{1,0:T(8,128)(2,1)}, u32[]{:S(2)}, u32[]{:S(2)}) collective-permute-start(bf16[128,1792]{1,0:T(8,128)(2,1)} %get-tuple-element.103), channel_id=1, source_target_pairs={{0,8},{8,0},{16,24},{24,16},{1,9},{9,1},{17,25},{25,17},{2,10},{10... | collective-permute-start | bytes 1376264 | tf_op jit(solution)/shard_map/ppermute | solution.py:28
  114.7 22.5 %collective-permute-start.16 = (bf16[2,128,1792]{2,1,0:T(8,128)(2,1)}, bf16[2,128,1792]{2,1,0:T(8,128)(2,1)}, u32[]{:S(2)}, u32[]{:S(2)}) collective-permute-start(bf16[2,128,1792]{2,1,0:T(8,128)(2,1)} %get-tuple-element.108.refs_2_.refs_3_), channel_id=1, source_target_pairs={{8,16},{16,8},{9,17},{17,9},{10,18},{18,10},{11,19},{19,11},{12,20... | collective-permute-start | bytes 2752520 | tf_op jit(solution)/shard_map/ppermute | solution.py:28
  119.6 29.5 %collective-permute-start.17 = (bf16[2,128,1792]{2,1,0:T(8,128)(2,1)}, bf16[2,128,1792]{2,1,0:T(8,128)(2,1)}, u32[]{:S(2)}, u32[]{:S(2)}) collective-permute-start(bf16[2,128,1792]{2,1,0:T(8,128)(2,1)} %get-tuple-element.110.refs_3_.refs_4_), channel_id=1, source_target_pairs={{8,0},{16,24},{9,1},{17,25},{10,2},{18,26},{11,3},{19,27},{12,4},{... | collective-permute-start | bytes 2752520 | tf_op jit(solution)/shard_map/ppermute | solution.py:28
  124.0 45.6 %collective-permute-start.21 = (bf16[2,128,1792]{2,1,0:T(8,128)(2,1)}, bf16[2,128,1792]{2,1,0:T(8,128)(2,1)}, u32[]{:S(2)}, u32[]{:S(2)}) collective-permute-start(bf16[2,128,1792]{2,1,0:T(8,128)(2,1)} %get-tuple-element.120.refs_2_), channel_id=1, source_target_pairs={{8,16},{16,8},{9,17},{17,9},{10,18},{18,10},{11,19},{19,11},{12,20... | collective-permute-start | bytes 2752520 | tf_op jit(solution)/shard_map/ppermute | solution.py:28
  125.7 44.0 %collective-permute-start.22 = (bf16[2,128,1792]{2,1,0:T(8,128)(2,1)}, bf16[2,128,1792]{2,1,0:T(8,128)(2,1)}, u32[]{:S(2)}, u32[]{:S(2)}) collective-permute-start(bf16[2,128,1792]{2,1,0:T(8,128)(2,1)} %get-tuple-element.120.refs_2_), channel_id=1, source_target_pairs={{0,8},{8,0},{16,24},{24,16},{1,9},{9,1},{17,25},{25,17},{2,10},{10... | collective-permute-start | bytes 2752520 | tf_op jit(solution)/shard_map/ppermute | solution.py:28
  155.8 25.3 %collective-permute-start.23 = (bf16[2,128,1792]{2,1,0:T(8,128)(2,1)}, bf16[2,128,1792]{2,1,0:T(8,128)(2,1)}, u32[]{:S(2)}, u32[]{:S(2)}) collective-permute-start(bf16[2,128,1792]{2,1,0:T(8,128)(2,1)} %get-tuple-element.123.refs_5_.refs_6_), channel_id=1, source_target_pairs={{8,0},{16,24},{9,1},{17,25},{10,2},{18,26},{11,3},{19,27},{12,4},{... | collective-permute-start | bytes 2752520 | tf_op jit(solution)/shard_map/ppermute | solution.py:28
  169.7 28.9 %collective-permute-start.24 = (bf16[2,128,1792]{2,1,0:T(8,128)(2,1)}, bf16[2,128,1792]{2,1,0:T(8,128)(2,1)}, u32[]{:S(2)}, u32[]{:S(2)}) collective-permute-start(bf16[2,128,1792]{2,1,0:T(8,128)(2,1)} %get-tuple-element.130.refs_3_), channel_id=1, source_target_pairs={{8,16},{16,8},{9,17},{17,9},{10,18},{18,10},{11,19},{19,11},{12,20... | collective-permute-start | bytes 2752520 | tf_op jit(solution)/shard_map/ppermute | solution.py:28
  171.3 29.1 %collective-permute-start.25 = (bf16[2,128,1792]{2,1,0:T(8,128)(2,1)}, bf16[2,128,1792]{2,1,0:T(8,128)(2,1)}, u32[]{:S(2)}, u32[]{:S(2)}) collective-permute-start(bf16[2,128,1792]{2,1,0:T(8,128)(2,1)} %get-tuple-element.132.refs_4_), channel_id=1, source_target_pairs={{8,0},{16,24},{9,1},{17,25},{10,2},{18,26},{11,3},{19,27},{12,4},{... | collective-permute-start | bytes 2752520 | tf_op jit(solution)/shard_map/ppermute | solution.py:28
  198.6 23.8 %collective-permute-start.26 = (bf16[2,128,1792]{2,1,0:T(8,128)(2,1)}, bf16[2,128,1792]{2,1,0:T(8,128)(2,1)}, u32[]{:S(2)}, u32[]{:S(2)}) collective-permute-start(bf16[2,128,1792]{2,1,0:T(8,128)(2,1)} %get-tuple-element.133.refs_6_), channel_id=1, source_target_pairs={{8,0},{16,24},{9,1},{17,25},{10,2},{18,26},{11,3},{19,27},{12,4},{... | collective-permute-start | bytes 2752520 | tf_op jit(solution)/shard_map/ppermute | solution.py:28
  238.4 11.8 %collective-permute-start.28 = (bf16[64,1024]{1,0:T(8,128)(2,1)}, bf16[64,1024]{1,0:T(8,128)(2,1)}, u32[]{:S(2)}, u32[]{:S(2)}) collective-permute-start(bf16[64,1024]{1,0:T(8,128)(2,1)} %get-tuple-element.143), channel_id=1, source_target_pairs={{0,4},{4,0},{1,5},{5,1},{2,6},{6,2},{3,7},{7,3},{8,12},{12,8},{9,1... | collective-permute-start | bytes 393224 | tf_op jit(solution)/shard_map/ppermute | solution.py:418
  240.0 10.3 %collective-permute-start.29 = (bf16[64,1024]{1,0:T(8,128)(2,1)}, bf16[64,1024]{1,0:T(8,128)(2,1)}, u32[]{:S(2)}, u32[]{:S(2)}) collective-permute-start(bf16[64,1024]{1,0:T(8,128)(2,1)} %get-tuple-element.144), channel_id=1, source_target_pairs={{0,2},{2,0},{1,3},{3,1},{4,6},{6,4},{5,7},{7,5},{8,10},{10,8},{9,1... | collective-permute-start | bytes 393224 | tf_op jit(solution)/shard_map/ppermute | solution.py:419
  (7 other events, 31.9 us)

commit v3 on v2

--- a/solution.py
+++ b/solution.py
@@ -12,7 +12,8 @@
 LEAD = (((0,), (0,)), ((), ()))
 STRAIGHT = (((1,), (0,)), ((), ()))
 ANY = pl.BlockSpec(memory_space=pl.ANY)
-VMEM_LIMIT = 64 * 1024 * 1024
+MIB = 1024 * 1024
+SMALL, MEDIUM, LARGE = 8, 16, 28
 
 ENDS_IN = [(0, 1), (3, 2)]
 MIDDLE = [(1, 2), (2, 1)]
@@ -28,6 +29,10 @@
     return lax.ppermute(x, "inp", perm)
 
 
+LAST_TILE = 512
+ALL = ("own", "pair", "near", "near_end", "far", "far_end")
+
+
 def tile_of(size, most):
     return max(t for t in range(128, most + 1, 128) if size % t == 0)
 
@@ -44,7 +49,7 @@
     def __init__(self, token):
         self.token = token
 
-    def call(self, body, grid, ins, in_specs, outs, out_specs, aliases=(), scalars=None, scratch=()):
+    def call(self, body, grid, ins, in_specs, outs, out_specs, aliases=(), scalars=None, scratch=(), mib=SMALL):
         lead = 0 if scalars is None else 1
 
         def kernel(*refs):
@@ -62,7 +67,7 @@
             ),
             out_shape=[jax.ShapeDtypeStruct(self.token.shape, self.token.dtype), *outs],
             input_output_aliases=pairs,
-            compiler_params=pltpu.CompilerParams(vmem_limit_bytes=VMEM_LIMIT),
+            compiler_params=pltpu.CompilerParams(vmem_limit_bytes=mib * MIB),
         )(*(() if scalars is None else (scalars,)), self.token, *ins)
         self.token = given[0]
         return given[1:]
@@ -79,9 +84,6 @@
         )
 
 
-CUTS = (7, 7)
-
-
 def swiglu_grads(part_ref, second_ref, third_ref, g_ref, u_ref, out_ref):
     share = part_ref[...] + third_ref[...].astype(F32) + second_ref[...].astype(F32)
     g, u = g_ref[...], u_ref[...]
@@ -130,33 +132,43 @@
     out_ref[...] = (g * jax.nn.sigmoid(g) * u_ref[...]).astype(BF)
 
 
-def joined(own, pair, near, near_end, far, far_end):
-    return jnp.concatenate([own, pair, near + near_end, far + far_end], axis=0)
-
-
-def input_sums(piece_refs, held, wg_ref, wu_ref):
+def joined(*pieces):
+    alone = pieces[: len(pieces) % 4] if len(pieces) < 4 else pieces[:2]
+    if len(pieces) == 2:
+        alone = ()
+    pairs = pieces[len(alone) :]
+    return jnp.concatenate([*alone, *[a + b for a, b in zip(pairs[::2], pairs[1::2])]], axis=0)
+
+
+def input_sums(piece_refs, held, wg_ref, wu_ref, before_ref):
     @pl.when(pl.program_id(0) == 0)
     def _():
         for which in range(2):
             held[which] = joined(*[r[which] for r in piece_refs])
 
-    return dot(held[0], wg_ref[...], LAST) + dot(held[1], wu_ref[...], LAST)
-
-
-def input_sums_first(*refs):
-    refs[8][...] = input_sums(refs[:6], refs[9], *refs[6:8])
-
-
-def input_sums_last(where_ref, *refs):
-    mine_ref, other_ref, held, total = refs[9:]
-    total[...] = refs[8][...] + input_sums(refs[:6], held, *refs[6:8])
-    half = total.shape[0] // 8
+    total = dot(held[0], wg_ref[...], LAST) + dot(held[1], wu_ref[...], LAST)
+    return total if before_ref is None else total + before_ref[...]
+
+
+def input_sums_first(count, *refs):
+    refs[-2][...] = input_sums(refs[:count], refs[-1], *refs[count : count + 2], None)
+
+
+def input_sums_more(count, *refs):
+    refs[-2][...] = input_sums(refs[:count], refs[-1], *refs[count : count + 3])
+
+
+def input_sums_last(where_ref, far_ref, end_ref, wg_ref, wu_ref, before_ref, others_ref, mine_ref, other_ref, held, total):
+    rows = before_ref.shape[0]
+    total[: 3 * rows, :] = others_ref[...]
+    total[3 * rows :, :] = input_sums((far_ref, end_ref), held, wg_ref, wu_ref, before_ref)
+    half = rows // 2
     z, core = where_ref[0], where_ref[2] % 2
     for k in range(4):
         start = place(k, z) * 2
-        rows = slice(k * half, (k + 1) * half)
-        mine_ref[rows, :] = total[pl.ds(pl.multiple_of((start + core) * half, half), half), :]
-        other_ref[rows, :] = total[pl.ds(pl.multiple_of((start + 1 - core) * half, half), half), :].astype(BF)
+        at = slice(k * half, (k + 1) * half)
+        mine_ref[at, :] = total[pl.ds(pl.multiple_of((start + core) * half, half), half), :]
+        other_ref[at, :] = total[pl.ds(pl.multiple_of((start + 1 - core) * half, half), half), :].astype(BF)
 
 
 def weight_grads(inputs_ref, *refs):
@@ -199,9 +211,10 @@
     z, o, t = lax.axis_index("inp"), lax.axis_index("out"), lax.axis_index("tok")
     where = jnp.stack([z, o, t]).astype(jnp.int32)
     chain = Chain(jnp.zeros((8, 128), F32))
-    step = ff // 14
-    widths = [c * step for c in CUTS]
-    cuts = [(sum(widths[:c]), w) for c, w in enumerate(widths)]
+    half = ff // 2
+    cuts = [(0, half), (half, half)]
+    widths = [half, half]
+    group_cuts = cuts
 
     def cols(height, tile, start, row=0):
         return pl.BlockSpec((height, tile), lambda j, *_: (row, start // tile + j))
@@ -235,8 +248,7 @@
         specs = [cols(tokens, tile, 0), cols(tokens // 2, tile, 0)]
         if c:
             part, rest = chain.call(
-                partial_sums, (w // tile,), (grads, w_down), [whole(tokens, depth), w_spec], outs, specs
-            )
+                partial_sums, (w // tile,), (grads, w_down), [whole(tokens, depth), w_spec], outs, specs, mib=MEDIUM)
             given = grads
         else:
             part, rest, given = chain.call(
@@ -246,8 +258,7 @@
                 [whole(rows, depth)] * 4 + [w_spec],
                 [*outs, shape((tokens, depth), BF)],
                 [*specs, whole(tokens, depth)],
-                scalars=where,
-            )
+                scalars=where, mib=MEDIUM)
         return given, part, send(rest, ENDS_IN)
 
     def pass_on(c):
@@ -283,14 +294,15 @@
             seconds[c + 1] = send(second, MIDDLE)
         thirds[c] = send(third, PAIRS)
 
-    def grads_of(c):
-        start, w = cuts[c]
+    def grads_of(c, g):
+        start, w = group_cuts[g]
         tile = tile_of(w, 1024)
+        at = start - cuts[c][0]
         own = chain.call(
             swiglu_grads,
             (w // tile,),
             (parts[c], seconds[c], thirds[c], saved_gate, saved_up),
-            [cols(rows, tile, 0)] * 3 + [cols(rows, tile, start)] * 2,
+            [cols(rows, tile, at)] * 3 + [cols(rows, tile, start)] * 2,
             [shape((2, rows, w), BF)],
             [pl.BlockSpec((2, rows, tile), lambda j: (0, 0, j))],
         )[0]
@@ -313,44 +325,49 @@
         return others
 
     def pieces(x):
-        return [x[k] for k in ("own", "pair", "near", "near_end", "far", "far_end")]
-
-    def input_step(c, before):
-        start, w = cuts[c]
+        return [x[k] for k in ALL]
+
+    def input_step(g, before, names):
+        start, w = group_cuts[g]
         tile = tile_of(depth, 512)
-        first, last = before is None, c + 1 == len(cuts)
+        wide = pl.BlockSpec((pl.Element(tile), pl.Element(w)), lambda j: (j * tile, start))
+        count = len(names)
+        height = rows * len([k for k in names if not k.endswith("_end")])
+        across = cols(height, tile, 0)
+        return chain.call(
+            functools.partial(input_sums_first if before is None else input_sums_more, count),
+            (depth // tile,),
+            [*[groups[g][k] for k in names], w_gate, w_up] + ([] if before is None else [before]),
+            [whole(2, rows, w)] * count + [wide, wide] + ([] if before is None else [across]),
+            [shape((height, depth), F32)],
+            [across],
+            scratch=[pltpu.VMEM((2, height, w), BF)], mib=LARGE)[0]
+
+    def input_last(g, before, others):
+        start, w = group_cuts[g]
+        tile = tile_of(depth, LAST_TILE)
         wide = pl.BlockSpec((pl.Element(tile), pl.Element(w)), lambda j, *_: (j * tile, start))
-        across = cols(tokens, tile, 0)
-        held = [pltpu.VMEM((2, tokens, w), BF)]
-        ins = [*pieces(groups[c]), w_gate, w_up]
-        specs = [whole(2, rows, w)] * 6 + [wide, wide]
-        if first:
-            return chain.call(
-                input_sums_first, (depth // tile,), ins, specs, [shape((tokens, depth), F32)], [across], scratch=held
-            )[0]
         return chain.call(
             input_sums_last,
             (depth // tile,),
-            [*ins, before],
-            [*specs, across],
+            [groups[g]["far"], groups[g]["far_end"], w_gate, w_up, before, others],
+            [whole(2, rows, w)] * 2 + [wide, wide, cols(rows, tile, 0, 3), cols(3 * rows, tile, 0)],
             [shape((tokens // 2, depth), F32), shape((tokens // 2, depth), BF)],
             [cols(tokens // 2, tile, 0)] * 2,
             scalars=where,
-            scratch=[*held, pltpu.VMEM((tokens, tile), F32)],
-        )
-
-    def weights_step(c, before):
-        start, w = cuts[c]
+            scratch=[pltpu.VMEM((2, rows, w), BF), pltpu.VMEM((tokens, tile), F32)], mib=LARGE)
+
+    def weights_step(g, before):
+        start, w = group_cuts[g]
         tile = tile_of(w, 1024)
         return chain.call(
             weight_grads,
             (w // tile,),
-            (inputs, *pieces(groups[c]), *before),
+            (inputs, *pieces(groups[g]), *before),
             [whole(depth, tokens)] + [pl.BlockSpec((2, rows, tile), lambda j: (0, 0, j))] * 6 + [ANY] * len(before),
             [shape((depth, ff), BF)] * 2,
             [cols(depth, tile, start)] * 2,
-            aliases=[(7, 0), (8, 1)] if before else (),
-        )
+            aliases=[(7, 0), (8, 1)] if before else (), mib=LARGE)
 
     def down_step():
         tile = tile_of(ff, 1024)
@@ -360,13 +377,12 @@
             [grads, *pieces(h)],
             [whole(tokens, depth)] + [cols(rows, tile, 0)] * 6,
             [shape((ff, depth), BF)],
-            [pl.BlockSpec((tile, depth), lambda j, *_: (j, 0))],
-        )[0]
+            [pl.BlockSpec((tile, depth), lambda j, *_: (j, 0))], mib=MEDIUM)[0]
 
     n = len(cuts)
-    parts, firsts, seconds, thirds, groups = ([None] * n for _ in range(5))
+    parts, firsts, seconds, thirds = ([None] * n for _ in range(4))
     out_grads = tok_swaps(out_grad)
-    h = spread(Chain(jnp.zeros((8, 128), F32)).call(*hidden_args())[0])
+    h = spread(Chain(jnp.zeros((8, 128), F32)).call(*hidden_args(), mib=MEDIUM)[0])
     out_grads = tok_last(*out_grads)
     grads, parts[0], firsts[0] = partial(0)
     _, parts[1], firsts[1] = partial(1)
@@ -376,12 +392,13 @@
     (h["near_end"],) = spread_end(h, h["near_end"])
     hand_out(0)
     (h["far_end"],) = chain.relay(h["far_end"])
-    groups[0] = grads_of(0)
+    groups = [grads_of(0, 0)]
+    down = down_step()
     hand_out(1)
     spread_far(groups[0])
     (thirds[1],) = chain.relay(thirds[1])
     spread_near(groups[0])
-    groups[1] = grads_of(1)
+    groups.append(grads_of(1, 1))
     spread_end(groups[0])
     (groups[0]["near_end"],) = chain.relay(groups[0]["near_end"])
     (inputs_b,) = chain.relay(saved_input.astype(BF))
@@ -395,14 +412,14 @@
         [whole(depth, tokens)],
         scalars=where,
     )[0]
-    down = down_step()
     spread_near(groups[1])
     spread_far(groups[1])
     (groups[0]["far_end"],) = chain.relay(groups[0]["far_end"])
-    total = input_step(0, None)
+    total = input_step(0, None, ALL)
     weights = weights_step(0, ())
     spread_end(groups[1])
-    mine, other = input_step(1, total)
+    others = input_step(1, total, ALL[:4])
+    mine, other = input_last(1, total, others)
     got = lax.ppermute(other, "tok", CORE_SWAP)
     keep, *others = chain.call(
         split_again,

time: 253 us -> 235 us (0.929)
  Pallas kernels: 82.9 us -> 46.6 us
  waiting for transfers between devices: 90.8 us -> 125 us
  starting transfers between devices: 74 us -> 54.6 us
  local copies, waits for them, and re-layouts: 1.18 us -> 7.07 us
    pallas_call x32 -> x33, Pallas kernels: 82.9 us -> 46.6 us  [call(): pl.pallas_call(kernel, grid_spec=pltpu.PrefetchScalarGridSpec(num_scalar_...]
    ppermute x21, waiting for transfers between devices: 81 us -> 116 us  [send(): return lax.ppermute(x, 'inp', perm)]
    ppermute x21, starting transfers between devices: 66.4 us -> 46.9 us  [send(): return lax.ppermute(x, 'inp', perm)]
    unnamed x0 -> x24, local copies, waits for them, and re-layouts: none -> 7.07 us
  transfers between devices with their start and end apart: 31 -> 31, of which waited for: 15 -> 18; matrix products, arithmetic and copies ran while one was open for 1% -> 0% of each run, Pallas kernels for 27% -> 17%
where the time goes in v3:
time: 235 us; the launch traced here: 234 us
  waiting for transfers between devices  125 us (53%)
  starting transfers between devices  54.6 us (23%)
  Pallas kernels  46.6 us (20%)
  local copies, waits for them, and re-layouts  7.07 us (3%)
    ppermute x21, waiting for transfers between devices, send(): return lax.ppermute(x, 'inp', perm)  116 us
    ppermute x21, starting transfers between devices, send(): return lax.ppermute(x, 'inp', perm)  46.9 us
    pallas_call x33, Pallas kernels, call(): pl.pallas_call(kernel, grid_spec=pltpu.PrefetchScalarGridSpec(num_scalar_...  46.6 us
    unnamed x24, local copies, waits for them, and re-layouts  7.07 us
    ppermute x2, waiting for transfers between devices, tok_swaps(): lax.ppermute(x, 'tok', X_SWAP)  5.84 us
  transfers between devices with their start and end apart: 31, of which 18 were waited for; matrix products, arithmetic and copies ran while one was open for 0% of the time, Pallas kernels for 17%

profile of v3, /device:TPU:0, one launch (start us, length us, event | category | flops | bytes accessed | tf_op | source)
XLA Modules:
  0.0 234.5 jit_solution(13410973540916436439)
XLA Ops:
  8.7 4.4 %collective-permute-start.4 = (bf16[128,3584]{1,0:T(8,128)(2,1)}, bf16[128,3584]{1,0:T(8,128)(2,1)S(1)}, u32[]{:S(2)}, u32[]{:S(2)}) collective-permute-start(bf16[128,3584]{1,0:T(8,128)(2,1)} %get-tuple-element.84.refs_2_), channel_id=1, source_target_pairs={{0,8},{8,0},{16,24},{24,16},{1,9},{9,1},{17,25},{25,17},{2,10},{10... | collective-permute-start | bytes 2752520 | tf_op jit(solution)/shard_map/ppermute | solution.py:29
  19.1 3.6 %shard_map.103 = (f32[8,128]{1,0:T(8,128)S(1)}, f32[512,1792]{1,0:T(8,128)S(1)}, bf16[256,1792]{1,0:T(8,128)(2,1)S(1)}, bf16[512,1024]{1,0:T(8,128)(2,1)S(1)}) custom-call(s32[3]{0:T(128)S(1)} %pad_add_fusion.refs_0_, f32[8,128]{1,0:T(8,128)S(1)} %get-tuple-element.79.refs_1_, bf16[128,1024]{1,0:T(8,128)(2,1)S(1)} %copy-done.6, ...), custom_call_target="tpu_custom_call", output_to_operand_aliasing={{0}: (1, {})} | custom-call | tf_op jit(solution)/shard_map/pallas_call | solution.py:59
  27.6 6.6 %collective-permute-done.4.refs_1_ = bf16[128,3584]{1,0:T(8,128)(2,1)S(1)} collective-permute-done((bf16[128,3584]{1,0:T(8,128)(2,1)}, bf16[128,3584]{1,0:T(8,128)(2,1)S(1)}, u32[]{:S(2)}, u32[]{:S(2)}) %collective-permute-start.4) | collective-permute-done | bytes 917536 | tf_op jit(solution)/shard_map/ppermute | solution.py:29
  36.3 6.0 %collective-permute-start.9 = (bf16[256,1792]{1,0:T(8,128)(2,1)S(1)}, bf16[256,1792]{1,0:T(8,128)(2,1)S(1)}, u32[]{:S(2)}, u32[]{:S(2)}) collective-permute-start(bf16[256,1792]{1,0:T(8,128)(2,1)S(1)} %get-tuple-element.94), channel_id=1, source_target_pairs={{0,8},{24,16},{1,9},{25,17},{2,10},{26,18},{3,11},{27,19},{4,12},{... | collective-permute-start | bytes 2752520 | tf_op jit(solution)/shard_map/ppermute | solution.py:29
  42.3 11.5 %collective-permute-done.5.refs_1_ = bf16[256,1792]{1,0:T(8,128)(2,1)S(1)} collective-permute-done((bf16[256,1792]{1,0:T(8,128)(2,1)S(1)}, bf16[256,1792]{1,0:T(8,128)(2,1)S(1)}, u32[]{:S(2)}, u32[]{:S(2)}) %collective-permute-start.5) | collective-permute-done | bytes 917536 | tf_op jit(solution)/shard_map/ppermute | solution.py:29
  58.4 13.3 %collective-permute-done.9.refs_3_ = bf16[256,1792]{1,0:T(8,128)(2,1)S(1)} collective-permute-done((bf16[256,1792]{1,0:T(8,128)(2,1)S(1)}, bf16[256,1792]{1,0:T(8,128)(2,1)S(1)}, u32[]{:S(2)}, u32[]{:S(2)}) %collective-permute-start.9) | collective-permute-done | bytes 917536 | tf_op jit(solution)/shard_map/ppermute | solution.py:29
  72.0 6.0 %collective-permute-start.11 = (bf16[128,1792]{1,0:T(8,128)(2,1)S(1)}, bf16[128,1792]{1,0:T(8,128)(2,1)S(1)}, u32[]{:S(2)}, u32[]{:S(2)}) collective-permute-start(bf16[128,1792]{1,0:T(8,128)(2,1)S(1)} %get-tuple-element.99), channel_id=1, source_target_pairs={{0,8},{8,0},{16,24},{24,16},{1,9},{9,1},{17,25},{25,17},{2,10},{10... | collective-permute-start | bytes 1376264 | tf_op jit(solution)/shard_map/ppermute | solution.py:29
  80.2 7.0 %collective-permute-done.11.refs_3_ = bf16[128,1792]{1,0:T(8,128)(2,1)S(1)} collective-permute-done((bf16[128,1792]{1,0:T(8,128)(2,1)S(1)}, bf16[128,1792]{1,0:T(8,128)(2,1)S(1)}, u32[]{:S(2)}, u32[]{:S(2)}) %collective-permute-start.11) | collective-permute-done | bytes 458784 | tf_op jit(solution)/shard_map/ppermute | solution.py:29
  88.9 7.1 %shard_map.113 = (f32[8,128]{1,0:T(8,128)S(1)}, bf16[3584,1024]{1,0:T(8,128)(2,1)}) custom-call(f32[8,128]{1,0:T(8,128)S(1)} %get-tuple-element.100.refs_0_, bf16[512,1024]{1,0:T(8,128)(2,1)S(1)} %get-tuple-element.82.refs_1_, bf16[128,3584]{1,0:T(8,128)(2,1)} %get-tuple-element.84.refs_2_, ...), custom_call_target="tpu_custom_call", output_to_operand_aliasing={{0}: (0, {})} | custom-call | tf_op jit(solution)/shard_map/pallas_call | solution.py:59
  96.1 7.2 %collective-permute-start.14 = (bf16[128,1792]{1,0:T(8,128)(2,1)S(1)}, bf16[128,1792]{1,0:T(8,128)(2,1)S(1)}, u32[]{:S(2)}, u32[]{:S(2)}) collective-permute-start(bf16[128,1792]{1,0:T(8,128)(2,1)S(1)} %get-tuple-element.108), channel_id=1, source_target_pairs={{0,8},{8,0},{16,24},{24,16},{1,9},{9,1},{17,25},{25,17},{2,10},{10... | collective-permute-start | bytes 1376264 | tf_op jit(solution)/shard_map/ppermute | solution.py:29
  103.3 8.2 %collective-permute-done.13.refs_1_ = bf16[2,128,1792]{2,1,0:T(8,128)(2,1)S(1)} collective-permute-done((bf16[2,128,1792]{2,1,0:T(8,128)(2,1)S(1)}, bf16[2,128,1792]{2,1,0:T(8,128)(2,1)S(1)}, u32[]{:S(2)}, u32[]{:S(2)}) %collective-permute-start.13) | collective-permute-done | bytes 917536 | tf_op jit(solution)/shard_map/ppermute | solution.py:29
  112.2 5.4 %collective-permute-done.14.refs_1_ = bf16[128,1792]{1,0:T(8,128)(2,1)S(1)} collective-permute-done((bf16[128,1792]{1,0:T(8,128)(2,1)S(1)}, bf16[128,1792]{1,0:T(8,128)(2,1)S(1)}, u32[]{:S(2)}, u32[]{:S(2)}) %collective-permute-start.14) | collective-permute-done | bytes 458784 | tf_op jit(solution)/shard_map/ppermute | solution.py:29
  120.7 7.3 %collective-permute-start.22 = (bf16[2,128,1792]{2,1,0:T(8,128)(2,1)S(1)}, bf16[2,128,1792]{2,1,0:T(8,128)(2,1)S(1)}, u32[]{:S(2)}, u32[]{:S(2)}) collective-permute-start(bf16[2,128,1792]{2,1,0:T(8,128)(2,1)S(1)} %get-tuple-element.122.refs_1_.refs_2_), channel_id=1, source_target_pairs={{0,8},{8,0},{16,24},{24,16},{1,9},{9,1},{17,25},{25,17},{2,10},{10... | collective-permute-start | bytes 2752520 | tf_op jit(solution)/shard_map/ppermute | solution.py:29
  128.0 17.3 %collective-permute-done.17.refs_1_ = bf16[2,128,1792]{2,1,0:T(8,128)(2,1)S(1)} collective-permute-done((bf16[2,128,1792]{2,1,0:T(8,128)(2,1)S(1)}, bf16[2,128,1792]{2,1,0:T(8,128)(2,1)S(1)}, u32[]{:S(2)}, u32[]{:S(2)}) %collective-permute-start.17) | collective-permute-done | bytes 917536 | tf_op jit(solution)/shard_map/ppermute | solution.py:29
  145.9 5.8 %collective-permute-done.18.refs_1_ = bf16[128,1024]{1,0:T(8,128)(2,1)S(1)} collective-permute-done((bf16[128,1024]{1,0:T(8,128)(2,1)S(1)}, bf16[128,1024]{1,0:T(8,128)(2,1)S(1)}, u32[]{:S(2)}, u32[]{:S(2)}) %collective-permute-start.18) | collective-permute-done | bytes 262176 | tf_op jit(solution)/shard_map/ppermute | solution.py:226
  154.2 4.5 %collective-permute-done.22.refs_1_ = bf16[2,128,1792]{2,1,0:T(8,128)(2,1)S(1)} collective-permute-done((bf16[2,128,1792]{2,1,0:T(8,128)(2,1)S(1)}, bf16[2,128,1792]{2,1,0:T(8,128)(2,1)S(1)}, u32[]{:S(2)}, u32[]{:S(2)}) %collective-permute-start.22) | collective-permute-done | bytes 917536 | tf_op jit(solution)/shard_map/ppermute | solution.py:29
  160.9 17.5 %collective-permute-done.23.refs_1_ = bf16[2,128,1792]{2,1,0:T(8,128)(2,1)S(1)} collective-permute-done((bf16[2,128,1792]{2,1,0:T(8,128)(2,1)S(1)}, bf16[2,128,1792]{2,1,0:T(8,128)(2,1)S(1)}, u32[]{:S(2)}, u32[]{:S(2)}) %collective-permute-start.23) | collective-permute-done | bytes 917536 | tf_op jit(solution)/shard_map/ppermute | solution.py:29
  178.4 5.2 %shard_map.127 = (f32[8,128]{1,0:T(8,128)S(1)}, f32[512,1024]{1,0:T(8,128)S(1)}) custom-call(f32[8,128]{1,0:T(8,128)S(1)} %get-tuple-element.126.refs_0_, bf16[2,128,1792]{2,1,0:T(8,128)(2,1)S(1)} %get-tuple-element.106.refs_1_.refs_2_, bf16[2,128,1792]{2,1,0:T(8,128)(2,1)S(1)} %get-tuple-element.113.refs_2_.refs_3_, ...), custom_call_target="tpu_custom_call", output_to_operand_aliasing={{0}: (0, {})} | custom-call | tf_op jit(solution)/shard_map/pallas_call | solution.py:59
  183.5 6.6 %shard_map.128 = (f32[8,128]{1,0:T(8,128)S(1)}, bf16[1024,3584]{1,0:T(8,128)(2,1)}, bf16[1024,3584]{1,0:T(8,128)(2,1)}) custom-call(f32[8,128]{1,0:T(8,128)S(1)} %get-tuple-element.129.refs_0_, bf16[1024,512]{1,0:T(8,128)(2,1)S(1)} %get-tuple-element.130.refs_1_, ...), custom_call_target="tpu_custom_call", output_to_operand_aliasing={{0}: (0, {})} | custom-call | tf_op jit(solution)/shard_map/pallas_call | solution.py:59
  191.4 6.6 %collective-permute-done.25.refs_4_.refs_5_ = bf16[2,128,1792]{2,1,0:T(8,128)(2,1)S(1)} collective-permute-done((bf16[2,128,1792]{2,1,0:T(8,128)(2,1)S(1)}, bf16[2,128,1792]{2,1,0:T(8,128)(2,1)S(1)}, u32[]{:S(2)}, u32[]{:S(2)}) %collective-permute-start.25) | collective-permute-done | bytes 917536 | tf_op jit(solution)/shard_map/ppermute | solution.py:29
  198.0 4.2 %shard_map.130 = (f32[8,128]{1,0:T(8,128)S(1)}, f32[384,1024]{1,0:T(8,128)S(1)}) custom-call(f32[8,128]{1,0:T(8,128)S(1)} %get-tuple-element.133.refs_0_, bf16[2,128,1792]{2,1,0:T(8,128)(2,1)S(1)} %get-tuple-element.122.refs_1_.refs_2_, bf16[2,128,1792]{2,1,0:T(8,128)(2,1)S(1)} %get-tuple-element.132.refs_2_.refs_3_, ...), custom_call_target="tpu_custom_call", output_to_operand_aliasing={{0}: (0, {})} | custom-call | tf_op jit(solution)/shard_map/pallas_call | solution.py:59
  202.2 14.5 %collective-permute-done.26.refs_3_.refs_7_ = bf16[2,128,1792]{2,1,0:T(8,128)(2,1)S(1)} collective-permute-done((bf16[2,128,1792]{2,1,0:T(8,128)(2,1)S(1)}, bf16[2,128,1792]{2,1,0:T(8,128)(2,1)S(1)}, u32[]{:S(2)}, u32[]{:S(2)}) %collective-permute-start.26) | collective-permute-done | bytes 917536 | tf_op jit(solution)/shard_map/ppermute | solution.py:29
  216.7 4.3 %shard_map.131 = (f32[8,128]{1,0:T(8,128)S(1)}, f32[256,1024]{1,0:T(8,128)S(1)}, bf16[256,1024]{1,0:T(8,128)(2,1)S(1)}) custom-call(s32[3]{0:T(128)S(1)} %pad_add_fusion.refs_0_, f32[8,128]{1,0:T(8,128)S(1)} %get-tuple-element.136.refs_1_, bf16[2,128,1792]{2,1,0:T(8,128)(2,1)S(1)} %get-tuple-element.137.refs_2_.refs_6_, ...), custom_call_target="tpu_custom_call", output_to_operand_aliasing={{0}: (1, {})} | custom-call | tf_op jit(solution)/shard_map/pallas_call | solution.py:59
  227.2 6.6 %shard_map.133 = (f32[8,128]{1,0:T(8,128)S(1)}, bf16[1024,3584]{1,0:T(8,128)(2,1)}, bf16[1024,3584]{1,0:T(8,128)(2,1)}) custom-call(f32[8,128]{1,0:T(8,128)S(1)} %get-tuple-element.142.refs_0_, bf16[1024,512]{1,0:T(8,128)(2,1)S(1)} %get-tuple-element.130.refs_1_, ...), custom_call_target="tpu_custom_call", output_to_operand_aliasing={{0}: (0, {}), {1}: (8, {}), {2}: (9, {})} | custom-call | tf_op jit(solution)/shard_map/pallas_call | solution.py:59
  (101 shorter events, 46.9 us)
Async XLA Ops:
  0.6 12.5 %collective-permute-start = (bf16[128,1024]{1,0:T(8,128)(2,1)}, bf16[128,1024]{1,0:T(8,128)(2,1)S(1)}, u32[]{:S(2)}, u32[]{:S(2)}) collective-permute-start(bf16[128,1024]{1,0:T(8,128)(2,1)} %refs_2_.3), channel_id=1, source_target_pairs={{0,2},{2,0},{1,3},{3,1},{4,6},{6,4},{5,7},{7,5},{8,10},{10,8},{9,1... | collective-permute-start | bytes 786440 | tf_op jit(solution)/shard_map/ppermute | solution.py:226
  8.0 19.6 %collective-permute-start.3 = (bf16[128,3584]{1,0:T(8,128)(2,1)}, bf16[128,3584]{1,0:T(8,128)(2,1)S(1)}, u32[]{:S(2)}, u32[]{:S(2)}) collective-permute-start(bf16[128,3584]{1,0:T(8,128)(2,1)} %get-tuple-element.84.refs_2_), channel_id=1, source_target_pairs={{8,16},{16,8},{9,17},{17,9},{10,18},{18,10},{11,19},{19,11},{12,20... | collective-permute-start | bytes 2752520 | tf_op jit(solution)/shard_map/ppermute | solution.py:29
  8.7 25.5 %collective-permute-start.4 = (bf16[128,3584]{1,0:T(8,128)(2,1)}, bf16[128,3584]{1,0:T(8,128)(2,1)S(1)}, u32[]{:S(2)}, u32[]{:S(2)}) collective-permute-start(bf16[128,3584]{1,0:T(8,128)(2,1)} %get-tuple-element.84.refs_2_), channel_id=1, source_target_pairs={{0,8},{8,0},{16,24},{24,16},{1,9},{9,1},{17,25},{25,17},{2,10},{10... | collective-permute-start | bytes 2752520 | tf_op jit(solution)/shard_map/ppermute | solution.py:29
  22.6 31.2 %collective-permute-start.5 = (bf16[256,1792]{1,0:T(8,128)(2,1)S(1)}, bf16[256,1792]{1,0:T(8,128)(2,1)S(1)}, u32[]{:S(2)}, u32[]{:S(2)}) collective-permute-start(bf16[256,1792]{1,0:T(8,128)(2,1)S(1)} %get-tuple-element.87), channel_id=1, source_target_pairs={{0,8},{24,16},{1,9},{25,17},{2,10},{26,18},{3,11},{27,19},{4,12},{... | collective-permute-start | bytes 2752520 | tf_op jit(solution)/shard_map/ppermute | solution.py:29
  34.3 20.9 %collective-permute-start.6 = (bf16[128,3584]{1,0:T(8,128)(2,1)S(1)}, bf16[128,3584]{1,0:T(8,128)(2,1)S(1)}, u32[]{:S(2)}, u32[]{:S(2)}) collective-permute-start(bf16[128,3584]{1,0:T(8,128)(2,1)S(1)} %get-tuple-element.90.refs_3_), channel_id=1, source_target_pairs={{8,16},{16,8},{9,17},{17,9},{10,18},{18,10},{11,19},{19,11},{12,20... | collective-permute-start | bytes 2752520 | tf_op jit(solution)/shard_map/ppermute | solution.py:29
  35.0 22.2 %collective-permute-start.7 = (bf16[128,3584]{1,0:T(8,128)(2,1)S(1)}, bf16[128,3584]{1,0:T(8,128)(2,1)S(1)}, u32[]{:S(2)}, u32[]{:S(2)}) collective-permute-start(bf16[128,3584]{1,0:T(8,128)(2,1)S(1)} %get-tuple-element.91.refs_4_), channel_id=1, source_target_pairs={{8,0},{16,24},{9,1},{17,25},{10,2},{18,26},{11,3},{19,27},{12,4},{... | collective-permute-start | bytes 2752520 | tf_op jit(solution)/shard_map/ppermute | solution.py:29
  36.3 35.4 %collective-permute-start.9 = (bf16[256,1792]{1,0:T(8,128)(2,1)S(1)}, bf16[256,1792]{1,0:T(8,128)(2,1)S(1)}, u32[]{:S(2)}, u32[]{:S(2)}) collective-permute-start(bf16[256,1792]{1,0:T(8,128)(2,1)S(1)} %get-tuple-element.94), channel_id=1, source_target_pairs={{0,8},{24,16},{1,9},{25,17},{2,10},{26,18},{3,11},{27,19},{4,12},{... | collective-permute-start | bytes 2752520 | tf_op jit(solution)/shard_map/ppermute | solution.py:29
  54.3 17.4 %collective-permute-start.8 = (bf16[256,1792]{1,0:T(8,128)(2,1)S(1)}, bf16[256,1792]{1,0:T(8,128)(2,1)S(1)}, u32[]{:S(2)}, u32[]{:S(2)}) collective-permute-start(bf16[256,1792]{1,0:T(8,128)(2,1)S(1)} %get-tuple-element.93), channel_id=1, source_target_pairs={{8,16},{16,8},{9,17},{17,9},{10,18},{18,10},{11,19},{19,11},{12,20... | collective-permute-start | bytes 2752520 | tf_op jit(solution)/shard_map/ppermute | solution.py:29
  57.1 23.1 %collective-permute-start.10 = (bf16[128,3584]{1,0:T(8,128)(2,1)S(1)}, bf16[128,3584]{1,0:T(8,128)(2,1)S(1)}, u32[]{:S(2)}, u32[]{:S(2)}) collective-permute-start(bf16[128,3584]{1,0:T(8,128)(2,1)S(1)} %get-tuple-element.97.refs_6_), channel_id=1, source_target_pairs={{8,0},{16,24},{9,1},{17,25},{10,2},{18,26},{11,3},{19,27},{12,4},{... | collective-permute-start | bytes 2752520 | tf_op jit(solution)/shard_map/ppermute | solution.py:29
  72.0 15.2 %collective-permute-start.11 = (bf16[128,1792]{1,0:T(8,128)(2,1)S(1)}, bf16[128,1792]{1,0:T(8,128)(2,1)S(1)}, u32[]{:S(2)}, u32[]{:S(2)}) collective-permute-start(bf16[128,1792]{1,0:T(8,128)(2,1)S(1)} %get-tuple-element.99), channel_id=1, source_target_pairs={{0,8},{8,0},{16,24},{24,16},{1,9},{9,1},{17,25},{25,17},{2,10},{10... | collective-permute-start | bytes 1376264 | tf_op jit(solution)/shard_map/ppermute | solution.py:29
  78.0 18.0 %collective-permute-start.12 = (bf16[256,1792]{1,0:T(8,128)(2,1)S(1)}, bf16[256,1792]{1,0:T(8,128)(2,1)S(1)}, u32[]{:S(2)}, u32[]{:S(2)}) collective-permute-start(bf16[256,1792]{1,0:T(8,128)(2,1)S(1)} %get-tuple-element.104), channel_id=1, source_target_pairs={{8,16},{16,8},{9,17},{17,9},{10,18},{18,10},{11,19},{19,11},{12,20... | collective-permute-start | bytes 2752520 | tf_op jit(solution)/shard_map/ppermute | solution.py:29
  88.1 23.4 %collective-permute-start.13 = (bf16[2,128,1792]{2,1,0:T(8,128)(2,1)S(1)}, bf16[2,128,1792]{2,1,0:T(8,128)(2,1)S(1)}, u32[]{:S(2)}, u32[]{:S(2)}) collective-permute-start(bf16[2,128,1792]{2,1,0:T(8,128)(2,1)S(1)} %get-tuple-element.106.refs_1_.refs_2_), channel_id=1, source_target_pairs={{0,8},{8,0},{16,24},{24,16},{1,9},{9,1},{17,25},{25,17},{2,10},{10... | collective-permute-start | bytes 2752520 | tf_op jit(solution)/shard_map/ppermute | solution.py:29
  88.2 29.4 %collective-permute-start.15 = (bf16[2,128,1792]{2,1,0:T(8,128)(2,1)S(1)}, bf16[2,128,1792]{2,1,0:T(8,128)(2,1)S(1)}, u32[]{:S(2)}, u32[]{:S(2)}) collective-permute-start(bf16[2,128,1792]{2,1,0:T(8,128)(2,1)S(1)} %get-tuple-element.106.refs_1_.refs_2_), channel_id=1, source_target_pairs={{8,16},{16,8},{9,17},{17,9},{10,18},{18,10},{11,19},{19,11},{12,20... | collective-permute-start | bytes 2752520 | tf_op jit(solution)/shard_map/ppermute | solution.py:29
  96.1 21.5 %collective-permute-start.14 = (bf16[128,1792]{1,0:T(8,128)(2,1)S(1)}, bf16[128,1792]{1,0:T(8,128)(2,1)S(1)}, u32[]{:S(2)}, u32[]{:S(2)}) collective-permute-start(bf16[128,1792]{1,0:T(8,128)(2,1)S(1)} %get-tuple-element.108), channel_id=1, source_target_pairs={{0,8},{8,0},{16,24},{24,16},{1,9},{9,1},{17,25},{25,17},{2,10},{10... | collective-permute-start | bytes 1376264 | tf_op jit(solution)/shard_map/ppermute | solution.py:29
  111.5 16.5 %collective-permute-start.16 = (bf16[2,128,1792]{2,1,0:T(8,128)(2,1)S(1)}, bf16[2,128,1792]{2,1,0:T(8,128)(2,1)S(1)}, u32[]{:S(2)}, u32[]{:S(2)}) collective-permute-start(bf16[2,128,1792]{2,1,0:T(8,128)(2,1)S(1)} %get-tuple-element.113.refs_2_.refs_3_), channel_id=1, source_target_pairs={{8,16},{16,8},{9,17},{17,9},{10,18},{18,10},{11,19},{19,11},{12,20... | collective-permute-start | bytes 2752520 | tf_op jit(solution)/shard_map/ppermute | solution.py:29
  117.6 27.8 %collective-permute-start.17 = (bf16[2,128,1792]{2,1,0:T(8,128)(2,1)S(1)}, bf16[2,128,1792]{2,1,0:T(8,128)(2,1)S(1)}, u32[]{:S(2)}, u32[]{:S(2)}) collective-permute-start(bf16[2,128,1792]{2,1,0:T(8,128)(2,1)S(1)} %get-tuple-element.115.refs_3_.refs_4_), channel_id=1, source_target_pairs={{8,0},{16,24},{9,1},{17,25},{10,2},{18,26},{11,3},{19,27},{12,4},{... | collective-permute-start | bytes 2752520 | tf_op jit(solution)/shard_map/ppermute | solution.py:29
  119.8 34.3 %collective-permute-start.21 = (bf16[2,128,1792]{2,1,0:T(8,128)(2,1)S(1)}, bf16[2,128,1792]{2,1,0:T(8,128)(2,1)S(1)}, u32[]{:S(2)}, u32[]{:S(2)}) collective-permute-start(bf16[2,128,1792]{2,1,0:T(8,128)(2,1)S(1)} %get-tuple-element.122.refs_1_.refs_2_), channel_id=1, source_target_pairs={{8,16},{16,8},{9,17},{17,9},{10,18},{18,10},{11,19},{19,11},{12,20... | collective-permute-start | bytes 2752520 | tf_op jit(solution)/shard_map/ppermute | solution.py:29
  120.7 38.0 %collective-permute-start.22 = (bf16[2,128,1792]{2,1,0:T(8,128)(2,1)S(1)}, bf16[2,128,1792]{2,1,0:T(8,128)(2,1)S(1)}, u32[]{:S(2)}, u32[]{:S(2)}) collective-permute-start(bf16[2,128,1792]{2,1,0:T(8,128)(2,1)S(1)} %get-tuple-element.122.refs_1_.refs_2_), channel_id=1, source_target_pairs={{0,8},{8,0},{16,24},{24,16},{1,9},{9,1},{17,25},{25,17},{2,10},{10... | collective-permute-start | bytes 2752520 | tf_op jit(solution)/shard_map/ppermute | solution.py:29
  151.8 26.6 %collective-permute-start.23 = (bf16[2,128,1792]{2,1,0:T(8,128)(2,1)S(1)}, bf16[2,128,1792]{2,1,0:T(8,128)(2,1)S(1)}, u32[]{:S(2)}, u32[]{:S(2)}) collective-permute-start(bf16[2,128,1792]{2,1,0:T(8,128)(2,1)S(1)} %get-tuple-element.125.refs_5_.refs_6_), channel_id=1, source_target_pairs={{8,0},{16,24},{9,1},{17,25},{10,2},{18,26},{11,3},{19,27},{12,4},{... | collective-permute-start | bytes 2752520 | tf_op jit(solution)/shard_map/ppermute | solution.py:29
  158.7 31.4 %collective-permute-start.24 = (bf16[2,128,1792]{2,1,0:T(8,128)(2,1)S(1)}, bf16[2,128,1792]{2,1,0:T(8,128)(2,1)S(1)}, u32[]{:S(2)}, u32[]{:S(2)}) collective-permute-start(bf16[2,128,1792]{2,1,0:T(8,128)(2,1)S(1)} %get-tuple-element.132.refs_2_.refs_3_), channel_id=1, source_target_pairs={{8,16},{16,8},{9,17},{17,9},{10,18},{18,10},{11,19},{19,11},{12,20... | collective-permute-start | bytes 2752520 | tf_op jit(solution)/shard_map/ppermute | solution.py:29
  159.4 38.6 %collective-permute-start.25 = (bf16[2,128,1792]{2,1,0:T(8,128)(2,1)S(1)}, bf16[2,128,1792]{2,1,0:T(8,128)(2,1)S(1)}, u32[]{:S(2)}, u32[]{:S(2)}) collective-permute-start(bf16[2,128,1792]{2,1,0:T(8,128)(2,1)S(1)} %get-tuple-element.134.refs_3_.refs_4_), channel_id=1, source_target_pairs={{8,0},{16,24},{9,1},{17,25},{10,2},{18,26},{11,3},{19,27},{12,4},{... | collective-permute-start | bytes 2752520 | tf_op jit(solution)/shard_map/ppermute | solution.py:29
  190.1 26.6 %collective-permute-start.26 = (bf16[2,128,1792]{2,1,0:T(8,128)(2,1)S(1)}, bf16[2,128,1792]{2,1,0:T(8,128)(2,1)S(1)}, u32[]{:S(2)}, u32[]{:S(2)}) collective-permute-start(bf16[2,128,1792]{2,1,0:T(8,128)(2,1)S(1)} %get-tuple-element.137.refs_2_.refs_6_), channel_id=1, source_target_pairs={{8,0},{16,24},{9,1},{17,25},{10,2},{18,26},{11,3},{19,27},{12,4},{... | collective-permute-start | bytes 2752520 | tf_op jit(solution)/shard_map/ppermute | solution.py:29
  223.6 10.1 %collective-permute-start.28 = (bf16[64,1024]{1,0:T(8,128)(2,1)S(1)}, bf16[64,1024]{1,0:T(8,128)(2,1)S(1)}, u32[]{:S(2)}, u32[]{:S(2)}) collective-permute-start(bf16[64,1024]{1,0:T(8,128)(2,1)S(1)} %get-tuple-element.147), channel_id=1, source_target_pairs={{0,4},{4,0},{1,5},{5,1},{2,6},{6,2},{3,7},{7,3},{8,12},{12,8},{9,1... | collective-permute-start | bytes 393224 | tf_op jit(solution)/shard_map/ppermute | solution.py:435
  225.2 8.5 %collective-permute-start.29 = (bf16[64,1024]{1,0:T(8,128)(2,1)S(1)}, bf16[64,1024]{1,0:T(8,128)(2,1)S(1)}, u32[]{:S(2)}, u32[]{:S(2)}) collective-permute-start(bf16[64,1024]{1,0:T(8,128)(2,1)S(1)} %get-tuple-element.148), channel_id=1, source_target_pairs={{0,2},{2,0},{1,3},{3,1},{4,6},{6,4},{5,7},{7,5},{8,10},{10,8},{9,1... | collective-permute-start | bytes 393224 | tf_op jit(solution)/shard_map/ppermute | solution.py:436
  (19 other events, 400.8 us)

commit v4 on v3

--- a/solution.py
+++ b/solution.py
@@ -1,4 +1,5 @@
 import functools
+import math
 
 import jax
 import jax.numpy as jnp
@@ -13,7 +14,7 @@
 STRAIGHT = (((1,), (0,)), ((), ()))
 ANY = pl.BlockSpec(memory_space=pl.ANY)
 MIB = 1024 * 1024
-SMALL, MEDIUM, LARGE = 8, 16, 28
+SMALL, MEDIUM, LARGE, WHOLE = 8, 16, 28, 62
 
 ENDS_IN = [(0, 1), (3, 2)]
 MIDDLE = [(1, 2), (2, 1)]
@@ -30,6 +31,7 @@
 
 
 LAST_TILE = 512
+FIRST = 7
 ALL = ("own", "pair", "near", "near_end", "far", "far_end")
 
 
@@ -177,6 +179,12 @@
     up_ref[...] = dot(inputs_ref[...], joined(*[r[1] for r in refs[:6]]), STRAIGHT).astype(BF)
 
 
+def halves(x_ref, low_ref, high_ref):
+    w = low_ref.shape[2]
+    low_ref[...] = x_ref[:, :, :w]
+    high_ref[...] = x_ref[:, :, w:]
+
+
 def down_grads(grads_ref, *refs):
     refs[-1][...] = dot(joined(*[r[...] for r in refs[:6]]), grads_ref[...], LEAD).astype(BF)
 
@@ -211,9 +219,9 @@
     z, o, t = lax.axis_index("inp"), lax.axis_index("out"), lax.axis_index("tok")
     where = jnp.stack([z, o, t]).astype(jnp.int32)
     chain = Chain(jnp.zeros((8, 128), F32))
-    half = ff // 2
-    cuts = [(0, half), (half, half)]
-    widths = [half, half]
+    first = ff // 14 * FIRST
+    cuts = [(0, first), (first, ff - first)]
+    widths = [w for _, w in cuts]
     group_cuts = cuts
 
     def cols(height, tile, start, row=0):
@@ -242,7 +250,7 @@
 
     def partial(c):
         start, w = cuts[c]
-        tile = tile_of(w, 1024)
+        tile = tile_of(math.gcd(start, w), 1024)
         w_spec = pl.BlockSpec((tile, depth), lambda j, *_: (start // tile + j, 0))
         outs = [shape((tokens, w), F32), shape((tokens // 2, w), BF)]
         specs = [cols(tokens, tile, 0), cols(tokens // 2, tile, 0)]
@@ -296,7 +304,7 @@
 
     def grads_of(c, g):
         start, w = group_cuts[g]
-        tile = tile_of(w, 1024)
+        tile = tile_of(math.gcd(start, w), 1024)
         at = start - cuts[c][0]
         own = chain.call(
             swiglu_grads,
@@ -343,31 +351,53 @@
             [across],
             scratch=[pltpu.VMEM((2, height, w), BF)], mib=LARGE)[0]
 
-    def input_last(g, before, others):
-        start, w = group_cuts[g]
+    def far_more(x, cut, before):
+        start, w = cut
+        tile = tile_of(depth, LAST_TILE)
+        wide = pl.BlockSpec((pl.Element(tile), pl.Element(w)), lambda j: (j * tile, start))
+        return chain.call(
+            functools.partial(input_sums_more, 2),
+            (depth // tile,),
+            [*x, w_gate, w_up, before],
+            [whole(2, rows, w)] * 2 + [wide, wide, cols(rows, tile, 0, 3)],
+            [shape((rows, depth), F32)],
+            [cols(rows, tile, 0)],
+            scratch=[pltpu.VMEM((2, rows, w), BF)],
+            mib=LARGE,
+        )[0]
+
+    def far_last(x, cut, before, others):
+        start, w = cut
         tile = tile_of(depth, LAST_TILE)
         wide = pl.BlockSpec((pl.Element(tile), pl.Element(w)), lambda j, *_: (j * tile, start))
         return chain.call(
             input_sums_last,
             (depth // tile,),
-            [groups[g]["far"], groups[g]["far_end"], w_gate, w_up, before, others],
-            [whole(2, rows, w)] * 2 + [wide, wide, cols(rows, tile, 0, 3), cols(3 * rows, tile, 0)],
+            [*x, w_gate, w_up, before, others],
+            [whole(2, rows, w)] * 2 + [wide, wide, cols(rows, tile, 0), cols(3 * rows, tile, 0)],
             [shape((tokens // 2, depth), F32), shape((tokens // 2, depth), BF)],
             [cols(tokens // 2, tile, 0)] * 2,
             scalars=where,
-            scratch=[pltpu.VMEM((2, rows, w), BF), pltpu.VMEM((tokens, tile), F32)], mib=LARGE)
-
-    def weights_step(g, before):
-        start, w = group_cuts[g]
-        tile = tile_of(w, 1024)
+            scratch=[pltpu.VMEM((2, rows, w), BF), pltpu.VMEM((tokens, tile), F32)],
+            mib=LARGE,
+        )
+
+    def weights_step(x, cut, at, before):
+        start, w = cut
+        tile = tile_of(math.gcd(math.gcd(start, at), w), 1024)
+        places = [at // tile if piece.shape[2] > w else 0 for piece in x]
         return chain.call(
             weight_grads,
             (w // tile,),
-            (inputs, *pieces(groups[g]), *before),
-            [whole(depth, tokens)] + [pl.BlockSpec((2, rows, tile), lambda j: (0, 0, j))] * 6 + [ANY] * len(before),
+            (inputs, *x, *before),
+            [whole(depth, tokens)]
+            + [pl.BlockSpec((2, rows, tile), lambda j, p=p: (0, 0, p + j)) for p in places]
+            + [ANY] * len(before),
             [shape((depth, ff), BF)] * 2,
             [cols(depth, tile, start)] * 2,
-            aliases=[(7, 0), (8, 1)] if before else (), mib=LARGE)
+            aliases=[(7, 0), (8, 1)] if before else (),
+            mib=LARGE,
+        )
 
     def down_step():
         tile = tile_of(ff, 1024)
@@ -382,7 +412,7 @@
     n = len(cuts)
     parts, firsts, seconds, thirds = ([None] * n for _ in range(4))
     out_grads = tok_swaps(out_grad)
-    h = spread(Chain(jnp.zeros((8, 128), F32)).call(*hidden_args(), mib=MEDIUM)[0])
+    h = spread(Chain(jnp.zeros((8, 128), F32)).call(*hidden_args(), mib=WHOLE)[0])
     out_grads = tok_last(*out_grads)
     grads, parts[0], firsts[0] = partial(0)
     _, parts[1], firsts[1] = partial(1)
@@ -416,10 +446,24 @@
     spread_far(groups[1])
     (groups[0]["far_end"],) = chain.relay(groups[0]["far_end"])
     total = input_step(0, None, ALL)
-    weights = weights_step(0, ())
-    spread_end(groups[1])
+    weights = weights_step(pieces(groups[0]), cuts[0], 0, ())
+    second = ff - first
+    part = second // 2
+    low_cut, high_cut = (first, part), (first + part, part)
+    low, high = chain.call(
+        halves,
+        (1,),
+        (groups[1]["far"],),
+        [whole(2, rows, second)],
+        [shape((2, rows, part), BF)] * 2,
+        [whole(2, rows, part)] * 2,
+    )
+    low, high = (low, send(low, OUTWARD)), (high, send(high, OUTWARD))
+    early = [groups[1][k] for k in ALL[:4]]
     others = input_step(1, total, ALL[:4])
-    mine, other = input_last(1, total, others)
+    total = far_more(low, low_cut, total)
+    weights = weights_step([*early, *low], low_cut, 0, weights)
+    mine, other = far_last(high, high_cut, total, others)
     got = lax.ppermute(other, "tok", CORE_SWAP)
     keep, *others = chain.call(
         split_again,
@@ -435,7 +479,7 @@
         lax.ppermute(others[0], "out", Y_SWAP),
         lax.ppermute(others[1], "tok", X_SWAP),
     )
-    weights = weights_step(1, weights)
+    weights = weights_step([*early, *high], high_cut, part, weights)
     result = chain.call(
         add_last,
         (1,),

time: 235 us -> 232 us (0.987)
  waiting for transfers between devices: 125 us -> 121 us
  local copies, waits for them, and re-layouts: 7.07 us -> 4.67 us
    ppermute x21 -> x22, waiting for transfers between devices: 116 us -> 109 us  [send(): return lax.ppermute(x, 'inp', perm)]
    unnamed x24 -> x22, local copies, waits for them, and re-layouts: 7.07 us -> 4.07 us
    pallas_call x33 -> x35, Pallas kernels: 46.6 us -> 48.7 us  [call(): pl.pallas_call(kernel, grid_spec=pltpu.PrefetchScalarGridSpec(num_scalar_...]
    ppermute x21 -> x22, starting transfers between devices: 46.9 us -> 48.9 us  [send(): return lax.ppermute(x, 'inp', perm)]
  transfers between devices with their start and end apart: 31 -> 32, of which waited for: 18 -> 21; matrix products, arithmetic and copies ran while one was open for 0% -> 0% of each run, Pallas kernels for 17% -> 19%
where the time goes in v4:
time: 232 us
  waiting for transfers between devices  121 us (52%)
  starting transfers between devices  56.5 us (24%)
  Pallas kernels  48.7 us (21%)
  local copies, waits for them, and re-layouts  4.67 us (2%)
    ppermute x22, waiting for transfers between devices, send(): return lax.ppermute(x, 'inp', perm)  109 us
    ppermute x22, starting transfers between devices, send(): return lax.ppermute(x, 'inp', perm)  48.9 us
    pallas_call x35, Pallas kernels, call(): pl.pallas_call(kernel, grid_spec=pltpu.PrefetchScalarGridSpec(num_scalar_...  48.7 us
    ppermute x2, waiting for transfers between devices, tok_swaps(): lax.ppermute(x, 'tok', X_SWAP)  5.84 us
  transfers between devices with their start and end apart: 32, of which 21 were waited for; matrix products, arithmetic and copies ran while one was open for 0% of the time, Pallas kernels for 19%

profile of v4, /device:TPU:0, one launch (start us, length us, event | category | flops | bytes accessed | tf_op | source)
XLA Modules:
  0.0 231.7 jit_solution(10710890995656944911)
XLA Ops:
  7.9 4.4 %collective-permute-start.4 = (bf16[128,3584]{1,0:T(8,128)(2,1)}, bf16[128,3584]{1,0:T(8,128)(2,1)S(1)}, u32[]{:S(2)}, u32[]{:S(2)}) collective-permute-start(bf16[128,3584]{1,0:T(8,128)(2,1)} %get-tuple-element.90.refs_2_), channel_id=1, source_target_pairs={{0,8},{8,0},{16,24},{24,16},{1,9},{9,1},{17,25},{25,17},{2,10},{10... | collective-permute-start | bytes 2752520 | tf_op jit(solution)/shard_map/ppermute | solution.py:30
  18.2 3.6 %shard_map.103 = (f32[8,128]{1,0:T(8,128)S(1)}, f32[512,1792]{1,0:T(8,128)S(1)}, bf16[256,1792]{1,0:T(8,128)(2,1)S(1)}, bf16[512,1024]{1,0:T(8,128)(2,1)S(1)}) custom-call(s32[3]{0:T(128)S(1)} %pad_add_fusion.refs_0_, f32[8,128]{1,0:T(8,128)S(1)} %get-tuple-element.85.refs_1_, bf16[128,1024]{1,0:T(8,128)(2,1)S(1)} %copy-done.5, ...), custom_call_target="tpu_custom_call", output_to_operand_aliasing={{0}: (1, {})} | custom-call | tf_op jit(solution)/shard_map/pallas_call | solution.py:61
  26.8 6.6 %collective-permute-done.4.refs_1_ = bf16[128,3584]{1,0:T(8,128)(2,1)S(1)} collective-permute-done((bf16[128,3584]{1,0:T(8,128)(2,1)}, bf16[128,3584]{1,0:T(8,128)(2,1)S(1)}, u32[]{:S(2)}, u32[]{:S(2)}) %collective-permute-start.4) | collective-permute-done | bytes 917536 | tf_op jit(solution)/shard_map/ppermute | solution.py:30
  35.4 6.0 %collective-permute-start.9 = (bf16[256,1792]{1,0:T(8,128)(2,1)S(1)}, bf16[256,1792]{1,0:T(8,128)(2,1)S(1)}, u32[]{:S(2)}, u32[]{:S(2)}) collective-permute-start(bf16[256,1792]{1,0:T(8,128)(2,1)S(1)} %get-tuple-element.100), channel_id=1, source_target_pairs={{0,8},{24,16},{1,9},{25,17},{2,10},{26,18},{3,11},{27,19},{4,12},{... | collective-permute-start | bytes 2752520 | tf_op jit(solution)/shard_map/ppermute | solution.py:30
  41.5 11.5 %collective-permute-done.5.refs_1_ = bf16[256,1792]{1,0:T(8,128)(2,1)S(1)} collective-permute-done((bf16[256,1792]{1,0:T(8,128)(2,1)S(1)}, bf16[256,1792]{1,0:T(8,128)(2,1)S(1)}, u32[]{:S(2)}, u32[]{:S(2)}) %collective-permute-start.5) | collective-permute-done | bytes 917536 | tf_op jit(solution)/shard_map/ppermute | solution.py:30
  57.6 13.3 %collective-permute-done.9.refs_3_ = bf16[256,1792]{1,0:T(8,128)(2,1)S(1)} collective-permute-done((bf16[256,1792]{1,0:T(8,128)(2,1)S(1)}, bf16[256,1792]{1,0:T(8,128)(2,1)S(1)}, u32[]{:S(2)}, u32[]{:S(2)}) %collective-permute-start.9) | collective-permute-done | bytes 917536 | tf_op jit(solution)/shard_map/ppermute | solution.py:30
  71.1 6.0 %collective-permute-start.11 = (bf16[128,1792]{1,0:T(8,128)(2,1)S(1)}, bf16[128,1792]{1,0:T(8,128)(2,1)S(1)}, u32[]{:S(2)}, u32[]{:S(2)}) collective-permute-start(bf16[128,1792]{1,0:T(8,128)(2,1)S(1)} %get-tuple-element.105), channel_id=1, source_target_pairs={{0,8},{8,0},{16,24},{24,16},{1,9},{9,1},{17,25},{25,17},{2,10},{10... | collective-permute-start | bytes 1376264 | tf_op jit(solution)/shard_map/ppermute | solution.py:30
  79.4 7.0 %collective-permute-done.11.refs_3_ = bf16[128,1792]{1,0:T(8,128)(2,1)S(1)} collective-permute-done((bf16[128,1792]{1,0:T(8,128)(2,1)S(1)}, bf16[128,1792]{1,0:T(8,128)(2,1)S(1)}, u32[]{:S(2)}, u32[]{:S(2)}) %collective-permute-start.11) | collective-permute-done | bytes 458784 | tf_op jit(solution)/shard_map/ppermute | solution.py:30
  88.1 6.4 %shard_map.113 = (f32[8,128]{1,0:T(8,128)S(1)}, bf16[3584,1024]{1,0:T(8,128)(2,1)}) custom-call(f32[8,128]{1,0:T(8,128)S(1)} %get-tuple-element.106.refs_0_, bf16[512,1024]{1,0:T(8,128)(2,1)S(1)} %get-tuple-element.88.refs_1_, bf16[128,3584]{1,0:T(8,128)(2,1)S(1)} %copy-done.4, ...), custom_call_target="tpu_custom_call", output_to_operand_aliasing={{0}: (0, {})} | custom-call | tf_op jit(solution)/shard_map/pallas_call | solution.py:61
  94.6 7.9 %collective-permute-start.14 = (bf16[128,1792]{1,0:T(8,128)(2,1)S(1)}, bf16[128,1792]{1,0:T(8,128)(2,1)S(1)}, u32[]{:S(2)}, u32[]{:S(2)}) collective-permute-start(bf16[128,1792]{1,0:T(8,128)(2,1)S(1)} %get-tuple-element.114), channel_id=1, source_target_pairs={{0,8},{8,0},{16,24},{24,16},{1,9},{9,1},{17,25},{25,17},{2,10},{10... | collective-permute-start | bytes 1376264 | tf_op jit(solution)/shard_map/ppermute | solution.py:30
  102.5 8.2 %collective-permute-done.13.refs_1_ = bf16[2,128,1792]{2,1,0:T(8,128)(2,1)S(1)} collective-permute-done((bf16[2,128,1792]{2,1,0:T(8,128)(2,1)S(1)}, bf16[2,128,1792]{2,1,0:T(8,128)(2,1)S(1)}, u32[]{:S(2)}, u32[]{:S(2)}) %collective-permute-start.13) | collective-permute-done | bytes 917536 | tf_op jit(solution)/shard_map/ppermute | solution.py:30
  111.4 5.4 %collective-permute-done.14.refs_1_ = bf16[128,1792]{1,0:T(8,128)(2,1)S(1)} collective-permute-done((bf16[128,1792]{1,0:T(8,128)(2,1)S(1)}, bf16[128,1792]{1,0:T(8,128)(2,1)S(1)}, u32[]{:S(2)}, u32[]{:S(2)}) %collective-permute-start.14) | collective-permute-done | bytes 458784 | tf_op jit(solution)/shard_map/ppermute | solution.py:30
  119.8 7.3 %collective-permute-start.22 = (bf16[2,128,1792]{2,1,0:T(8,128)(2,1)S(1)}, bf16[2,128,1792]{2,1,0:T(8,128)(2,1)S(1)}, u32[]{:S(2)}, u32[]{:S(2)}) collective-permute-start(bf16[2,128,1792]{2,1,0:T(8,128)(2,1)S(1)} %get-tuple-element.128.refs_1_.refs_2_), channel_id=1, source_target_pairs={{0,8},{8,0},{16,24},{24,16},{1,9},{9,1},{17,25},{25,17},{2,10},{10... | collective-permute-start | bytes 2752520 | tf_op jit(solution)/shard_map/ppermute | solution.py:30
  127.2 17.3 %collective-permute-done.17.refs_1_ = bf16[2,128,1792]{2,1,0:T(8,128)(2,1)S(1)} collective-permute-done((bf16[2,128,1792]{2,1,0:T(8,128)(2,1)S(1)}, bf16[2,128,1792]{2,1,0:T(8,128)(2,1)S(1)}, u32[]{:S(2)}, u32[]{:S(2)}) %collective-permute-start.17) | collective-permute-done | bytes 917536 | tf_op jit(solution)/shard_map/ppermute | solution.py:30
  145.1 5.8 %collective-permute-done.18.refs_1_ = bf16[128,1024]{1,0:T(8,128)(2,1)S(1)} collective-permute-done((bf16[128,1024]{1,0:T(8,128)(2,1)S(1)}, bf16[128,1024]{1,0:T(8,128)(2,1)S(1)}, u32[]{:S(2)}, u32[]{:S(2)}) %collective-permute-start.18) | collective-permute-done | bytes 262176 | tf_op jit(solution)/shard_map/ppermute | solution.py:234
  153.3 4.5 %collective-permute-done.22.refs_1_ = bf16[2,128,1792]{2,1,0:T(8,128)(2,1)S(1)} collective-permute-done((bf16[2,128,1792]{2,1,0:T(8,128)(2,1)S(1)}, bf16[2,128,1792]{2,1,0:T(8,128)(2,1)S(1)}, u32[]{:S(2)}, u32[]{:S(2)}) %collective-permute-start.22) | collective-permute-done | bytes 917536 | tf_op jit(solution)/shard_map/ppermute | solution.py:30
  160.0 17.5 %collective-permute-done.23.refs_1_ = bf16[2,128,1792]{2,1,0:T(8,128)(2,1)S(1)} collective-permute-done((bf16[2,128,1792]{2,1,0:T(8,128)(2,1)S(1)}, bf16[2,128,1792]{2,1,0:T(8,128)(2,1)S(1)}, u32[]{:S(2)}, u32[]{:S(2)}) %collective-permute-start.23) | collective-permute-done | bytes 917536 | tf_op jit(solution)/shard_map/ppermute | solution.py:30
  177.5 5.2 %shard_map.127 = (f32[8,128]{1,0:T(8,128)S(1)}, f32[512,1024]{1,0:T(8,128)S(1)}) custom-call(f32[8,128]{1,0:T(8,128)S(1)} %get-tuple-element.132.refs_0_, bf16[2,128,1792]{2,1,0:T(8,128)(2,1)S(1)} %get-tuple-element.112.refs_1_.refs_2_, bf16[2,128,1792]{2,1,0:T(8,128)(2,1)S(1)} %get-tuple-element.119.refs_2_.refs_3_, ...), custom_call_target="tpu_custom_call", output_to_operand_aliasing={{0}: (0, {})} | custom-call | tf_op jit(solution)/shard_map/pallas_call | solution.py:61
  182.7 6.6 %shard_map.128 = (f32[8,128]{1,0:T(8,128)S(1)}, bf16[1024,3584]{1,0:T(8,128)(2,1)}, bf16[1024,3584]{1,0:T(8,128)(2,1)}) custom-call(f32[8,128]{1,0:T(8,128)S(1)} %get-tuple-element.135.refs_0_, bf16[1024,512]{1,0:T(8,128)(2,1)S(1)} %get-tuple-element.136.refs_1_, ...), custom_call_target="tpu_custom_call", output_to_operand_aliasing={{0}: (0, {})} | custom-call | tf_op jit(solution)/shard_map/pallas_call | solution.py:61
  191.9 5.2 %collective-permute-done.25.refs_4_.refs_5_ = bf16[2,128,1792]{2,1,0:T(8,128)(2,1)S(1)} collective-permute-done((bf16[2,128,1792]{2,1,0:T(8,128)(2,1)S(1)}, bf16[2,128,1792]{2,1,0:T(8,128)(2,1)S(1)}, u32[]{:S(2)}, u32[]{:S(2)}) %collective-permute-start.25) | collective-permute-done | bytes 917536 | tf_op jit(solution)/shard_map/ppermute | solution.py:30
  197.1 4.2 %shard_map.130 = (f32[8,128]{1,0:T(8,128)S(1)}, f32[384,1024]{1,0:T(8,128)S(1)}) custom-call(f32[8,128]{1,0:T(8,128)S(1)} %get-tuple-element.139.refs_0_, bf16[2,128,1792]{2,1,0:T(8,128)(2,1)S(1)} %get-tuple-element.128.refs_1_.refs_2_, bf16[2,128,1792]{2,1,0:T(8,128)(2,1)S(1)} %get-tuple-element.138.refs_2_.refs_3_, ...), custom_call_target="tpu_custom_call", output_to_operand_aliasing={{0}: (0, {})} | custom-call | tf_op jit(solution)/shard_map/pallas_call | solution.py:61
  201.3 5.6 %collective-permute-done.26.refs_2_.refs_7_ = bf16[2,128,896]{2,1,0:T(8,128)(2,1)S(1)} collective-permute-done((bf16[2,128,896]{2,1,0:T(8,128)(2,1)S(1)}, bf16[2,128,896]{2,1,0:T(8,128)(2,1)S(1)}, u32[]{:S(2)}, u32[]{:S(2)}) %collective-permute-start.26) | collective-permute-done | bytes 458784 | tf_op jit(solution)/shard_map/ppermute | solution.py:30
  208.9 3.6 %shard_map.132 = (f32[8,128]{1,0:T(8,128)S(1)}, bf16[1024,3584]{1,0:T(8,128)(2,1)}, bf16[1024,3584]{1,0:T(8,128)(2,1)}) custom-call(f32[8,128]{1,0:T(8,128)S(1)} %get-tuple-element.144.refs_0_, bf16[1024,512]{1,0:T(8,128)(2,1)S(1)} %get-tuple-element.136.refs_1_, ...), custom_call_target="tpu_custom_call", output_to_operand_aliasing={{0}: (0, {}), {1}: (8, {}), {2}: (9, {})} | custom-call | tf_op jit(solution)/shard_map/pallas_call | solution.py:61
  225.0 3.6 %shard_map.135 = (f32[8,128]{1,0:T(8,128)S(1)}, bf16[1024,3584]{1,0:T(8,128)(2,1)}, bf16[1024,3584]{1,0:T(8,128)(2,1)}) custom-call(f32[8,128]{1,0:T(8,128)S(1)} %get-tuple-element.154.refs_0_, bf16[1024,512]{1,0:T(8,128)(2,1)S(1)} %get-tuple-element.136.refs_1_, ...), custom_call_target="tpu_custom_call", output_to_operand_aliasing={{0}: (0, {}), {1}: (8, {}), {2}: (9, {})} | custom-call | tf_op jit(solution)/shard_map/pallas_call | solution.py:61
  (103 shorter events, 58.1 us)
Async XLA Ops:
  0.6 11.7 %collective-permute-start = (bf16[128,1024]{1,0:T(8,128)(2,1)}, bf16[128,1024]{1,0:T(8,128)(2,1)S(1)}, u32[]{:S(2)}, u32[]{:S(2)}) collective-permute-start(bf16[128,1024]{1,0:T(8,128)(2,1)} %refs_2_.3), channel_id=1, source_target_pairs={{0,2},{2,0},{1,3},{3,1},{4,6},{6,4},{5,7},{7,5},{8,10},{10,8},{9,1... | collective-permute-start | bytes 786440 | tf_op jit(solution)/shard_map/ppermute | solution.py:234
  7.2 19.6 %collective-permute-start.3 = (bf16[128,3584]{1,0:T(8,128)(2,1)}, bf16[128,3584]{1,0:T(8,128)(2,1)S(1)}, u32[]{:S(2)}, u32[]{:S(2)}) collective-permute-start(bf16[128,3584]{1,0:T(8,128)(2,1)} %get-tuple-element.90.refs_2_), channel_id=1, source_target_pairs={{8,16},{16,8},{9,17},{17,9},{10,18},{18,10},{11,19},{19,11},{12,20... | collective-permute-start | bytes 2752520 | tf_op jit(solution)/shard_map/ppermute | solution.py:30
  7.9 25.5 %collective-permute-start.4 = (bf16[128,3584]{1,0:T(8,128)(2,1)}, bf16[128,3584]{1,0:T(8,128)(2,1)S(1)}, u32[]{:S(2)}, u32[]{:S(2)}) collective-permute-start(bf16[128,3584]{1,0:T(8,128)(2,1)} %get-tuple-element.90.refs_2_), channel_id=1, source_target_pairs={{0,8},{8,0},{16,24},{24,16},{1,9},{9,1},{17,25},{25,17},{2,10},{10... | collective-permute-start | bytes 2752520 | tf_op jit(solution)/shard_map/ppermute | solution.py:30
  21.8 31.2 %collective-permute-start.5 = (bf16[256,1792]{1,0:T(8,128)(2,1)S(1)}, bf16[256,1792]{1,0:T(8,128)(2,1)S(1)}, u32[]{:S(2)}, u32[]{:S(2)}) collective-permute-start(bf16[256,1792]{1,0:T(8,128)(2,1)S(1)} %get-tuple-element.93), channel_id=1, source_target_pairs={{0,8},{24,16},{1,9},{25,17},{2,10},{26,18},{3,11},{27,19},{4,12},{... | collective-permute-start | bytes 2752520 | tf_op jit(solution)/shard_map/ppermute | solution.py:30
  33.4 20.9 %collective-permute-start.6 = (bf16[128,3584]{1,0:T(8,128)(2,1)S(1)}, bf16[128,3584]{1,0:T(8,128)(2,1)S(1)}, u32[]{:S(2)}, u32[]{:S(2)}) collective-permute-start(bf16[128,3584]{1,0:T(8,128)(2,1)S(1)} %get-tuple-element.96.refs_3_), channel_id=1, source_target_pairs={{8,16},{16,8},{9,17},{17,9},{10,18},{18,10},{11,19},{19,11},{12,20... | collective-permute-start | bytes 2752520 | tf_op jit(solution)/shard_map/ppermute | solution.py:30
  34.1 22.2 %collective-permute-start.7 = (bf16[128,3584]{1,0:T(8,128)(2,1)S(1)}, bf16[128,3584]{1,0:T(8,128)(2,1)S(1)}, u32[]{:S(2)}, u32[]{:S(2)}) collective-permute-start(bf16[128,3584]{1,0:T(8,128)(2,1)S(1)} %get-tuple-element.97.refs_4_), channel_id=1, source_target_pairs={{8,0},{16,24},{9,1},{17,25},{10,2},{18,26},{11,3},{19,27},{12,4},{... | collective-permute-start | bytes 2752520 | tf_op jit(solution)/shard_map/ppermute | solution.py:30
  35.4 35.4 %collective-permute-start.9 = (bf16[256,1792]{1,0:T(8,128)(2,1)S(1)}, bf16[256,1792]{1,0:T(8,128)(2,1)S(1)}, u32[]{:S(2)}, u32[]{:S(2)}) collective-permute-start(bf16[256,1792]{1,0:T(8,128)(2,1)S(1)} %get-tuple-element.100), channel_id=1, source_target_pairs={{0,8},{24,16},{1,9},{25,17},{2,10},{26,18},{3,11},{27,19},{4,12},{... | collective-permute-start | bytes 2752520 | tf_op jit(solution)/shard_map/ppermute | solution.py:30
  53.5 17.4 %collective-permute-start.8 = (bf16[256,1792]{1,0:T(8,128)(2,1)S(1)}, bf16[256,1792]{1,0:T(8,128)(2,1)S(1)}, u32[]{:S(2)}, u32[]{:S(2)}) collective-permute-start(bf16[256,1792]{1,0:T(8,128)(2,1)S(1)} %get-tuple-element.99), channel_id=1, source_target_pairs={{8,16},{16,8},{9,17},{17,9},{10,18},{18,10},{11,19},{19,11},{12,20... | collective-permute-start | bytes 2752520 | tf_op jit(solution)/shard_map/ppermute | solution.py:30
  56.3 23.1 %collective-permute-start.10 = (bf16[128,3584]{1,0:T(8,128)(2,1)S(1)}, bf16[128,3584]{1,0:T(8,128)(2,1)S(1)}, u32[]{:S(2)}, u32[]{:S(2)}) collective-permute-start(bf16[128,3584]{1,0:T(8,128)(2,1)S(1)} %get-tuple-element.103.refs_6_), channel_id=1, source_target_pairs={{8,0},{16,24},{9,1},{17,25},{10,2},{18,26},{11,3},{19,27},{12,4},{... | collective-permute-start | bytes 2752520 | tf_op jit(solution)/shard_map/ppermute | solution.py:30
  71.1 15.2 %collective-permute-start.11 = (bf16[128,1792]{1,0:T(8,128)(2,1)S(1)}, bf16[128,1792]{1,0:T(8,128)(2,1)S(1)}, u32[]{:S(2)}, u32[]{:S(2)}) collective-permute-start(bf16[128,1792]{1,0:T(8,128)(2,1)S(1)} %get-tuple-element.105), channel_id=1, source_target_pairs={{0,8},{8,0},{16,24},{24,16},{1,9},{9,1},{17,25},{25,17},{2,10},{10... | collective-permute-start | bytes 1376264 | tf_op jit(solution)/shard_map/ppermute | solution.py:30
  77.1 17.4 %collective-permute-start.12 = (bf16[256,1792]{1,0:T(8,128)(2,1)S(1)}, bf16[256,1792]{1,0:T(8,128)(2,1)S(1)}, u32[]{:S(2)}, u32[]{:S(2)}) collective-permute-start(bf16[256,1792]{1,0:T(8,128)(2,1)S(1)} %get-tuple-element.110), channel_id=1, source_target_pairs={{8,16},{16,8},{9,17},{17,9},{10,18},{18,10},{11,19},{19,11},{12,20... | collective-permute-start | bytes 2752520 | tf_op jit(solution)/shard_map/ppermute | solution.py:30
  87.3 23.4 %collective-permute-start.13 = (bf16[2,128,1792]{2,1,0:T(8,128)(2,1)S(1)}, bf16[2,128,1792]{2,1,0:T(8,128)(2,1)S(1)}, u32[]{:S(2)}, u32[]{:S(2)}) collective-permute-start(bf16[2,128,1792]{2,1,0:T(8,128)(2,1)S(1)} %get-tuple-element.112.refs_1_.refs_2_), channel_id=1, source_target_pairs={{0,8},{8,0},{16,24},{24,16},{1,9},{9,1},{17,25},{25,17},{2,10},{10... | collective-permute-start | bytes 2752520 | tf_op jit(solution)/shard_map/ppermute | solution.py:30
  87.4 29.4 %collective-permute-start.15 = (bf16[2,128,1792]{2,1,0:T(8,128)(2,1)S(1)}, bf16[2,128,1792]{2,1,0:T(8,128)(2,1)S(1)}, u32[]{:S(2)}, u32[]{:S(2)}) collective-permute-start(bf16[2,128,1792]{2,1,0:T(8,128)(2,1)S(1)} %get-tuple-element.112.refs_1_.refs_2_), channel_id=1, source_target_pairs={{8,16},{16,8},{9,17},{17,9},{10,18},{18,10},{11,19},{19,11},{12,20... | collective-permute-start | bytes 2752520 | tf_op jit(solution)/shard_map/ppermute | solution.py:30
  94.6 22.1 %collective-permute-start.14 = (bf16[128,1792]{1,0:T(8,128)(2,1)S(1)}, bf16[128,1792]{1,0:T(8,128)(2,1)S(1)}, u32[]{:S(2)}, u32[]{:S(2)}) collective-permute-start(bf16[128,1792]{1,0:T(8,128)(2,1)S(1)} %get-tuple-element.114), channel_id=1, source_target_pairs={{0,8},{8,0},{16,24},{24,16},{1,9},{9,1},{17,25},{25,17},{2,10},{10... | collective-permute-start | bytes 1376264 | tf_op jit(solution)/shard_map/ppermute | solution.py:30
  110.6 16.5 %collective-permute-start.16 = (bf16[2,128,1792]{2,1,0:T(8,128)(2,1)S(1)}, bf16[2,128,1792]{2,1,0:T(8,128)(2,1)S(1)}, u32[]{:S(2)}, u32[]{:S(2)}) collective-permute-start(bf16[2,128,1792]{2,1,0:T(8,128)(2,1)S(1)} %get-tuple-element.119.refs_2_.refs_3_), channel_id=1, source_target_pairs={{8,16},{16,8},{9,17},{17,9},{10,18},{18,10},{11,19},{19,11},{12,20... | collective-permute-start | bytes 2752520 | tf_op jit(solution)/shard_map/ppermute | solution.py:30
  116.7 27.8 %collective-permute-start.17 = (bf16[2,128,1792]{2,1,0:T(8,128)(2,1)S(1)}, bf16[2,128,1792]{2,1,0:T(8,128)(2,1)S(1)}, u32[]{:S(2)}, u32[]{:S(2)}) collective-permute-start(bf16[2,128,1792]{2,1,0:T(8,128)(2,1)S(1)} %get-tuple-element.121.refs_3_.refs_4_), channel_id=1, source_target_pairs={{8,0},{16,24},{9,1},{17,25},{10,2},{18,26},{11,3},{19,27},{12,4},{... | collective-permute-start | bytes 2752520 | tf_op jit(solution)/shard_map/ppermute | solution.py:30
  119.0 34.3 %collective-permute-start.21 = (bf16[2,128,1792]{2,1,0:T(8,128)(2,1)S(1)}, bf16[2,128,1792]{2,1,0:T(8,128)(2,1)S(1)}, u32[]{:S(2)}, u32[]{:S(2)}) collective-permute-start(bf16[2,128,1792]{2,1,0:T(8,128)(2,1)S(1)} %get-tuple-element.128.refs_1_.refs_2_), channel_id=1, source_target_pairs={{8,16},{16,8},{9,17},{17,9},{10,18},{18,10},{11,19},{19,11},{12,20... | collective-permute-start | bytes 2752520 | tf_op jit(solution)/shard_map/ppermute | solution.py:30
  119.8 38.0 %collective-permute-start.22 = (bf16[2,128,1792]{2,1,0:T(8,128)(2,1)S(1)}, bf16[2,128,1792]{2,1,0:T(8,128)(2,1)S(1)}, u32[]{:S(2)}, u32[]{:S(2)}) collective-permute-start(bf16[2,128,1792]{2,1,0:T(8,128)(2,1)S(1)} %get-tuple-element.128.refs_1_.refs_2_), channel_id=1, source_target_pairs={{0,8},{8,0},{16,24},{24,16},{1,9},{9,1},{17,25},{25,17},{2,10},{10... | collective-permute-start | bytes 2752520 | tf_op jit(solution)/shard_map/ppermute | solution.py:30
  150.9 26.6 %collective-permute-start.23 = (bf16[2,128,1792]{2,1,0:T(8,128)(2,1)S(1)}, bf16[2,128,1792]{2,1,0:T(8,128)(2,1)S(1)}, u32[]{:S(2)}, u32[]{:S(2)}) collective-permute-start(bf16[2,128,1792]{2,1,0:T(8,128)(2,1)S(1)} %get-tuple-element.131.refs_5_.refs_6_), channel_id=1, source_target_pairs={{8,0},{16,24},{9,1},{17,25},{10,2},{18,26},{11,3},{19,27},{12,4},{... | collective-permute-start | bytes 2752520 | tf_op jit(solution)/shard_map/ppermute | solution.py:30
  157.8 31.4 %collective-permute-start.24 = (bf16[2,128,1792]{2,1,0:T(8,128)(2,1)S(1)}, bf16[2,128,1792]{2,1,0:T(8,128)(2,1)S(1)}, u32[]{:S(2)}, u32[]{:S(2)}) collective-permute-start(bf16[2,128,1792]{2,1,0:T(8,128)(2,1)S(1)} %get-tuple-element.138.refs_2_.refs_3_), channel_id=1, source_target_pairs={{8,16},{16,8},{9,17},{17,9},{10,18},{18,10},{11,19},{19,11},{12,20... | collective-permute-start | bytes 2752520 | tf_op jit(solution)/shard_map/ppermute | solution.py:30
  158.5 38.6 %collective-permute-start.25 = (bf16[2,128,1792]{2,1,0:T(8,128)(2,1)S(1)}, bf16[2,128,1792]{2,1,0:T(8,128)(2,1)S(1)}, u32[]{:S(2)}, u32[]{:S(2)}) collective-permute-start(bf16[2,128,1792]{2,1,0:T(8,128)(2,1)S(1)} %get-tuple-element.140.refs_3_.refs_4_), channel_id=1, source_target_pairs={{8,0},{16,24},{9,1},{17,25},{10,2},{18,26},{11,3},{19,27},{12,4},{... | collective-permute-start | bytes 2752520 | tf_op jit(solution)/shard_map/ppermute | solution.py:30
  189.3 17.6 %collective-permute-start.26 = (bf16[2,128,896]{2,1,0:T(8,128)(2,1)S(1)}, bf16[2,128,896]{2,1,0:T(8,128)(2,1)S(1)}, u32[]{:S(2)}, u32[]{:S(2)}) collective-permute-start(bf16[2,128,896]{2,1,0:T(8,128)(2,1)S(1)} %get-tuple-element.143.refs_1_.refs_6_), channel_id=1, source_target_pairs={{8,0},{16,24},{9,1},{17,25},{10,2},{18,26},{11,3},{19,27},{12,4},{... | collective-permute-start | bytes 1376264 | tf_op jit(solution)/shard_map/ppermute | solution.py:30
  190.6 25.3 %collective-permute-start.27 = (bf16[2,128,896]{2,1,0:T(8,128)(2,1)S(1)}, bf16[2,128,896]{2,1,0:T(8,128)(2,1)S(1)}, u32[]{:S(2)}, u32[]{:S(2)}) collective-permute-start(bf16[2,128,896]{2,1,0:T(8,128)(2,1)S(1)} %get-tuple-element.148.refs_2_.refs_6_), channel_id=1, source_target_pairs={{8,0},{16,24},{9,1},{17,25},{10,2},{18,26},{11,3},{19,27},{12,4},{... | collective-permute-start | bytes 1376264 | tf_op jit(solution)/shard_map/ppermute | solution.py:30
  223.5 7.5 %collective-permute-start.31 = (bf16[64,1024]{1,0:T(8,128)(2,1)S(1)}, bf16[64,1024]{1,0:T(8,128)(2,1)S(1)}, u32[]{:S(2)}, u32[]{:S(2)}) collective-permute-start(bf16[64,1024]{1,0:T(8,128)(2,1)S(1)} %get-tuple-element.161), channel_id=1, source_target_pairs={{0,6},{1,7},{2,4},{3,5},{4,2},{5,3},{6,0},{7,1},{8,14},{9,15},{10,... | collective-permute-start | bytes 393224 | tf_op jit(solution)/shard_map/ppermute | solution.py:478
  (19 other events, 421.8 us)

commit v5 on v4

--- a/solution.py
+++ b/solution.py
@@ -30,7 +30,7 @@
     return lax.ppermute(x, "inp", perm)
 
 
-LAST_TILE = 512
+LAST_TILE = 1024
 FIRST = 7
 ALL = ("own", "pair", "near", "near_end", "far", "far_end")
 
@@ -337,7 +337,7 @@
 
     def input_step(g, before, names):
         start, w = group_cuts[g]
-        tile = tile_of(depth, 512)
+        tile = tile_of(depth, 1024)
         wide = pl.BlockSpec((pl.Element(tile), pl.Element(w)), lambda j: (j * tile, start))
         count = len(names)
         height = rows * len([k for k in names if not k.endswith("_end")])
@@ -415,9 +415,9 @@
     h = spread(Chain(jnp.zeros((8, 128), F32)).call(*hidden_args(), mib=WHOLE)[0])
     out_grads = tok_last(*out_grads)
     grads, parts[0], firsts[0] = partial(0)
-    _, parts[1], firsts[1] = partial(1)
     spread_near(h)
     spread_far(h)
+    _, parts[1], firsts[1] = partial(1)
     pass_on(0)
     (h["near_end"],) = spread_end(h, h["near_end"])
     hand_out(0)

time: 232 us -> 231 us (level)
  Pallas kernels: 48.7 us -> 45 us
  waiting for transfers between devices: 121 us -> 124 us
    pallas_call x35, Pallas kernels: 48.7 us -> 45 us  [call(): pl.pallas_call(kernel, grid_spec=pltpu.PrefetchScalarGridSpec(num_scalar_...]
    ppermute x22, waiting for transfers between devices: 109 us -> 112 us  [send(): return lax.ppermute(x, 'inp', perm)]
  transfers between devices with their start and end apart: 32 -> 32, of which waited for: 21 -> 21; matrix products, arithmetic and copies ran while one was open for 0% -> 0% of each run, Pallas kernels for 19% -> 18%
where the time goes in v5:
time: 231 us
  waiting for transfers between devices  124 us (54%)
  starting transfers between devices  56.5 us (24%)
  Pallas kernels  45 us (19%)
  local copies, waits for them, and re-layouts  4.67 us (2%)
    ppermute x22, waiting for transfers between devices, send(): return lax.ppermute(x, 'inp', perm)  112 us
    ppermute x22, starting transfers between devices, send(): return lax.ppermute(x, 'inp', perm)  48.9 us
    pallas_call x35, Pallas kernels, call(): pl.pallas_call(kernel, grid_spec=pltpu.PrefetchScalarGridSpec(num_scalar_...  45 us
    ppermute x2, waiting for transfers between devices, tok_swaps(): lax.ppermute(x, 'tok', X_SWAP)  5.84 us
  transfers between devices with their start and end apart: 32, of which 21 were waited for; matrix products, arithmetic and copies ran while one was open for 0% of the time, Pallas kernels for 18%

profile of v5, /device:TPU:0, one launch (start us, length us, event | category | flops | bytes accessed | tf_op | source)
XLA Modules:
  0.0 230.9 jit_solution(543541301643957797)
XLA Ops:
  7.9 4.4 %collective-permute-start.4 = (bf16[128,3584]{1,0:T(8,128)(2,1)}, bf16[128,3584]{1,0:T(8,128)(2,1)S(1)}, u32[]{:S(2)}, u32[]{:S(2)}) collective-permute-start(bf16[128,3584]{1,0:T(8,128)(2,1)} %get-tuple-element.88.refs_2_), channel_id=1, source_target_pairs={{0,8},{8,0},{16,24},{24,16},{1,9},{9,1},{17,25},{25,17},{2,10},{10... | collective-permute-start | bytes 2752520 | tf_op jit(solution)/shard_map/ppermute | solution.py:30
  18.2 3.6 %shard_map.103 = (f32[8,128]{1,0:T(8,128)S(1)}, f32[512,1792]{1,0:T(8,128)S(1)}, bf16[256,1792]{1,0:T(8,128)(2,1)S(1)}, bf16[512,1024]{1,0:T(8,128)(2,1)S(1)}) custom-call(s32[3]{0:T(128)S(1)} %pad_add_fusion.refs_0_, f32[8,128]{1,0:T(8,128)S(1)} %get-tuple-element.85.refs_1_, bf16[128,1024]{1,0:T(8,128)(2,1)S(1)} %copy-done.5, ...), custom_call_target="tpu_custom_call", output_to_operand_aliasing={{0}: (1, {})} | custom-call | tf_op jit(solution)/shard_map/pallas_call | solution.py:61
  23.9 9.5 %collective-permute-done.4.refs_1_ = bf16[128,3584]{1,0:T(8,128)(2,1)S(1)} collective-permute-done((bf16[128,3584]{1,0:T(8,128)(2,1)}, bf16[128,3584]{1,0:T(8,128)(2,1)S(1)}, u32[]{:S(2)}, u32[]{:S(2)}) %collective-permute-start.4) | collective-permute-done | bytes 917536 | tf_op jit(solution)/shard_map/ppermute | solution.py:30
  38.4 6.0 %collective-permute-start.9 = (bf16[256,1792]{1,0:T(8,128)(2,1)S(1)}, bf16[256,1792]{1,0:T(8,128)(2,1)S(1)}, u32[]{:S(2)}, u32[]{:S(2)}) collective-permute-start(bf16[256,1792]{1,0:T(8,128)(2,1)S(1)} %get-tuple-element.100), channel_id=1, source_target_pairs={{0,8},{24,16},{1,9},{25,17},{2,10},{26,18},{3,11},{27,19},{4,12},{... | collective-permute-start | bytes 2752520 | tf_op jit(solution)/shard_map/ppermute | solution.py:30
  44.4 8.6 %collective-permute-done.5.refs_1_ = bf16[256,1792]{1,0:T(8,128)(2,1)S(1)} collective-permute-done((bf16[256,1792]{1,0:T(8,128)(2,1)S(1)}, bf16[256,1792]{1,0:T(8,128)(2,1)S(1)}, u32[]{:S(2)}, u32[]{:S(2)}) %collective-permute-start.5) | collective-permute-done | bytes 917536 | tf_op jit(solution)/shard_map/ppermute | solution.py:30
  57.6 13.3 %collective-permute-done.9.refs_3_ = bf16[256,1792]{1,0:T(8,128)(2,1)S(1)} collective-permute-done((bf16[256,1792]{1,0:T(8,128)(2,1)S(1)}, bf16[256,1792]{1,0:T(8,128)(2,1)S(1)}, u32[]{:S(2)}, u32[]{:S(2)}) %collective-permute-start.9) | collective-permute-done | bytes 917536 | tf_op jit(solution)/shard_map/ppermute | solution.py:30
  71.1 6.0 %collective-permute-start.11 = (bf16[128,1792]{1,0:T(8,128)(2,1)S(1)}, bf16[128,1792]{1,0:T(8,128)(2,1)S(1)}, u32[]{:S(2)}, u32[]{:S(2)}) collective-permute-start(bf16[128,1792]{1,0:T(8,128)(2,1)S(1)} %get-tuple-element.105), channel_id=1, source_target_pairs={{0,8},{8,0},{16,24},{24,16},{1,9},{9,1},{17,25},{25,17},{2,10},{10... | collective-permute-start | bytes 1376264 | tf_op jit(solution)/shard_map/ppermute | solution.py:30
  79.4 7.0 %collective-permute-done.11.refs_3_ = bf16[128,1792]{1,0:T(8,128)(2,1)S(1)} collective-permute-done((bf16[128,1792]{1,0:T(8,128)(2,1)S(1)}, bf16[128,1792]{1,0:T(8,128)(2,1)S(1)}, u32[]{:S(2)}, u32[]{:S(2)}) %collective-permute-start.11) | collective-permute-done | bytes 458784 | tf_op jit(solution)/shard_map/ppermute | solution.py:30
  88.1 6.4 %shard_map.113 = (f32[8,128]{1,0:T(8,128)S(1)}, bf16[3584,1024]{1,0:T(8,128)(2,1)}) custom-call(f32[8,128]{1,0:T(8,128)S(1)} %get-tuple-element.106.refs_0_, bf16[512,1024]{1,0:T(8,128)(2,1)S(1)} %get-tuple-element.91.refs_1_, bf16[128,3584]{1,0:T(8,128)(2,1)S(1)} %copy-done.4, ...), custom_call_target="tpu_custom_call", output_to_operand_aliasing={{0}: (0, {})} | custom-call | tf_op jit(solution)/shard_map/pallas_call | solution.py:61
  94.6 7.9 %collective-permute-start.14 = (bf16[128,1792]{1,0:T(8,128)(2,1)S(1)}, bf16[128,1792]{1,0:T(8,128)(2,1)S(1)}, u32[]{:S(2)}, u32[]{:S(2)}) collective-permute-start(bf16[128,1792]{1,0:T(8,128)(2,1)S(1)} %get-tuple-element.114), channel_id=1, source_target_pairs={{0,8},{8,0},{16,24},{24,16},{1,9},{9,1},{17,25},{25,17},{2,10},{10... | collective-permute-start | bytes 1376264 | tf_op jit(solution)/shard_map/ppermute | solution.py:30
  102.5 8.2 %collective-permute-done.13.refs_1_ = bf16[2,128,1792]{2,1,0:T(8,128)(2,1)S(1)} collective-permute-done((bf16[2,128,1792]{2,1,0:T(8,128)(2,1)S(1)}, bf16[2,128,1792]{2,1,0:T(8,128)(2,1)S(1)}, u32[]{:S(2)}, u32[]{:S(2)}) %collective-permute-start.13) | collective-permute-done | bytes 917536 | tf_op jit(solution)/shard_map/ppermute | solution.py:30
  111.4 5.4 %collective-permute-done.14.refs_1_ = bf16[128,1792]{1,0:T(8,128)(2,1)S(1)} collective-permute-done((bf16[128,1792]{1,0:T(8,128)(2,1)S(1)}, bf16[128,1792]{1,0:T(8,128)(2,1)S(1)}, u32[]{:S(2)}, u32[]{:S(2)}) %collective-permute-start.14) | collective-permute-done | bytes 458784 | tf_op jit(solution)/shard_map/ppermute | solution.py:30
  119.8 7.3 %collective-permute-start.22 = (bf16[2,128,1792]{2,1,0:T(8,128)(2,1)S(1)}, bf16[2,128,1792]{2,1,0:T(8,128)(2,1)S(1)}, u32[]{:S(2)}, u32[]{:S(2)}) collective-permute-start(bf16[2,128,1792]{2,1,0:T(8,128)(2,1)S(1)} %get-tuple-element.128.refs_1_.refs_2_), channel_id=1, source_target_pairs={{0,8},{8,0},{16,24},{24,16},{1,9},{9,1},{17,25},{25,17},{2,10},{10... | collective-permute-start | bytes 2752520 | tf_op jit(solution)/shard_map/ppermute | solution.py:30
  127.2 17.3 %collective-permute-done.17.refs_1_ = bf16[2,128,1792]{2,1,0:T(8,128)(2,1)S(1)} collective-permute-done((bf16[2,128,1792]{2,1,0:T(8,128)(2,1)S(1)}, bf16[2,128,1792]{2,1,0:T(8,128)(2,1)S(1)}, u32[]{:S(2)}, u32[]{:S(2)}) %collective-permute-start.17) | collective-permute-done | bytes 917536 | tf_op jit(solution)/shard_map/ppermute | solution.py:30
  145.1 5.8 %collective-permute-done.18.refs_1_ = bf16[128,1024]{1,0:T(8,128)(2,1)S(1)} collective-permute-done((bf16[128,1024]{1,0:T(8,128)(2,1)S(1)}, bf16[128,1024]{1,0:T(8,128)(2,1)S(1)}, u32[]{:S(2)}, u32[]{:S(2)}) %collective-permute-start.18) | collective-permute-done | bytes 262176 | tf_op jit(solution)/shard_map/ppermute | solution.py:234
  153.3 4.5 %collective-permute-done.22.refs_1_ = bf16[2,128,1792]{2,1,0:T(8,128)(2,1)S(1)} collective-permute-done((bf16[2,128,1792]{2,1,0:T(8,128)(2,1)S(1)}, bf16[2,128,1792]{2,1,0:T(8,128)(2,1)S(1)}, u32[]{:S(2)}, u32[]{:S(2)}) %collective-permute-start.22) | collective-permute-done | bytes 917536 | tf_op jit(solution)/shard_map/ppermute | solution.py:30
  160.0 17.5 %collective-permute-done.23.refs_1_ = bf16[2,128,1792]{2,1,0:T(8,128)(2,1)S(1)} collective-permute-done((bf16[2,128,1792]{2,1,0:T(8,128)(2,1)S(1)}, bf16[2,128,1792]{2,1,0:T(8,128)(2,1)S(1)}, u32[]{:S(2)}, u32[]{:S(2)}) %collective-permute-start.23) | collective-permute-done | bytes 917536 | tf_op jit(solution)/shard_map/ppermute | solution.py:30
  177.5 4.0 %shard_map.127 = (f32[8,128]{1,0:T(8,128)S(1)}, f32[512,1024]{1,0:T(8,128)S(1)}) custom-call(f32[8,128]{1,0:T(8,128)S(1)} %get-tuple-element.132.refs_0_, bf16[2,128,1792]{2,1,0:T(8,128)(2,1)S(1)} %get-tuple-element.112.refs_1_.refs_2_, bf16[2,128,1792]{2,1,0:T(8,128)(2,1)S(1)} %get-tuple-element.119.refs_2_.refs_3_, ...), custom_call_target="tpu_custom_call", output_to_operand_aliasing={{0}: (0, {})} | custom-call | tf_op jit(solution)/shard_map/pallas_call | solution.py:61
  181.5 6.6 %shard_map.128 = (f32[8,128]{1,0:T(8,128)S(1)}, bf16[1024,3584]{1,0:T(8,128)(2,1)}, bf16[1024,3584]{1,0:T(8,128)(2,1)}) custom-call(f32[8,128]{1,0:T(8,128)S(1)} %get-tuple-element.135.refs_0_, bf16[1024,512]{1,0:T(8,128)(2,1)S(1)} %get-tuple-element.136.refs_1_, ...), custom_call_target="tpu_custom_call", output_to_operand_aliasing={{0}: (0, {})} | custom-call | tf_op jit(solution)/shard_map/pallas_call | solution.py:61
  190.7 6.4 %collective-permute-done.25.refs_4_.refs_5_ = bf16[2,128,1792]{2,1,0:T(8,128)(2,1)S(1)} collective-permute-done((bf16[2,128,1792]{2,1,0:T(8,128)(2,1)S(1)}, bf16[2,128,1792]{2,1,0:T(8,128)(2,1)S(1)}, u32[]{:S(2)}, u32[]{:S(2)}) %collective-permute-start.25) | collective-permute-done | bytes 917536 | tf_op jit(solution)/shard_map/ppermute | solution.py:30
  200.2 6.8 %collective-permute-done.26.refs_2_.refs_7_ = bf16[2,128,896]{2,1,0:T(8,128)(2,1)S(1)} collective-permute-done((bf16[2,128,896]{2,1,0:T(8,128)(2,1)S(1)}, bf16[2,128,896]{2,1,0:T(8,128)(2,1)S(1)}, u32[]{:S(2)}, u32[]{:S(2)}) %collective-permute-start.26) | collective-permute-done | bytes 458784 | tf_op jit(solution)/shard_map/ppermute | solution.py:30
  208.3 3.6 %shard_map.132 = (f32[8,128]{1,0:T(8,128)S(1)}, bf16[1024,3584]{1,0:T(8,128)(2,1)}, bf16[1024,3584]{1,0:T(8,128)(2,1)}) custom-call(f32[8,128]{1,0:T(8,128)S(1)} %get-tuple-element.144.refs_0_, bf16[1024,512]{1,0:T(8,128)(2,1)S(1)} %get-tuple-element.136.refs_1_, ...), custom_call_target="tpu_custom_call", output_to_operand_aliasing={{0}: (0, {}), {1}: (8, {}), {2}: (9, {})} | custom-call | tf_op jit(solution)/shard_map/pallas_call | solution.py:61
  211.9 4.0 %collective-permute-done.27.refs_3_.refs_7_ = bf16[2,128,896]{2,1,0:T(8,128)(2,1)S(1)} collective-permute-done((bf16[2,128,896]{2,1,0:T(8,128)(2,1)S(1)}, bf16[2,128,896]{2,1,0:T(8,128)(2,1)S(1)}, u32[]{:S(2)}, u32[]{:S(2)}) %collective-permute-start.27) | collective-permute-done | bytes 458784 | tf_op jit(solution)/shard_map/ppermute | solution.py:30
  224.2 3.6 %shard_map.135 = (f32[8,128]{1,0:T(8,128)S(1)}, bf16[1024,3584]{1,0:T(8,128)(2,1)}, bf16[1024,3584]{1,0:T(8,128)(2,1)}) custom-call(f32[8,128]{1,0:T(8,128)S(1)} %get-tuple-element.154.refs_0_, bf16[1024,512]{1,0:T(8,128)(2,1)S(1)} %get-tuple-element.136.refs_1_, ...), custom_call_target="tpu_custom_call", output_to_operand_aliasing={{0}: (0, {}), {1}: (8, {}), {2}: (9, {})} | custom-call | tf_op jit(solution)/shard_map/pallas_call | solution.py:61
  (103 shorter events, 56.3 us)
Async XLA Ops:
  0.6 11.7 %collective-permute-start = (bf16[128,1024]{1,0:T(8,128)(2,1)}, bf16[128,1024]{1,0:T(8,128)(2,1)S(1)}, u32[]{:S(2)}, u32[]{:S(2)}) collective-permute-start(bf16[128,1024]{1,0:T(8,128)(2,1)} %refs_2_.3), channel_id=1, source_target_pairs={{0,2},{2,0},{1,3},{3,1},{4,6},{6,4},{5,7},{7,5},{8,10},{10,8},{9,1... | collective-permute-start | bytes 786440 | tf_op jit(solution)/shard_map/ppermute | solution.py:234
  7.2 16.7 %collective-permute-start.3 = (bf16[128,3584]{1,0:T(8,128)(2,1)}, bf16[128,3584]{1,0:T(8,128)(2,1)S(1)}, u32[]{:S(2)}, u32[]{:S(2)}) collective-permute-start(bf16[128,3584]{1,0:T(8,128)(2,1)} %get-tuple-element.88.refs_2_), channel_id=1, source_target_pairs={{8,16},{16,8},{9,17},{17,9},{10,18},{18,10},{11,19},{19,11},{12,20... | collective-permute-start | bytes 2752520 | tf_op jit(solution)/shard_map/ppermute | solution.py:30
  7.9 25.5 %collective-permute-start.4 = (bf16[128,3584]{1,0:T(8,128)(2,1)}, bf16[128,3584]{1,0:T(8,128)(2,1)S(1)}, u32[]{:S(2)}, u32[]{:S(2)}) collective-permute-start(bf16[128,3584]{1,0:T(8,128)(2,1)} %get-tuple-element.88.refs_2_), channel_id=1, source_target_pairs={{0,8},{8,0},{16,24},{24,16},{1,9},{9,1},{17,25},{25,17},{2,10},{10... | collective-permute-start | bytes 2752520 | tf_op jit(solution)/shard_map/ppermute | solution.py:30
  21.8 31.2 %collective-permute-start.5 = (bf16[256,1792]{1,0:T(8,128)(2,1)S(1)}, bf16[256,1792]{1,0:T(8,128)(2,1)S(1)}, u32[]{:S(2)}, u32[]{:S(2)}) collective-permute-start(bf16[256,1792]{1,0:T(8,128)(2,1)S(1)} %get-tuple-element.93), channel_id=1, source_target_pairs={{0,8},{24,16},{1,9},{25,17},{2,10},{26,18},{3,11},{27,19},{4,12},{... | collective-permute-start | bytes 2752520 | tf_op jit(solution)/shard_map/ppermute | solution.py:30
  33.4 20.9 %collective-permute-start.6 = (bf16[128,3584]{1,0:T(8,128)(2,1)S(1)}, bf16[128,3584]{1,0:T(8,128)(2,1)S(1)}, u32[]{:S(2)}, u32[]{:S(2)}) collective-permute-start(bf16[128,3584]{1,0:T(8,128)(2,1)S(1)} %get-tuple-element.96.refs_3_), channel_id=1, source_target_pairs={{8,16},{16,8},{9,17},{17,9},{10,18},{18,10},{11,19},{19,11},{12,20... | collective-permute-start | bytes 2752520 | tf_op jit(solution)/shard_map/ppermute | solution.py:30
  34.1 22.2 %collective-permute-start.7 = (bf16[128,3584]{1,0:T(8,128)(2,1)S(1)}, bf16[128,3584]{1,0:T(8,128)(2,1)S(1)}, u32[]{:S(2)}, u32[]{:S(2)}) collective-permute-start(bf16[128,3584]{1,0:T(8,128)(2,1)S(1)} %get-tuple-element.97.refs_4_), channel_id=1, source_target_pairs={{8,0},{16,24},{9,1},{17,25},{10,2},{18,26},{11,3},{19,27},{12,4},{... | collective-permute-start | bytes 2752520 | tf_op jit(solution)/shard_map/ppermute | solution.py:30
  38.4 32.5 %collective-permute-start.9 = (bf16[256,1792]{1,0:T(8,128)(2,1)S(1)}, bf16[256,1792]{1,0:T(8,128)(2,1)S(1)}, u32[]{:S(2)}, u32[]{:S(2)}) collective-permute-start(bf16[256,1792]{1,0:T(8,128)(2,1)S(1)} %get-tuple-element.100), channel_id=1, source_target_pairs={{0,8},{24,16},{1,9},{25,17},{2,10},{26,18},{3,11},{27,19},{4,12},{... | collective-permute-start | bytes 2752520 | tf_op jit(solution)/shard_map/ppermute | solution.py:30
  53.5 17.4 %collective-permute-start.8 = (bf16[256,1792]{1,0:T(8,128)(2,1)S(1)}, bf16[256,1792]{1,0:T(8,128)(2,1)S(1)}, u32[]{:S(2)}, u32[]{:S(2)}) collective-permute-start(bf16[256,1792]{1,0:T(8,128)(2,1)S(1)} %get-tuple-element.99), channel_id=1, source_target_pairs={{8,16},{16,8},{9,17},{17,9},{10,18},{18,10},{11,19},{19,11},{12,20... | collective-permute-start | bytes 2752520 | tf_op jit(solution)/shard_map/ppermute | solution.py:30
  56.3 23.1 %collective-permute-start.10 = (bf16[128,3584]{1,0:T(8,128)(2,1)S(1)}, bf16[128,3584]{1,0:T(8,128)(2,1)S(1)}, u32[]{:S(2)}, u32[]{:S(2)}) collective-permute-start(bf16[128,3584]{1,0:T(8,128)(2,1)S(1)} %get-tuple-element.103.refs_6_), channel_id=1, source_target_pairs={{8,0},{16,24},{9,1},{17,25},{10,2},{18,26},{11,3},{19,27},{12,4},{... | collective-permute-start | bytes 2752520 | tf_op jit(solution)/shard_map/ppermute | solution.py:30
  71.1 15.2 %collective-permute-start.11 = (bf16[128,1792]{1,0:T(8,128)(2,1)S(1)}, bf16[128,1792]{1,0:T(8,128)(2,1)S(1)}, u32[]{:S(2)}, u32[]{:S(2)}) collective-permute-start(bf16[128,1792]{1,0:T(8,128)(2,1)S(1)} %get-tuple-element.105), channel_id=1, source_target_pairs={{0,8},{8,0},{16,24},{24,16},{1,9},{9,1},{17,25},{25,17},{2,10},{10... | collective-permute-start | bytes 1376264 | tf_op jit(solution)/shard_map/ppermute | solution.py:30
  77.1 17.4 %collective-permute-start.12 = (bf16[256,1792]{1,0:T(8,128)(2,1)S(1)}, bf16[256,1792]{1,0:T(8,128)(2,1)S(1)}, u32[]{:S(2)}, u32[]{:S(2)}) collective-permute-start(bf16[256,1792]{1,0:T(8,128)(2,1)S(1)} %get-tuple-element.110), channel_id=1, source_target_pairs={{8,16},{16,8},{9,17},{17,9},{10,18},{18,10},{11,19},{19,11},{12,20... | collective-permute-start | bytes 2752520 | tf_op jit(solution)/shard_map/ppermute | solution.py:30
  87.3 23.4 %collective-permute-start.13 = (bf16[2,128,1792]{2,1,0:T(8,128)(2,1)S(1)}, bf16[2,128,1792]{2,1,0:T(8,128)(2,1)S(1)}, u32[]{:S(2)}, u32[]{:S(2)}) collective-permute-start(bf16[2,128,1792]{2,1,0:T(8,128)(2,1)S(1)} %get-tuple-element.112.refs_1_.refs_2_), channel_id=1, source_target_pairs={{0,8},{8,0},{16,24},{24,16},{1,9},{9,1},{17,25},{25,17},{2,10},{10... | collective-permute-start | bytes 2752520 | tf_op jit(solution)/shard_map/ppermute | solution.py:30
  87.4 29.4 %collective-permute-start.15 = (bf16[2,128,1792]{2,1,0:T(8,128)(2,1)S(1)}, bf16[2,128,1792]{2,1,0:T(8,128)(2,1)S(1)}, u32[]{:S(2)}, u32[]{:S(2)}) collective-permute-start(bf16[2,128,1792]{2,1,0:T(8,128)(2,1)S(1)} %get-tuple-element.112.refs_1_.refs_2_), channel_id=1, source_target_pairs={{8,16},{16,8},{9,17},{17,9},{10,18},{18,10},{11,19},{19,11},{12,20... | collective-permute-start | bytes 2752520 | tf_op jit(solution)/shard_map/ppermute | solution.py:30
  94.6 22.1 %collective-permute-start.14 = (bf16[128,1792]{1,0:T(8,128)(2,1)S(1)}, bf16[128,1792]{1,0:T(8,128)(2,1)S(1)}, u32[]{:S(2)}, u32[]{:S(2)}) collective-permute-start(bf16[128,1792]{1,0:T(8,128)(2,1)S(1)} %get-tuple-element.114), channel_id=1, source_target_pairs={{0,8},{8,0},{16,24},{24,16},{1,9},{9,1},{17,25},{25,17},{2,10},{10... | collective-permute-start | bytes 1376264 | tf_op jit(solution)/shard_map/ppermute | solution.py:30
  110.6 16.5 %collective-permute-start.16 = (bf16[2,128,1792]{2,1,0:T(8,128)(2,1)S(1)}, bf16[2,128,1792]{2,1,0:T(8,128)(2,1)S(1)}, u32[]{:S(2)}, u32[]{:S(2)}) collective-permute-start(bf16[2,128,1792]{2,1,0:T(8,128)(2,1)S(1)} %get-tuple-element.119.refs_2_.refs_3_), channel_id=1, source_target_pairs={{8,16},{16,8},{9,17},{17,9},{10,18},{18,10},{11,19},{19,11},{12,20... | collective-permute-start | bytes 2752520 | tf_op jit(solution)/shard_map/ppermute | solution.py:30
  116.7 27.8 %collective-permute-start.17 = (bf16[2,128,1792]{2,1,0:T(8,128)(2,1)S(1)}, bf16[2,128,1792]{2,1,0:T(8,128)(2,1)S(1)}, u32[]{:S(2)}, u32[]{:S(2)}) collective-permute-start(bf16[2,128,1792]{2,1,0:T(8,128)(2,1)S(1)} %get-tuple-element.121.refs_3_.refs_4_), channel_id=1, source_target_pairs={{8,0},{16,24},{9,1},{17,25},{10,2},{18,26},{11,3},{19,27},{12,4},{... | collective-permute-start | bytes 2752520 | tf_op jit(solution)/shard_map/ppermute | solution.py:30
  119.0 34.3 %collective-permute-start.21 = (bf16[2,128,1792]{2,1,0:T(8,128)(2,1)S(1)}, bf16[2,128,1792]{2,1,0:T(8,128)(2,1)S(1)}, u32[]{:S(2)}, u32[]{:S(2)}) collective-permute-start(bf16[2,128,1792]{2,1,0:T(8,128)(2,1)S(1)} %get-tuple-element.128.refs_1_.refs_2_), channel_id=1, source_target_pairs={{8,16},{16,8},{9,17},{17,9},{10,18},{18,10},{11,19},{19,11},{12,20... | collective-permute-start | bytes 2752520 | tf_op jit(solution)/shard_map/ppermute | solution.py:30
  119.8 38.0 %collective-permute-start.22 = (bf16[2,128,1792]{2,1,0:T(8,128)(2,1)S(1)}, bf16[2,128,1792]{2,1,0:T(8,128)(2,1)S(1)}, u32[]{:S(2)}, u32[]{:S(2)}) collective-permute-start(bf16[2,128,1792]{2,1,0:T(8,128)(2,1)S(1)} %get-tuple-element.128.refs_1_.refs_2_), channel_id=1, source_target_pairs={{0,8},{8,0},{16,24},{24,16},{1,9},{9,1},{17,25},{25,17},{2,10},{10... | collective-permute-start | bytes 2752520 | tf_op jit(solution)/shard_map/ppermute | solution.py:30
  150.9 26.6 %collective-permute-start.23 = (bf16[2,128,1792]{2,1,0:T(8,128)(2,1)S(1)}, bf16[2,128,1792]{2,1,0:T(8,128)(2,1)S(1)}, u32[]{:S(2)}, u32[]{:S(2)}) collective-permute-start(bf16[2,128,1792]{2,1,0:T(8,128)(2,1)S(1)} %get-tuple-element.131.refs_5_.refs_6_), channel_id=1, source_target_pairs={{8,0},{16,24},{9,1},{17,25},{10,2},{18,26},{11,3},{19,27},{12,4},{... | collective-permute-start | bytes 2752520 | tf_op jit(solution)/shard_map/ppermute | solution.py:30
  157.8 30.3 %collective-permute-start.24 = (bf16[2,128,1792]{2,1,0:T(8,128)(2,1)S(1)}, bf16[2,128,1792]{2,1,0:T(8,128)(2,1)S(1)}, u32[]{:S(2)}, u32[]{:S(2)}) collective-permute-start(bf16[2,128,1792]{2,1,0:T(8,128)(2,1)S(1)} %get-tuple-element.138.refs_2_.refs_3_), channel_id=1, source_target_pairs={{8,16},{16,8},{9,17},{17,9},{10,18},{18,10},{11,19},{19,11},{12,20... | collective-permute-start | bytes 2752520 | tf_op jit(solution)/shard_map/ppermute | solution.py:30
  158.5 38.6 %collective-permute-start.25 = (bf16[2,128,1792]{2,1,0:T(8,128)(2,1)S(1)}, bf16[2,128,1792]{2,1,0:T(8,128)(2,1)S(1)}, u32[]{:S(2)}, u32[]{:S(2)}) collective-permute-start(bf16[2,128,1792]{2,1,0:T(8,128)(2,1)S(1)} %get-tuple-element.140.refs_3_.refs_4_), channel_id=1, source_target_pairs={{8,0},{16,24},{9,1},{17,25},{10,2},{18,26},{11,3},{19,27},{12,4},{... | collective-permute-start | bytes 2752520 | tf_op jit(solution)/shard_map/ppermute | solution.py:30
  188.1 18.8 %collective-permute-start.26 = (bf16[2,128,896]{2,1,0:T(8,128)(2,1)S(1)}, bf16[2,128,896]{2,1,0:T(8,128)(2,1)S(1)}, u32[]{:S(2)}, u32[]{:S(2)}) collective-permute-start(bf16[2,128,896]{2,1,0:T(8,128)(2,1)S(1)} %get-tuple-element.143.refs_1_.refs_6_), channel_id=1, source_target_pairs={{8,0},{16,24},{9,1},{17,25},{10,2},{18,26},{11,3},{19,27},{12,4},{... | collective-permute-start | bytes 1376264 | tf_op jit(solution)/shard_map/ppermute | solution.py:30
  189.4 26.4 %collective-permute-start.27 = (bf16[2,128,896]{2,1,0:T(8,128)(2,1)S(1)}, bf16[2,128,896]{2,1,0:T(8,128)(2,1)S(1)}, u32[]{:S(2)}, u32[]{:S(2)}) collective-permute-start(bf16[2,128,896]{2,1,0:T(8,128)(2,1)S(1)} %get-tuple-element.148.refs_2_.refs_6_), channel_id=1, source_target_pairs={{8,0},{16,24},{9,1},{17,25},{10,2},{18,26},{11,3},{19,27},{12,4},{... | collective-permute-start | bytes 1376264 | tf_op jit(solution)/shard_map/ppermute | solution.py:30
  222.7 7.5 %collective-permute-start.31 = (bf16[64,1024]{1,0:T(8,128)(2,1)S(1)}, bf16[64,1024]{1,0:T(8,128)(2,1)S(1)}, u32[]{:S(2)}, u32[]{:S(2)}) collective-permute-start(bf16[64,1024]{1,0:T(8,128)(2,1)S(1)} %get-tuple-element.161), channel_id=1, source_target_pairs={{0,6},{1,7},{2,4},{3,5},{4,2},{5,3},{6,0},{7,1},{8,14},{9,15},{10,... | collective-permute-start | bytes 393224 | tf_op jit(solution)/shard_map/ppermute | solution.py:478
  (19 other events, 433.4 us)

commit v6 on v5

--- a/solution.py
+++ b/solution.py
@@ -431,6 +431,8 @@
     groups.append(grads_of(1, 1))
     spread_end(groups[0])
     (groups[0]["near_end"],) = chain.relay(groups[0]["near_end"])
+    spread_near(groups[1])
+    spread_far(groups[1])
     (inputs_b,) = chain.relay(saved_input.astype(BF))
     in_raw = tok_last(*tok_swaps(inputs_b))
     inputs = chain.call(
@@ -442,8 +444,6 @@
         [whole(depth, tokens)],
         scalars=where,
     )[0]
-    spread_near(groups[1])
-    spread_far(groups[1])
     (groups[0]["far_end"],) = chain.relay(groups[0]["far_end"])
     total = input_step(0, None, ALL)
     weights = weights_step(pieces(groups[0]), cuts[0], 0, ())

time: 231 us -> 231 us (level)
  transfers between devices with their start and end apart: 32 -> 32, of which waited for: 21 -> 20; matrix products, arithmetic and copies ran while one was open for 0% -> 0% of each run, Pallas kernels for 18% -> 18%
where the time goes in v6:
time: 231 us
  waiting for transfers between devices  123 us (53%)
  starting transfers between devices  57 us (25%)
  Pallas kernels  44.9 us (19%)
  local copies, waits for them, and re-layouts  4.67 us (2%)
    ppermute x22, waiting for transfers between devices, send(): return lax.ppermute(x, 'inp', perm)  112 us
    ppermute x22, starting transfers between devices, send(): return lax.ppermute(x, 'inp', perm)  49.2 us
    pallas_call x35, Pallas kernels, call(): pl.pallas_call(kernel, grid_spec=pltpu.PrefetchScalarGridSpec(num_scalar_...  44.9 us
  transfers between devices with their start and end apart: 32, of which 20 were waited for; matrix products, arithmetic and copies ran while one was open for 0% of the time, Pallas kernels for 18%

profile of v6, /device:TPU:0, one launch (start us, length us, event | category | flops | bytes accessed | tf_op | source)
XLA Modules:
  0.0 230.9 jit_solution(14842939903351134100)
XLA Ops:
  7.9 4.4 %collective-permute-start.4 = (bf16[128,3584]{1,0:T(8,128)(2,1)}, bf16[128,3584]{1,0:T(8,128)(2,1)S(1)}, u32[]{:S(2)}, u32[]{:S(2)}) collective-permute-start(bf16[128,3584]{1,0:T(8,128)(2,1)} %get-tuple-element.88.refs_2_), channel_id=1, source_target_pairs={{0,8},{8,0},{16,24},{24,16},{1,9},{9,1},{17,25},{25,17},{2,10},{10... | collective-permute-start | bytes 2752520 | tf_op jit(solution)/shard_map/ppermute | solution.py:30
  14.2 3.1 %copy-done = bf16[3584,1024]{1,0:T(8,128)(2,1)S(1)} copy-done((bf16[3584,1024]{1,0:T(8,128)(2,1)S(1)}, bf16[3584,1024]{1,0:T(8,128)(2,1)}, u32[]{:S(2)}) %copy-start) | copy-done | bytes 7340056
  18.2 3.6 %shard_map.103 = (f32[8,128]{1,0:T(8,128)S(1)}, f32[512,1792]{1,0:T(8,128)S(1)}, bf16[256,1792]{1,0:T(8,128)(2,1)S(1)}, bf16[512,1024]{1,0:T(8,128)(2,1)S(1)}) custom-call(s32[3]{0:T(128)S(1)} %pad_add_fusion.refs_0_, f32[8,128]{1,0:T(8,128)S(1)} %get-tuple-element.85.refs_1_, bf16[128,1024]{1,0:T(8,128)(2,1)S(1)} %copy-done.5, ...), custom_call_target="tpu_custom_call", output_to_operand_aliasing={{0}: (1, {})} | custom-call | tf_op jit(solution)/shard_map/pallas_call | solution.py:61
  23.9 9.5 %collective-permute-done.4.refs_1_ = bf16[128,3584]{1,0:T(8,128)(2,1)S(1)} collective-permute-done((bf16[128,3584]{1,0:T(8,128)(2,1)}, bf16[128,3584]{1,0:T(8,128)(2,1)S(1)}, u32[]{:S(2)}, u32[]{:S(2)}) %collective-permute-start.4) | collective-permute-done | bytes 917536 | tf_op jit(solution)/shard_map/ppermute | solution.py:30
  38.4 6.0 %collective-permute-start.9 = (bf16[256,1792]{1,0:T(8,128)(2,1)S(1)}, bf16[256,1792]{1,0:T(8,128)(2,1)S(1)}, u32[]{:S(2)}, u32[]{:S(2)}) collective-permute-start(bf16[256,1792]{1,0:T(8,128)(2,1)S(1)} %get-tuple-element.100), channel_id=1, source_target_pairs={{0,8},{24,16},{1,9},{25,17},{2,10},{26,18},{3,11},{27,19},{4,12},{... | collective-permute-start | bytes 2752520 | tf_op jit(solution)/shard_map/ppermute | solution.py:30
  44.4 8.6 %collective-permute-done.5.refs_1_ = bf16[256,1792]{1,0:T(8,128)(2,1)S(1)} collective-permute-done((bf16[256,1792]{1,0:T(8,128)(2,1)S(1)}, bf16[256,1792]{1,0:T(8,128)(2,1)S(1)}, u32[]{:S(2)}, u32[]{:S(2)}) %collective-permute-start.5) | collective-permute-done | bytes 917536 | tf_op jit(solution)/shard_map/ppermute | solution.py:30
  57.6 13.3 %collective-permute-done.9.refs_3_ = bf16[256,1792]{1,0:T(8,128)(2,1)S(1)} collective-permute-done((bf16[256,1792]{1,0:T(8,128)(2,1)S(1)}, bf16[256,1792]{1,0:T(8,128)(2,1)S(1)}, u32[]{:S(2)}, u32[]{:S(2)}) %collective-permute-start.9) | collective-permute-done | bytes 917536 | tf_op jit(solution)/shard_map/ppermute | solution.py:30
  71.1 6.0 %collective-permute-start.11 = (bf16[128,1792]{1,0:T(8,128)(2,1)S(1)}, bf16[128,1792]{1,0:T(8,128)(2,1)S(1)}, u32[]{:S(2)}, u32[]{:S(2)}) collective-permute-start(bf16[128,1792]{1,0:T(8,128)(2,1)S(1)} %get-tuple-element.105), channel_id=1, source_target_pairs={{0,8},{8,0},{16,24},{24,16},{1,9},{9,1},{17,25},{25,17},{2,10},{10... | collective-permute-start | bytes 1376264 | tf_op jit(solution)/shard_map/ppermute | solution.py:30
  79.4 7.0 %collective-permute-done.11.refs_3_ = bf16[128,1792]{1,0:T(8,128)(2,1)S(1)} collective-permute-done((bf16[128,1792]{1,0:T(8,128)(2,1)S(1)}, bf16[128,1792]{1,0:T(8,128)(2,1)S(1)}, u32[]{:S(2)}, u32[]{:S(2)}) %collective-permute-start.11) | collective-permute-done | bytes 458784 | tf_op jit(solution)/shard_map/ppermute | solution.py:30
  88.1 6.4 %shard_map.113 = (f32[8,128]{1,0:T(8,128)S(1)}, bf16[3584,1024]{1,0:T(8,128)(2,1)}) custom-call(f32[8,128]{1,0:T(8,128)S(1)} %get-tuple-element.106.refs_0_, bf16[512,1024]{1,0:T(8,128)(2,1)S(1)} %get-tuple-element.91.refs_1_, bf16[128,3584]{1,0:T(8,128)(2,1)S(1)} %copy-done.4, ...), custom_call_target="tpu_custom_call", output_to_operand_aliasing={{0}: (0, {})} | custom-call | tf_op jit(solution)/shard_map/pallas_call | solution.py:61
  94.6 7.9 %collective-permute-start.14 = (bf16[128,1792]{1,0:T(8,128)(2,1)S(1)}, bf16[128,1792]{1,0:T(8,128)(2,1)S(1)}, u32[]{:S(2)}, u32[]{:S(2)}) collective-permute-start(bf16[128,1792]{1,0:T(8,128)(2,1)S(1)} %get-tuple-element.114), channel_id=1, source_target_pairs={{0,8},{8,0},{16,24},{24,16},{1,9},{9,1},{17,25},{25,17},{2,10},{10... | collective-permute-start | bytes 1376264 | tf_op jit(solution)/shard_map/ppermute | solution.py:30
  102.5 8.2 %collective-permute-done.13.refs_1_ = bf16[2,128,1792]{2,1,0:T(8,128)(2,1)S(1)} collective-permute-done((bf16[2,128,1792]{2,1,0:T(8,128)(2,1)S(1)}, bf16[2,128,1792]{2,1,0:T(8,128)(2,1)S(1)}, u32[]{:S(2)}, u32[]{:S(2)}) %collective-permute-start.13) | collective-permute-done | bytes 917536 | tf_op jit(solution)/shard_map/ppermute | solution.py:30
  111.5 5.2 %collective-permute-done.14.refs_1_ = bf16[128,1792]{1,0:T(8,128)(2,1)S(1)} collective-permute-done((bf16[128,1792]{1,0:T(8,128)(2,1)S(1)}, bf16[128,1792]{1,0:T(8,128)(2,1)S(1)}, u32[]{:S(2)}, u32[]{:S(2)}) %collective-permute-start.14) | collective-permute-done | bytes 458784 | tf_op jit(solution)/shard_map/ppermute | solution.py:30
  119.8 7.3 %collective-permute-start.19 = (bf16[2,128,1792]{2,1,0:T(8,128)(2,1)S(1)}, bf16[2,128,1792]{2,1,0:T(8,128)(2,1)S(1)}, u32[]{:S(2)}, u32[]{:S(2)}) collective-permute-start(bf16[2,128,1792]{2,1,0:T(8,128)(2,1)S(1)} %get-tuple-element.123.refs_1_.refs_2_), channel_id=1, source_target_pairs={{0,8},{8,0},{16,24},{24,16},{1,9},{9,1},{17,25},{25,17},{2,10},{10... | collective-permute-start | bytes 2752520 | tf_op jit(solution)/shard_map/ppermute | solution.py:30
  128.4 16.1 %collective-permute-done.17.refs_1_ = bf16[2,128,1792]{2,1,0:T(8,128)(2,1)S(1)} collective-permute-done((bf16[2,128,1792]{2,1,0:T(8,128)(2,1)S(1)}, bf16[2,128,1792]{2,1,0:T(8,128)(2,1)S(1)}, u32[]{:S(2)}, u32[]{:S(2)}) %collective-permute-start.17) | collective-permute-done | bytes 917536 | tf_op jit(solution)/shard_map/ppermute | solution.py:30
  144.5 19.7 %collective-permute-done.19.refs_1_ = bf16[2,128,1792]{2,1,0:T(8,128)(2,1)S(1)} collective-permute-done((bf16[2,128,1792]{2,1,0:T(8,128)(2,1)S(1)}, bf16[2,128,1792]{2,1,0:T(8,128)(2,1)S(1)}, u32[]{:S(2)}, u32[]{:S(2)}) %collective-permute-start.19) | collective-permute-done | bytes 917536 | tf_op jit(solution)/shard_map/ppermute | solution.py:30
  167.1 4.3 %collective-permute-done.20.refs_1_ = bf16[128,1024]{1,0:T(8,128)(2,1)S(1)} collective-permute-done((bf16[128,1024]{1,0:T(8,128)(2,1)S(1)}, bf16[128,1024]{1,0:T(8,128)(2,1)S(1)}, u32[]{:S(2)}, u32[]{:S(2)}) %collective-permute-start.20) | collective-permute-done | bytes 262176 | tf_op jit(solution)/shard_map/ppermute | solution.py:234
  173.8 10.0 %collective-permute-done.23.refs_1_ = bf16[2,128,1792]{2,1,0:T(8,128)(2,1)S(1)} collective-permute-done((bf16[2,128,1792]{2,1,0:T(8,128)(2,1)S(1)}, bf16[2,128,1792]{2,1,0:T(8,128)(2,1)S(1)}, u32[]{:S(2)}, u32[]{:S(2)}) %collective-permute-start.23) | collective-permute-done | bytes 917536 | tf_op jit(solution)/shard_map/ppermute | solution.py:30
  183.9 4.0 %shard_map.127 = (f32[8,128]{1,0:T(8,128)S(1)}, f32[512,1024]{1,0:T(8,128)S(1)}) custom-call(f32[8,128]{1,0:T(8,128)S(1)} %get-tuple-element.132.refs_0_, bf16[2,128,1792]{2,1,0:T(8,128)(2,1)S(1)} %get-tuple-element.112.refs_1_.refs_2_, bf16[2,128,1792]{2,1,0:T(8,128)(2,1)S(1)} %get-tuple-element.119.refs_2_.refs_3_, ...), custom_call_target="tpu_custom_call", output_to_operand_aliasing={{0}: (0, {})} | custom-call | tf_op jit(solution)/shard_map/pallas_call | solution.py:61
  187.9 6.6 %shard_map.128 = (f32[8,128]{1,0:T(8,128)S(1)}, bf16[1024,3584]{1,0:T(8,128)(2,1)}, bf16[1024,3584]{1,0:T(8,128)(2,1)}) custom-call(f32[8,128]{1,0:T(8,128)S(1)} %get-tuple-element.135.refs_0_, bf16[1024,512]{1,0:T(8,128)(2,1)S(1)} %get-tuple-element.136.refs_1_, ...), custom_call_target="tpu_custom_call", output_to_operand_aliasing={{0}: (0, {})} | custom-call | tf_op jit(solution)/shard_map/pallas_call | solution.py:61
  197.3 5.9 %collective-permute-done.25.refs_4_.refs_5_ = bf16[2,128,1792]{2,1,0:T(8,128)(2,1)S(1)} collective-permute-done((bf16[2,128,1792]{2,1,0:T(8,128)(2,1)S(1)}, bf16[2,128,1792]{2,1,0:T(8,128)(2,1)S(1)}, u32[]{:S(2)}, u32[]{:S(2)}) %collective-permute-start.25) | collective-permute-done | bytes 917536 | tf_op jit(solution)/shard_map/ppermute | solution.py:30
  206.2 4.7 %collective-permute-done.26.refs_2_.refs_7_ = bf16[2,128,896]{2,1,0:T(8,128)(2,1)S(1)} collective-permute-done((bf16[2,128,896]{2,1,0:T(8,128)(2,1)S(1)}, bf16[2,128,896]{2,1,0:T(8,128)(2,1)S(1)}, u32[]{:S(2)}, u32[]{:S(2)}) %collective-permute-start.26) | collective-permute-done | bytes 458784 | tf_op jit(solution)/shard_map/ppermute | solution.py:30
  212.3 3.6 %shard_map.132 = (f32[8,128]{1,0:T(8,128)S(1)}, bf16[1024,3584]{1,0:T(8,128)(2,1)}, bf16[1024,3584]{1,0:T(8,128)(2,1)}) custom-call(f32[8,128]{1,0:T(8,128)S(1)} %get-tuple-element.144.refs_0_, bf16[1024,512]{1,0:T(8,128)(2,1)S(1)} %get-tuple-element.136.refs_1_, ...), custom_call_target="tpu_custom_call", output_to_operand_aliasing={{0}: (0, {}), {1}: (8, {}), {2}: (9, {})} | custom-call | tf_op jit(solution)/shard_map/pallas_call | solution.py:61
  224.2 3.6 %shard_map.135 = (f32[8,128]{1,0:T(8,128)S(1)}, bf16[1024,3584]{1,0:T(8,128)(2,1)}, bf16[1024,3584]{1,0:T(8,128)(2,1)}) custom-call(f32[8,128]{1,0:T(8,128)S(1)} %get-tuple-element.154.refs_0_, bf16[1024,512]{1,0:T(8,128)(2,1)S(1)} %get-tuple-element.136.refs_1_, ...), custom_call_target="tpu_custom_call", output_to_operand_aliasing={{0}: (0, {}), {1}: (8, {}), {2}: (9, {})} | custom-call | tf_op jit(solution)/shard_map/pallas_call | solution.py:61
  (103 shorter events, 55.0 us)
Async XLA Ops:
  0.6 11.7 %collective-permute-start = (bf16[128,1024]{1,0:T(8,128)(2,1)}, bf16[128,1024]{1,0:T(8,128)(2,1)S(1)}, u32[]{:S(2)}, u32[]{:S(2)}) collective-permute-start(bf16[128,1024]{1,0:T(8,128)(2,1)} %refs_2_.3), channel_id=1, source_target_pairs={{0,2},{2,0},{1,3},{3,1},{4,6},{6,4},{5,7},{7,5},{8,10},{10,8},{9,1... | collective-permute-start | bytes 786440 | tf_op jit(solution)/shard_map/ppermute | solution.py:234
  7.2 16.7 %collective-permute-start.3 = (bf16[128,3584]{1,0:T(8,128)(2,1)}, bf16[128,3584]{1,0:T(8,128)(2,1)S(1)}, u32[]{:S(2)}, u32[]{:S(2)}) collective-permute-start(bf16[128,3584]{1,0:T(8,128)(2,1)} %get-tuple-element.88.refs_2_), channel_id=1, source_target_pairs={{8,16},{16,8},{9,17},{17,9},{10,18},{18,10},{11,19},{19,11},{12,20... | collective-permute-start | bytes 2752520 | tf_op jit(solution)/shard_map/ppermute | solution.py:30
  7.9 25.5 %collective-permute-start.4 = (bf16[128,3584]{1,0:T(8,128)(2,1)}, bf16[128,3584]{1,0:T(8,128)(2,1)S(1)}, u32[]{:S(2)}, u32[]{:S(2)}) collective-permute-start(bf16[128,3584]{1,0:T(8,128)(2,1)} %get-tuple-element.88.refs_2_), channel_id=1, source_target_pairs={{0,8},{8,0},{16,24},{24,16},{1,9},{9,1},{17,25},{25,17},{2,10},{10... | collective-permute-start | bytes 2752520 | tf_op jit(solution)/shard_map/ppermute | solution.py:30
  21.8 31.2 %collective-permute-start.5 = (bf16[256,1792]{1,0:T(8,128)(2,1)S(1)}, bf16[256,1792]{1,0:T(8,128)(2,1)S(1)}, u32[]{:S(2)}, u32[]{:S(2)}) collective-permute-start(bf16[256,1792]{1,0:T(8,128)(2,1)S(1)} %get-tuple-element.93), channel_id=1, source_target_pairs={{0,8},{24,16},{1,9},{25,17},{2,10},{26,18},{3,11},{27,19},{4,12},{... | collective-permute-start | bytes 2752520 | tf_op jit(solution)/shard_map/ppermute | solution.py:30
  33.4 20.9 %collective-permute-start.6 = (bf16[128,3584]{1,0:T(8,128)(2,1)S(1)}, bf16[128,3584]{1,0:T(8,128)(2,1)S(1)}, u32[]{:S(2)}, u32[]{:S(2)}) collective-permute-start(bf16[128,3584]{1,0:T(8,128)(2,1)S(1)} %get-tuple-element.96.refs_3_), channel_id=1, source_target_pairs={{8,16},{16,8},{9,17},{17,9},{10,18},{18,10},{11,19},{19,11},{12,20... | collective-permute-start | bytes 2752520 | tf_op jit(solution)/shard_map/ppermute | solution.py:30
  34.1 22.2 %collective-permute-start.7 = (bf16[128,3584]{1,0:T(8,128)(2,1)S(1)}, bf16[128,3584]{1,0:T(8,128)(2,1)S(1)}, u32[]{:S(2)}, u32[]{:S(2)}) collective-permute-start(bf16[128,3584]{1,0:T(8,128)(2,1)S(1)} %get-tuple-element.97.refs_4_), channel_id=1, source_target_pairs={{8,0},{16,24},{9,1},{17,25},{10,2},{18,26},{11,3},{19,27},{12,4},{... | collective-permute-start | bytes 2752520 | tf_op jit(solution)/shard_map/ppermute | solution.py:30
  38.4 32.5 %collective-permute-start.9 = (bf16[256,1792]{1,0:T(8,128)(2,1)S(1)}, bf16[256,1792]{1,0:T(8,128)(2,1)S(1)}, u32[]{:S(2)}, u32[]{:S(2)}) collective-permute-start(bf16[256,1792]{1,0:T(8,128)(2,1)S(1)} %get-tuple-element.100), channel_id=1, source_target_pairs={{0,8},{24,16},{1,9},{25,17},{2,10},{26,18},{3,11},{27,19},{4,12},{... | collective-permute-start | bytes 2752520 | tf_op jit(solution)/shard_map/ppermute | solution.py:30
  53.5 17.4 %collective-permute-start.8 = (bf16[256,1792]{1,0:T(8,128)(2,1)S(1)}, bf16[256,1792]{1,0:T(8,128)(2,1)S(1)}, u32[]{:S(2)}, u32[]{:S(2)}) collective-permute-start(bf16[256,1792]{1,0:T(8,128)(2,1)S(1)} %get-tuple-element.99), channel_id=1, source_target_pairs={{8,16},{16,8},{9,17},{17,9},{10,18},{18,10},{11,19},{19,11},{12,20... | collective-permute-start | bytes 2752520 | tf_op jit(solution)/shard_map/ppermute | solution.py:30
  56.3 23.1 %collective-permute-start.10 = (bf16[128,3584]{1,0:T(8,128)(2,1)S(1)}, bf16[128,3584]{1,0:T(8,128)(2,1)S(1)}, u32[]{:S(2)}, u32[]{:S(2)}) collective-permute-start(bf16[128,3584]{1,0:T(8,128)(2,1)S(1)} %get-tuple-element.103.refs_6_), channel_id=1, source_target_pairs={{8,0},{16,24},{9,1},{17,25},{10,2},{18,26},{11,3},{19,27},{12,4},{... | collective-permute-start | bytes 2752520 | tf_op jit(solution)/shard_map/ppermute | solution.py:30
  71.1 15.2 %collective-permute-start.11 = (bf16[128,1792]{1,0:T(8,128)(2,1)S(1)}, bf16[128,1792]{1,0:T(8,128)(2,1)S(1)}, u32[]{:S(2)}, u32[]{:S(2)}) collective-permute-start(bf16[128,1792]{1,0:T(8,128)(2,1)S(1)} %get-tuple-element.105), channel_id=1, source_target_pairs={{0,8},{8,0},{16,24},{24,16},{1,9},{9,1},{17,25},{25,17},{2,10},{10... | collective-permute-start | bytes 1376264 | tf_op jit(solution)/shard_map/ppermute | solution.py:30
  77.1 17.4 %collective-permute-start.12 = (bf16[256,1792]{1,0:T(8,128)(2,1)S(1)}, bf16[256,1792]{1,0:T(8,128)(2,1)S(1)}, u32[]{:S(2)}, u32[]{:S(2)}) collective-permute-start(bf16[256,1792]{1,0:T(8,128)(2,1)S(1)} %get-tuple-element.110), channel_id=1, source_target_pairs={{8,16},{16,8},{9,17},{17,9},{10,18},{18,10},{11,19},{19,11},{12,20... | collective-permute-start | bytes 2752520 | tf_op jit(solution)/shard_map/ppermute | solution.py:30
  87.3 23.4 %collective-permute-start.13 = (bf16[2,128,1792]{2,1,0:T(8,128)(2,1)S(1)}, bf16[2,128,1792]{2,1,0:T(8,128)(2,1)S(1)}, u32[]{:S(2)}, u32[]{:S(2)}) collective-permute-start(bf16[2,128,1792]{2,1,0:T(8,128)(2,1)S(1)} %get-tuple-element.112.refs_1_.refs_2_), channel_id=1, source_target_pairs={{0,8},{8,0},{16,24},{24,16},{1,9},{9,1},{17,25},{25,17},{2,10},{10... | collective-permute-start | bytes 2752520 | tf_op jit(solution)/shard_map/ppermute | solution.py:30
  87.4 29.4 %collective-permute-start.15 = (bf16[2,128,1792]{2,1,0:T(8,128)(2,1)S(1)}, bf16[2,128,1792]{2,1,0:T(8,128)(2,1)S(1)}, u32[]{:S(2)}, u32[]{:S(2)}) collective-permute-start(bf16[2,128,1792]{2,1,0:T(8,128)(2,1)S(1)} %get-tuple-element.112.refs_1_.refs_2_), channel_id=1, source_target_pairs={{8,16},{16,8},{9,17},{17,9},{10,18},{18,10},{11,19},{19,11},{12,20... | collective-permute-start | bytes 2752520 | tf_op jit(solution)/shard_map/ppermute | solution.py:30
  94.6 22.1 %collective-permute-start.14 = (bf16[128,1792]{1,0:T(8,128)(2,1)S(1)}, bf16[128,1792]{1,0:T(8,128)(2,1)S(1)}, u32[]{:S(2)}, u32[]{:S(2)}) collective-permute-start(bf16[128,1792]{1,0:T(8,128)(2,1)S(1)} %get-tuple-element.114), channel_id=1, source_target_pairs={{0,8},{8,0},{16,24},{24,16},{1,9},{9,1},{17,25},{25,17},{2,10},{10... | collective-permute-start | bytes 1376264 | tf_op jit(solution)/shard_map/ppermute | solution.py:30
  110.6 16.5 %collective-permute-start.16 = (bf16[2,128,1792]{2,1,0:T(8,128)(2,1)S(1)}, bf16[2,128,1792]{2,1,0:T(8,128)(2,1)S(1)}, u32[]{:S(2)}, u32[]{:S(2)}) collective-permute-start(bf16[2,128,1792]{2,1,0:T(8,128)(2,1)S(1)} %get-tuple-element.119.refs_2_.refs_3_), channel_id=1, source_target_pairs={{8,16},{16,8},{9,17},{17,9},{10,18},{18,10},{11,19},{19,11},{12,20... | collective-permute-start | bytes 2752520 | tf_op jit(solution)/shard_map/ppermute | solution.py:30
  116.7 27.8 %collective-permute-start.17 = (bf16[2,128,1792]{2,1,0:T(8,128)(2,1)S(1)}, bf16[2,128,1792]{2,1,0:T(8,128)(2,1)S(1)}, u32[]{:S(2)}, u32[]{:S(2)}) collective-permute-start(bf16[2,128,1792]{2,1,0:T(8,128)(2,1)S(1)} %get-tuple-element.121.refs_3_.refs_4_), channel_id=1, source_target_pairs={{8,0},{16,24},{9,1},{17,25},{10,2},{18,26},{11,3},{19,27},{12,4},{... | collective-permute-start | bytes 2752520 | tf_op jit(solution)/shard_map/ppermute | solution.py:30
  119.0 25.6 %collective-permute-start.18 = (bf16[2,128,1792]{2,1,0:T(8,128)(2,1)S(1)}, bf16[2,128,1792]{2,1,0:T(8,128)(2,1)S(1)}, u32[]{:S(2)}, u32[]{:S(2)}) collective-permute-start(bf16[2,128,1792]{2,1,0:T(8,128)(2,1)S(1)} %get-tuple-element.123.refs_1_.refs_2_), channel_id=1, source_target_pairs={{8,16},{16,8},{9,17},{17,9},{10,18},{18,10},{11,19},{19,11},{12,20... | collective-permute-start | bytes 2752520 | tf_op jit(solution)/shard_map/ppermute | solution.py:30
  119.8 44.4 %collective-permute-start.19 = (bf16[2,128,1792]{2,1,0:T(8,128)(2,1)S(1)}, bf16[2,128,1792]{2,1,0:T(8,128)(2,1)S(1)}, u32[]{:S(2)}, u32[]{:S(2)}) collective-permute-start(bf16[2,128,1792]{2,1,0:T(8,128)(2,1)S(1)} %get-tuple-element.123.refs_1_.refs_2_), channel_id=1, source_target_pairs={{0,8},{8,0},{16,24},{24,16},{1,9},{9,1},{17,25},{25,17},{2,10},{10... | collective-permute-start | bytes 2752520 | tf_op jit(solution)/shard_map/ppermute | solution.py:30
  127.1 56.7 %collective-permute-start.23 = (bf16[2,128,1792]{2,1,0:T(8,128)(2,1)S(1)}, bf16[2,128,1792]{2,1,0:T(8,128)(2,1)S(1)}, u32[]{:S(2)}, u32[]{:S(2)}) collective-permute-start(bf16[2,128,1792]{2,1,0:T(8,128)(2,1)S(1)} %get-tuple-element.131.refs_5_.refs_6_), channel_id=1, source_target_pairs={{8,0},{16,24},{9,1},{17,25},{10,2},{18,26},{11,3},{19,27},{12,4},{... | collective-permute-start | bytes 2752520 | tf_op jit(solution)/shard_map/ppermute | solution.py:30
  164.2 30.2 %collective-permute-start.24 = (bf16[2,128,1792]{2,1,0:T(8,128)(2,1)S(1)}, bf16[2,128,1792]{2,1,0:T(8,128)(2,1)S(1)}, u32[]{:S(2)}, u32[]{:S(2)}) collective-permute-start(bf16[2,128,1792]{2,1,0:T(8,128)(2,1)S(1)} %get-tuple-element.138.refs_2_.refs_3_), channel_id=1, source_target_pairs={{8,16},{16,8},{9,17},{17,9},{10,18},{18,10},{11,19},{19,11},{12,20... | collective-permute-start | bytes 2752520 | tf_op jit(solution)/shard_map/ppermute | solution.py:30
  165.6 37.6 %collective-permute-start.25 = (bf16[2,128,1792]{2,1,0:T(8,128)(2,1)S(1)}, bf16[2,128,1792]{2,1,0:T(8,128)(2,1)S(1)}, u32[]{:S(2)}, u32[]{:S(2)}) collective-permute-start(bf16[2,128,1792]{2,1,0:T(8,128)(2,1)S(1)} %get-tuple-element.140.refs_3_.refs_4_), channel_id=1, source_target_pairs={{8,0},{16,24},{9,1},{17,25},{10,2},{18,26},{11,3},{19,27},{12,4},{... | collective-permute-start | bytes 2752520 | tf_op jit(solution)/shard_map/ppermute | solution.py:30
  194.5 16.4 %collective-permute-start.26 = (bf16[2,128,896]{2,1,0:T(8,128)(2,1)S(1)}, bf16[2,128,896]{2,1,0:T(8,128)(2,1)S(1)}, u32[]{:S(2)}, u32[]{:S(2)}) collective-permute-start(bf16[2,128,896]{2,1,0:T(8,128)(2,1)S(1)} %get-tuple-element.143.refs_1_.refs_6_), channel_id=1, source_target_pairs={{8,0},{16,24},{9,1},{17,25},{10,2},{18,26},{11,3},{19,27},{12,4},{... | collective-permute-start | bytes 1376264 | tf_op jit(solution)/shard_map/ppermute | solution.py:30
  195.8 20.1 %collective-permute-start.27 = (bf16[2,128,896]{2,1,0:T(8,128)(2,1)S(1)}, bf16[2,128,896]{2,1,0:T(8,128)(2,1)S(1)}, u32[]{:S(2)}, u32[]{:S(2)}) collective-permute-start(bf16[2,128,896]{2,1,0:T(8,128)(2,1)S(1)} %get-tuple-element.148.refs_2_.refs_6_), channel_id=1, source_target_pairs={{8,0},{16,24},{9,1},{17,25},{10,2},{18,26},{11,3},{19,27},{12,4},{... | collective-permute-start | bytes 1376264 | tf_op jit(solution)/shard_map/ppermute | solution.py:30
  222.8 7.5 %collective-permute-start.31 = (bf16[64,1024]{1,0:T(8,128)(2,1)S(1)}, bf16[64,1024]{1,0:T(8,128)(2,1)S(1)}, u32[]{:S(2)}, u32[]{:S(2)}) collective-permute-start(bf16[64,1024]{1,0:T(8,128)(2,1)S(1)} %get-tuple-element.161), channel_id=1, source_target_pairs={{0,6},{1,7},{2,4},{3,5},{4,2},{5,3},{6,0},{7,1},{8,14},{9,15},{10,... | collective-permute-start | bytes 393224 | tf_op jit(solution)/shard_map/ppermute | solution.py:478
  (19 other events, 477.9 us)
